TPU v7x, 32 devices: a whole 2x2x4 slice. The times are simulated.
32 devices in a mesh: wide: 8 (over z, x), narrow: 4 (over y, core).
Axes of the slice: x: 2, y: 2, z: 4, core: 2. Of those that a mesh axis runs over, the one named last changes fastest.
Arguments:
- latent: bfloat16 [2048, 4096], P('wide', 'narrow'), may hold values from -90 to 90
- actions: int32 [2048], P('wide'), may hold values from 0 to 255
- action_table: bfloat16 [256, 4096], P(None, 'narrow'), may hold values from -3 to 3
- norm1_gain: float32 [4096], P('narrow'), may hold values from 0.5 to 1.5
- w_query: bfloat16 [4096, 2048], P(None, 'narrow'), may hold values from -0.140625 to 0.140625
- w_key: bfloat16 [4096, 2048], P(None, 'narrow'), may hold values from -0.140625 to 0.140625
- w_value: bfloat16 [4096, 2048], P(None, 'narrow'), may hold values from -0.09375 to 0.09375
- w_out: bfloat16 [2048, 4096], P(None, 'narrow'), may hold values from -0.125 to 0.125
- key_cache: bfloat16 [16, 512, 2048], P('wide', None, 'narrow'), may hold values from -460 to 460
- value_cache: bfloat16 [16, 512, 2048], P('wide', None, 'narrow'), may hold values from -6 to 6
- norm2_gain: float32 [4096], P('narrow'), may hold values from 0.5 to 1.5
- policy_in: bfloat16 [4096, 512], P('narrow'), may hold values from -0.09375 to 0.09375
- value_in: bfloat16 [4096, 512], P('narrow'), may hold values from -0.09375 to 0.09375
- policy_out: bfloat16 [512, 256], replicated, may hold values from -12.5 to 12.5
- value_out: bfloat16 [512], replicated, may hold values from -0.25 to 0.25
- targets: int32 [2048], P('wide'), may hold values from 0 to 255
- returns: float32 [2048], P('wide'), may hold values from -19 to 19
Outputs:
- new_latent: bfloat16 [2048, 4096], P('wide', 'narrow')
- losses: float32 [2], replicated
- policy_in_grad: bfloat16 [4096, 512], P('narrow')
- value_in_grad: bfloat16 [4096, 512], P('narrow')
- policy_out_grad: bfloat16 [512, 256], replicated
- value_out_grad: bfloat16 [512], replicated
All inputs are finite; a program needn't handle non-finite values.
Results may differ from a plain program's by a relative error of at most 0.019.
Values may be sent and summed in bfloat16 or wider, within the bound.
No kernel may reach another device: no remote copies, remote signals or barrier semaphores. Data moves between devices by JAX's collectives and lax.ppermute only.
A program may use at most 64 MiB of HBM per device.

v0:
```python
import functools

import jax
import jax.numpy as jnp
from jax import lax
from jax.experimental import pallas as pl
from jax.experimental.pallas import tpu as pltpu
from jax.sharding import PartitionSpec as P

HD = 128
EPSILON = 1e-05
F32 = jnp.float32
BF16 = jnp.bfloat16
MIB = 1 << 20


def swap(block, bit):
    size = lax.axis_size("narrow")
    return lax.ppermute(block, "narrow", [(n, n ^ bit) for n in range(size)])


def far_bits():
    bit = lax.axis_size("narrow") // 2
    while bit > 1:
        yield bit
        bit //= 2


def far_blocks(block):
    blocks = {0: block}
    for bit in far_bits():
        blocks.update({d ^ bit: swap(b, bit) for d, b in list(blocks.items())})
    return blocks


def pass_blocks(blocks, *earlier):
    far = {d ^ 1: swap(after(b, *earlier), 1) for d, b in blocks.items() if d > 1}
    return {**blocks, **far}


def after(block, *earlier):
    return lax.optimization_barrier((block, *earlier))[0]


def ring_order(size):
    return list(range(0, size, 2)) + list(range(size - 1, 0, -2))


def ring_step(block, way):
    order = ring_order(lax.axis_size("wide"))
    pairs = [(a, order[(i + way) % len(order)]) for i, a in enumerate(order)]
    return lax.ppermute(block, "wide", pairs)


class Ring:
    def __init__(self):
        self.arrived = []

    def step(self, *pair):
        held = self.arrived[-2] if len(self.arrived) > 1 else ((), ())
        up, down = (after(b, *h) for b, h in zip(pair, held))
        self.arrived.append(((ring_step(up, 1),), (ring_step(down, -1),)))
        return [self.arrived[-1][0][0], self.arrived[-1][1][0]]


def dot(a, b):
    return jnp.dot(a, b, preferred_element_type=F32)


def column(row):
    return jnp.transpose(jnp.broadcast_to(row, (128, row.shape[1])))[:, :1]


def whole(shape):
    return pl.BlockSpec(shape, lambda i, p: (0,) * len(shape))


def weight_spec(ds, rows, columns):
    def at(i, p):
        d = jnp.int32(ds[0])
        for j in range(1, len(ds)):
            d = jnp.where(i == j, ds[j], d)
        return (p[0] ^ d, 0)

    return pl.BlockSpec((rows, columns), at)


def add_products(x_refs, w_refs, add):
    for step, x_ref in enumerate(x_refs):

        @pl.when(pl.program_id(0) == step)
        def _():
            for j, w_ref in enumerate(w_refs):
                add(j, dot(x_ref[...], w_ref[...]))


def row_of(values):
    return jnp.transpose(jnp.broadcast_to(values, (values.shape[0], 128)))[:8]


def embed(p_ref, latent_ref, actions_ref, table_ref, gain_ref, tokens_out, block_out):
    shape = (table_ref.shape[0], latent_ref.shape[0])
    onehot = (lax.broadcasted_iota(jnp.int32, shape, 0) == actions_ref[...]).astype(BF16)
    picked = lax.dot_general(
        onehot, table_ref[...], (((0,), (0,)), ((), ())), preferred_element_type=F32
    )
    tokens = latent_ref[...].astype(F32) + picked
    tokens_out[...] = tokens
    count = latent_ref.shape[0]
    block_out[:count] = (tokens * gain_ref[...]).astype(BF16)
    block_out[count:] = jnp.zeros_like(block_out[count:])
    rest = row_of(jnp.sum(tokens * tokens, axis=1, keepdims=True))[:1]
    rows = lax.broadcasted_iota(jnp.int32, (16, count), 0)
    terms = jnp.zeros((16, count), F32)
    for k in range(3):
        term = rest.astype(BF16).astype(F32)
        terms = jnp.where(rows == k, term, terms)
        rest = rest - term
    block_out[count:, :count] = terms.astype(BF16)


def begin(near, far, p_ref, *refs):
    count = len(near)
    x_refs, weights, caches = refs[:count], refs[count : count + 3], refs[count + 3 : count + 5]
    acc, *outs, held, sems = refs[count + 5 :]
    size, cols = held.shape[1:]
    copies = []

    def send(src, dst):
        copies.append(pltpu.make_async_copy(src, dst, sems.at[len(copies)]))
        copies[-1].start()

    for i, d in enumerate(near + far):
        start = pl.multiple_of((p_ref[0] ^ d) * size, size)
        for j, w_ref in enumerate(weights):
            k = i * 3 + j
            send(
                w_ref.at[pl.ds(start, size)],
                held.at[k] if i < len(near) else outs[k - 3 * len(near)],
            )
    for src, dst in zip(caches, outs[-2:]):
        send(src, dst)
    for i in range(len(near)):
        for j in range(3):
            copies[i * 3 + j].wait()
            product = dot(x_refs[i][...], held[i * 3 + j])
            at = slice(j * cols, (j + 1) * cols)
            acc[:, at] = product if i == 0 else acc[:, at] + product
    for copy in copies[3 * len(near) :]:
        copy.wait()


def project_more(count, p_ref, acc_ref, *refs):
    x_refs, w_refs, out = refs[:count], refs[count:-1], refs[-1]
    cols = w_refs[0].shape[1]
    for j in range(3):
        at = slice(j * cols, (j + 1) * cols)
        total = acc_ref[:, at]
        for i, x_ref in enumerate(x_refs):
            total = total + dot(x_ref[...], w_refs[i * 3 + j][...])
        out[:, at] = total


def attend(count, sources, full_width, p_ref, acc_ref, keys_ref, values_ref, *refs):
    squares_refs, refs = refs[:sources], refs[sources:]
    project_more(count, p_ref, acc_ref, *refs[:-2], refs[-1])
    out, acc = refs[-2:]
    cols = refs[count].shape[1]
    squares = sum(jnp.sum(ref[:8].astype(F32), axis=0, keepdims=True) for ref in squares_refs)
    attend_heads(full_width, cols, squares, keys_ref, values_ref, out, acc)


def attend_heads(full_width, cols, squares, keys_ref, values_ref, out, acc):
    scenes = keys_ref.shape[0]
    branch = acc.shape[0] // scenes
    inverse = column(lax.rsqrt(squares / full_width + EPSILON))
    scaling = HD ** (-0.5)
    for s in range(scenes):
        rows = slice(s * branch, (s + 1) * branch)
        scale = inverse[rows]
        for h in range(cols // HD):
            at = slice(h * HD, (h + 1) * HD)
            q, k, v = (
                (acc[rows, j * cols + h * HD : j * cols + (h + 1) * HD] * scale).astype(BF16)
                for j in range(3)
            )
            scores = (
                lax.dot_general(
                    q,
                    keys_ref[s, :, at],
                    (((1,), (1,)), ((), ())),
                    preferred_element_type=F32,
                )
                * scaling
            )
            own = jnp.sum(q.astype(F32) * k.astype(F32), axis=1, keepdims=True) * scaling
            highest = jnp.maximum(jnp.max(scores, axis=1, keepdims=True), own)
            expd = jnp.exp(scores - highest)
            own_exp = jnp.exp(own - highest)
            total = jnp.sum(expd, axis=1, keepdims=True) + own_exp
            weights = (expd / total).astype(BF16)
            own_weight = (own_exp / total).astype(BF16)
            mixed = dot(weights, values_ref[s, :, at])
            mixed = mixed + own_weight.astype(F32) * v.astype(F32)
            out[rows, at] = mixed.astype(BF16)


def update_near(scenes, p_ref, tokens_ref, *refs):
    x_refs, w_ref, out = refs[:-2], refs[-2], refs[-1]
    for step in range(len(x_refs) // scenes):

        @pl.when(pl.program_id(0) == step)
        def _():
            x = jnp.concatenate(
                [ref[...] for ref in x_refs[step * scenes : (step + 1) * scenes]], axis=0
            )
            out[...] = (tokens_ref if step == 0 else out)[...] + dot(x, w_ref[...])


def update(count, p_ref, acc_ref, gain_ref, policy_ref, value_ref, *refs):
    x_refs, w_ref = refs[:count], refs[count]
    latent_out, keep_out, give_out, squares_out, turned_out, acc = refs[-6:]

    @pl.when(pl.program_id(0) == 0)
    def _():
        acc[...] = acc_ref[...]

    def add(j, product):
        acc[...] += product

    add_products(x_refs, [w_ref], add)

    @pl.when(pl.program_id(0) == count - 1)
    def _():
        state = acc[...]
        latent_out[...] = state.astype(BF16)
        squares = jnp.sum(state * state, axis=1, keepdims=True)
        squares_out[...] = row_of(squares)
        gained = (state * gain_ref[...]).astype(BF16)
        turned_out[...] = jnp.transpose(gained)
        policy = dot(gained, policy_ref[...])
        value = dot(gained, value_ref[...])

        @pl.when(p_ref[0] % 2 == 0)
        def _():
            keep_out[...] = policy
            give_out[...] = value.astype(BF16)

        @pl.when(p_ref[0] % 2 == 1)
        def _():
            keep_out[...] = value
            give_out[...] = policy.astype(BF16)


def heads(full_width, total_rows, p_ref, mine_ref, theirs_ref, squares_ref, policy_out_ref,
          value_out_ref, targets_ref, returns_ref, payload_out, give_out, hidden_ref):
    inverse = column(lax.rsqrt(squares_ref[:1] / full_width + EPSILON))
    pre = (mine_ref[...].astype(F32) + theirs_ref[...].astype(F32)) * inverse
    sigma = jax.nn.sigmoid(pre)
    hidden = (pre * sigma).astype(BF16)
    hidden_ref[...] = hidden
    slope = sigma * (1.0 + pre * (1.0 - sigma)) * inverse
    factor = total_rows ** (-0.5)
    count = hidden.shape[0]
    quarter = give_out.shape[0]
    part = 4 * quarter
    at = slice(count, count + quarter)

    def put_sums(grad, loss):
        shape = (payload_out.shape[0] - count - quarter, hidden.shape[1])
        rows = lax.broadcasted_iota(jnp.int32, shape, 0)
        lanes = lax.broadcasted_iota(jnp.int32, shape, 1)
        sums = jnp.where(rows == 0, grad, 0.0)
        for lane in range(3):
            term = loss.astype(BF16).astype(F32)
            sums = jnp.where((rows == 1) & (lanes == lane), term, sums)
            loss = loss - term
        payload_out[count + quarter :] = sums.astype(BF16)

    @pl.when(p_ref[0] % 2 == 0)
    def _():
        weight = policy_out_ref[...]
        logits = dot(hidden, weight)
        top = jnp.max(logits, axis=1, keepdims=True)
        log_total = top + jnp.log(jnp.sum(jnp.exp(logits - top), axis=1, keepdims=True))
        actions = lax.broadcasted_iota(jnp.int32, logits.shape, 1).astype(F32)
        onehot = (actions == column(targets_ref[...].astype(F32))).astype(F32)
        picked = jnp.sum(logits * onehot, axis=1, keepdims=True)
        loss = jnp.sum(log_total - picked, axis=0, keepdims=True)
        dlogits = ((jnp.exp(logits - log_total) - onehot) * factor).astype(BF16)
        back = lax.dot_general(
            dlogits, weight, (((1,), (1,)), ((), ())), preferred_element_type=F32
        )
        payload_out[:count] = (back * slope).astype(BF16)
        start = pl.multiple_of((p_ref[0] // 2) * part, part)
        grad = lax.dot_general(
            hidden_ref[:, pl.ds(start, part)],
            dlogits,
            (((0,), (0,)), ((), ())),
            preferred_element_type=F32,
        ).astype(BF16)
        parts = [grad[k * quarter : (k + 1) * quarter] for k in range(4)]
        payload_out[at] = jnp.concatenate(parts[:2], axis=1)
        give_out[...] = jnp.concatenate(parts[2:], axis=1)
        put_sums(jnp.zeros((1, hidden.shape[1]), F32), loss)

    @pl.when(p_ref[0] % 2 == 1)
    def _():
        weight = value_out_ref[...].astype(F32)
        hidden_f = hidden.astype(F32)
        value = jnp.sum(hidden_f * weight, axis=1, keepdims=True)
        errors = value - column(returns_ref[...])
        loss = 0.5 * jnp.sum(errors * errors, axis=0, keepdims=True)
        dvalue = (errors * factor).astype(BF16).astype(F32)
        payload_out[:count] = (dvalue * weight * slope).astype(BF16)
        payload_out[at] = jnp.zeros_like(give_out)
        give_out[...] = jnp.zeros_like(give_out)
        put_sums(jnp.sum(dvalue * hidden_f, axis=0, keepdims=True), loss)


def sums(total_rows, p_ref, *refs):
    count = (len(refs) - 3) // 4
    share_out, losses_out, grad_out = refs[-3:]

    def total(d_refs):
        *shards, ahead, back = [ref[...].astype(F32) for ref in d_refs]
        return sum(shards, jnp.concatenate([ahead, back], axis=1))

    own, other, own_sums, other_sums = (
        total(refs[k * count : (k + 1) * count]) for k in range(4)
    )
    first = p_ref[0] % 2 == 0
    quarter = own.shape[0]
    width = share_out.shape[1]
    for k, part in enumerate((jnp.where(first, own, other), jnp.where(first, other, own))):
        for j in range(2):
            at = (2 * k + j) * quarter
            share_out[at : at + quarter] = part[:, j * width : (j + 1) * width].astype(BF16)
    policy = jnp.where(first, own_sums, other_sums)
    value = jnp.where(first, other_sums, own_sums)
    grad_out[...] = value[0].astype(BF16)

    def loss(part):
        lanes = lax.broadcasted_iota(jnp.int32, (1, part.shape[1]), 1)
        return jnp.sum(jnp.where(lanes < 3, part[1:2], 0.0), axis=1, keepdims=True) / total_rows

    lanes = lax.broadcasted_iota(jnp.int32, (1, 2), 1)
    losses_out[...] = jnp.where(lanes == 0, loss(policy), loss(value))


def join(ds, p_ref, *refs):
    out = refs[-1]
    size = refs[0].shape[0]
    for d, ref in zip(ds, refs[:-1]):
        out[pl.ds(pl.multiple_of(((p_ref[0] ^ d) // 2) * size, size), size)] = ref[...]


def factors(turned_refs, own_refs, other_refs, halved):
    turned = jnp.concatenate([ref[...] for ref in turned_refs], axis=1)
    for d_refs in (own_refs, other_refs):
        shards = [ref[...] for ref in d_refs]
        if halved:
            shards[-2:] = [jnp.concatenate(shards[-2:], axis=1)]
        yield dot(turned, jnp.concatenate(shards, axis=0))


def gradients_start(turned_count, count, p_ref, *refs):
    turned, own, other = refs[:turned_count], refs[turned_count:][:count], refs[turned_count + count : -2]
    for out, product in zip(refs[-2:], factors(turned, own, other, False)):
        out[...] = product


def gradients_end(turned_count, count, p_ref, *refs):
    sums, refs, outs = refs[:2], refs[2:-2], refs[-2:]
    turned, own, other = refs[:turned_count], refs[turned_count:][:count], refs[turned_count + count :]
    own, other = (
        (acc[...] + product).astype(BF16)
        for acc, product in zip(sums, factors(turned, own, other, True))
    )

    @pl.when(p_ref[0] % 2 == 0)
    def _():
        outs[0][...] = own
        outs[1][...] = other

    @pl.when(p_ref[0] % 2 == 1)
    def _():
        outs[1][...] = own
        outs[0][...] = other


def call(body, name, place, steps, operands, in_specs, outs, out_specs, flops, limit, scratch=(), aliases=None):
    bytes_accessed = sum(x.size * x.dtype.itemsize for x in (*operands, *outs)) if flops else 0
    return pl.pallas_call(
        body,
        name=name,
        out_shape=outs,
        input_output_aliases=aliases or {},
        grid_spec=pltpu.PrefetchScalarGridSpec(
            num_scalar_prefetch=1,
            grid=(steps,),
            in_specs=in_specs,
            out_specs=out_specs,
            scratch_shapes=scratch,
        ),
        compiler_params=pltpu.CompilerParams(
            dimension_semantics=("arbitrary",), vmem_limit_bytes=limit
        ),
        cost_estimate=pl.CostEstimate(
            flops=flops, bytes_accessed=bytes_accessed, transcendentals=0
        ),
    )(place, *operands)


def per_device(
    latent,
    actions,
    action_table,
    norm1_gain,
    w_query,
    w_key,
    w_value,
    w_out,
    key_cache,
    value_cache,
    norm2_gain,
    policy_in,
    value_in,
    policy_out,
    value_out,
    targets,
    returns,
):
    rows, width = latent.shape
    narrow_size = lax.axis_size("narrow")
    wide_size = lax.axis_size("wide")
    full_width = width * narrow_size
    cols = w_query.shape[1]
    total_rows = rows * wide_size
    action_count = action_table.shape[0]
    hidden_count = policy_in.shape[1]
    index = lax.axis_index("narrow").astype(jnp.int32)
    place = index[None]
    first = index % 2 == 0
    chips = narrow_size // 2
    near = [0, 1]
    direct = list(range(2, narrow_size, 2))
    passed = [d + 1 for d in direct]

    far = direct + passed
    scenes = key_cache.shape[0]
    branch = rows // scenes
    hbm = functools.partial(pltpu.with_memory_space_constraint, memory_space=pltpu.HBM)

    block_shape = (rows + 16, width)
    tokens, block = call(
        embed, "embed", place, 1,
        [
            hbm(latent), hbm(actions[None, :]), hbm(action_table),
            hbm(norm1_gain[None, :]),
        ],
        [
            whole((rows, width)), whole((1, rows)), whole(action_table.shape),
            whole((1, width)),
        ],
        [
            jax.ShapeDtypeStruct((rows, width), F32),
            jax.ShapeDtypeStruct(block_shape, BF16),
        ],
        [whole((rows, width)), whole(block_shape)],
        2 * rows * width * action_count, 16 * MIB,
    )
    blocks = {**far_blocks(block), 1: swap(block, 1)}

    weights = [hbm(w) for w in (w_query, w_key, w_value)]
    x_spec = whole((rows, width))
    acc_shape = jax.ShapeDtypeStruct((rows, 3 * cols), F32)
    weight_shape = jax.ShapeDtypeStruct((width, cols), BF16)
    weight_block = whole((width, cols))
    cache_shape = jax.ShapeDtypeStruct(key_cache.shape, BF16)
    outs = [weight_shape] * (3 * len(far)) + [cache_shape] * 2
    anywhere = pl.BlockSpec(memory_space=pl.ANY)
    flops = 2 * rows * width * 3 * cols
    acc, *staged, keys, values = call(
        functools.partial(begin, near, far), "begin", place, 1,
        [
            *(blocks[d] for d in near), *weights,
            hbm(key_cache), hbm(value_cache),
        ],
        [*[x_spec] * len(near), *[anywhere] * 5],
        [acc_shape, *outs], [whole(acc_shape.shape), *[anywhere] * len(outs)],
        flops * len(near), 20 * MIB,
        [
            pltpu.VMEM((3 * len(near), width, cols), BF16),
            pltpu.SemaphoreType.DMA((3 * len(near) + len(outs),)),
        ],
    )
    staged_direct = staged[: 3 * len(direct)]
    staged_passed = staged[3 * len(direct) :]

    acc_spec = whole(acc_shape.shape)
    blocks = pass_blocks(blocks, acc)
    acc = call(
        functools.partial(project_more, len(direct)), "project", place, 1,
        [acc, *(blocks[d] for d in direct), *staged_direct],
        [acc_spec, *[x_spec] * len(direct), *[weight_block] * len(staged_direct)],
        [acc_shape], [acc_spec], flops * len(direct), 24 * MIB,
    )[0]

    attended = []
    for s in range(scenes):
        at = functools.partial(lambda s, i, p: (s, 0), s)
        squares_spec = pl.BlockSpec(
            (16, branch), functools.partial(lambda s, i, p: (rows // 16, s), s)
        )
        cache_spec = pl.BlockSpec(
            (1, *key_cache.shape[1:]), functools.partial(lambda s, i, p: (s, 0, 0), s)
        )
        one = call(
            functools.partial(attend, len(passed), narrow_size, full_width), f"attend{s}", place, 1,
            [
                acc, keys, values, *blocks.values(),
                *(blocks[d] for d in passed), *staged_passed,
            ],
            [
                pl.BlockSpec((branch, 3 * cols), at), cache_spec, cache_spec,
                *[squares_spec] * narrow_size,
                *[pl.BlockSpec((branch, width), at)] * len(passed), *[weight_block] * len(staged_passed),
            ],
            [jax.ShapeDtypeStruct((branch, cols), BF16)], [whole((branch, cols))],
            0, 20 * MIB, [pltpu.VMEM((branch, 3 * cols), F32)],
        )[0]
        attended.append({**far_blocks(one), 1: swap(one, 1)})

    half = (rows, hidden_count)
    full_shapes = [
        jax.ShapeDtypeStruct((rows, width), BF16),
        jax.ShapeDtypeStruct(half, F32),
        jax.ShapeDtypeStruct(half, BF16),
        jax.ShapeDtypeStruct((8, rows), F32),
    ]
    chunk = whole((branch, cols))
    acc = call(
        functools.partial(update_near, scenes), "update_near", place, len(near),
        [tokens, *(one[d] for d in near for one in attended), w_out],
        [
            whole((rows, width)), *[chunk] * (scenes * len(near)),
            weight_spec(near, cols, width),
        ],
        [jax.ShapeDtypeStruct((rows, width), F32)], [whole((rows, width))],
        2 * rows * width * cols * len(near), 16 * MIB,
    )[0]
    filled, turned, shards = [], [], []
    ring = Ring()
    for s in range(scenes):
        ds = far
        around = pass_blocks(attended[s], *turned)
        at = functools.partial(lambda s, i, p: (s, 0), s)
        operands = [
            acc, norm2_gain[None, :], policy_in, value_in,
            *(around[d] for d in ds), w_out, *filled,
        ]
        *filled, one = call(
            functools.partial(update, len(ds)), f"update{s}", place, len(ds), operands,
            [
                pl.BlockSpec((branch, width), at),
                whole((1, width)), whole(policy_in.shape), whole(value_in.shape),
                *[chunk] * len(ds), weight_spec(ds, cols, width),
                *[anywhere] * len(filled),
            ],
            [*full_shapes, jax.ShapeDtypeStruct((width, branch), BF16)],
            [
                pl.BlockSpec((branch, width), at),
                pl.BlockSpec((branch, hidden_count), at),
                pl.BlockSpec((branch, hidden_count), at),
                pl.BlockSpec((8, branch), functools.partial(lambda s, i, p: (0, s), s)),
                whole((width, branch)),
            ],
            2 * branch * width * (cols * len(ds) + 2 * hidden_count), 28 * MIB,
            [pltpu.VMEM((branch, width), F32)],
            {1 + len(operands) - len(filled) + k: k for k in range(len(filled))},
        )
        turned.append(one)
        if s == 0:
            shards.append([ring.step(one, one)])
    new_latent, keep, give, squares = filled

    for bit in (1, *far_bits()):
        squares = squares + swap(squares, bit)
    pre = keep + swap(after(give, *shards[0][0]), 1).astype(F32)
    mine = pre.astype(BF16)
    *upper, last = far_bits()
    for bit in upper:
        mine = (mine.astype(F32) + swap(mine, bit).astype(F32)).astype(BF16)
    rounds = wide_size // 2
    shards += [[ring.step(one, one)] for one in turned[1:]]
    for shard in shards:
        shard.append(ring.step(*shard[-1]))
    theirs = after(swap(mine, last), *shards[0][-1], *(b for one in shards for b in one[0]))
    quarter = hidden_count // chips // 4
    payload_shape = (rows + quarter + 16, hidden_count)
    payload, give = call(
        functools.partial(heads, full_width, total_rows), "heads", place, 1,
        [
            mine, theirs, squares, policy_out, value_out[None, :], targets[None, :],
            returns[None, :],
        ],
        [
            whole(half), whole(half), whole((8, rows)), whole(policy_out.shape),
            whole((1, hidden_count)), whole((1, rows)), whole((1, rows)),
        ],
        [
            jax.ShapeDtypeStruct(payload_shape, BF16),
            jax.ShapeDtypeStruct((quarter, hidden_count), BF16),
        ],
        [whole(payload_shape), whole((quarter, hidden_count))],
        6 * rows * hidden_count * action_count, 16 * MIB, [pltpu.VMEM(half, BF16)],
    )
    taken = jnp.where(first, payload[rows : rows + quarter], swap(give, 1))
    payload = lax.dynamic_update_slice(payload, taken, (rows, 0))

    payload_rounds = [[payload, payload]]
    for step in range(2, rounds - 1):
        for shard in shards:
            if len(payload_rounds) < rounds:
                payload_rounds.append(ring.step(*payload_rounds[-1]))
            shard.append(ring.step(*shard[-1]))
    while len(payload_rounds) < rounds:
        payload_rounds.append(ring.step(*payload_rounds[-1]))
    cut = scenes // 2
    for one, other in zip(shards[:cut], shards[cut:]):
        up, down = ring.step(one[-1][0], other[-1][1])
        one.append([up])
        other.append([down])
    size = hidden_count // 2
    up, down = payload_rounds[-1]
    payload_rounds.append(ring.step(up[:, :size], down[:, size:]))
    turned_all = list(turned)
    for step in range(rounds):
        for way in range(len(shards[0][step])):
            turned_all += [shard[step][way] for shard in shards]
    payload_own = [payload, *(b for pair in payload_rounds[1:] for b in pair)]
    payload_other = [swap(b, 1) for b in payload_own]

    pieces = [*payload_own, *payload_other]
    share_shape = (4 * quarter, action_count)
    share, losses, value_out_grad = call(
        functools.partial(sums, total_rows), "sums", place, 1, [*pieces, *pieces],
        [
            pl.BlockSpec((count, b.shape[1]), functools.partial(lambda at, i, p: (at, 0), start // count))
            for start, count in ((rows, quarter), (rows + quarter, 16))
            for b in pieces
        ],
        [
            jax.ShapeDtypeStruct(share_shape, BF16),
            jax.ShapeDtypeStruct((1, 2), F32),
            jax.ShapeDtypeStruct((hidden_count,), BF16),
        ],
        [whole(share_shape), whole((1, 2)), whole((hidden_count,))], 0, 8 * MIB,
    )
    losses = losses.reshape(2)
    shares = far_blocks(share)
    policy_out_grad = call(
        functools.partial(join, list(shares)), "join", place, 1, list(shares.values()),
        [whole(share_shape)] * len(shares),
        [jax.ShapeDtypeStruct((hidden_count, action_count), BF16)],
        [whole((hidden_count, action_count))], 0, 8 * MIB,
    )[0]

    block = 256
    grad_spec = pl.BlockSpec((block, hidden_count), lambda i, p: (i, 0))
    grad_flops = 4 * rows * width * hidden_count
    split = wide_size - 3

    def gradient(body, name, operands, specs, count, turned, own, other, dtype):
        return call(
            functools.partial(body, len(turned), len(own)), name, place, width // block,
            [*operands, *turned, *own, *other],
            [
                *specs,
                *[pl.BlockSpec((block, branch), lambda i, p: (i, 0))] * len(turned),
                *[
                    pl.BlockSpec(
                        (rows, b.shape[1]), lambda i, p: (0, 0), pipeline_mode=pl.Buffered(1)
                    )
                    for b in (*own, *other)
                ],
            ],
            [jax.ShapeDtypeStruct((width, hidden_count), dtype)] * 2, [grad_spec] * 2,
            grad_flops * count, 18 * MIB,
        )

    starts = gradient(
        gradients_start, "gradients_start", [], [], split, turned_all[: scenes * split],
        payload_own[:split], payload_other[:split], F32,
    )
    policy_in_grad, value_in_grad = gradient(
        gradients_end, "gradients_end", starts, [grad_spec] * 2, wide_size - split,
        turned_all[scenes * split :], payload_own[split:], payload_other[split:], BF16,
    )
    return (new_latent, losses, policy_in_grad, value_in_grad, policy_out_grad, value_out_grad)


def solution(mesh):
    placed = (
        P("wide", "narrow"),
        P("wide"),
        P(None, "narrow"),
        P("narrow"),
        P(None, "narrow"),
        P(None, "narrow"),
        P(None, "narrow"),
        P(None, "narrow"),
        P("wide", None, "narrow"),
        P("wide", None, "narrow"),
        P("narrow"),
        P("narrow", None),
        P("narrow", None),
        P(),
        P(),
        P("wide"),
        P("wide"),
    )
    return jax.shard_map(
        per_device,
        mesh=mesh,
        in_specs=placed,
        out_specs=(P("wide", "narrow"), P(), P("narrow", None), P("narrow", None), P(), P()),
        check_vma=False,
    )
```

profile of v0, /device:TPU:0, one launch (start us, length us, event | category | flops | bytes accessed | tf_op | source)
XLA Modules:
  0.0 124.4 jit_solution(3744884081460131764)
XLA Ops:
  0.6 1.7 %embed.1 = (f32[256,1024]{1,0:T(8,128)S(1)}, bf16[272,1024]{1,0:T(8,128)(2,1)S(1)}) custom-call(s32[1]{0:T(128)} %bitcast.p_ref, bf16[256,1024]{1,0:T(8,128)(2,1)} %latent_ref.1, s32[1,256]{1,0:T(1,128)} %bitcast.12, bf16[256,1024]{1,0:T(8,128)(2,1)} %table_ref.1, f32[1,1024]{1,0:T(1,128)} %bitcast.11), custom_call_target="tpu_custom_call" | custom-call | flops 134217728 | bytes 2659328 | tf_op jit(solution)/shard_map/embed/pallas_call | solution.py:394
  2.4 0.5 collective-permute-start
  2.9 2.6 %collective-permute-start.1 = (bf16[272,1024]{1,0:T(8,128)(2,1)S(1)}, bf16[272,1024]{1,0:T(8,128)(2,1)S(1)}, u32[]{:S(2)}, u32[]{:S(2)}) collective-permute-start(bf16[272,1024]{1,0:T(8,128)(2,1)S(1)} %get-tuple-element.59.refs_0_), channel_id=1, source_target_pairs={{0,2},{1,3},{2,0},{3,1},{4,6},{5,7},{6,4},{7,5},{8,10},{9,11},{10,... | collective-permute-start | bytes 1671176 | tf_op jit(solution)/shard_map/ppermute | solution.py:19
  5.5 5.3 %begin.1 = (f32[256,1536]{1,0:T(8,128)S(1)}, bf16[1024,512]{1,0:T(8,128)(2,1)S(1)}, bf16[1024,512]{1,0:T(8,128)(2,1)S(1)}, bf16[1024,512]{1,0:T(8,128)(2,1)S(1)}...) custom-call(s32[1]{0:T(128)} %bitcast.p_ref, ...), custom_call_target="tpu_custom_call" | custom-call | flops 1610612736 | bytes 25755648 | tf_op jit(solution)/shard_map/begin/pallas_call | solution.py:394
  10.8 7.9 %collective-permute-done.1.refs_0_.refs_1_ = bf16[272,1024]{1,0:T(8,128)(2,1)S(1)} collective-permute-done((bf16[272,1024]{1,0:T(8,128)(2,1)S(1)}, bf16[272,1024]{1,0:T(8,128)(2,1)S(1)}, u32[]{:S(2)}, u32[]{:S(2)}) %collective-permute-start.1) | collective-permute-done | bytes 557088 | tf_op jit(solution)/shard_map/ppermute | solution.py:19
  18.7 1.0 project.1.acc_ref
  19.7 1.0 collective-permute-done.2.refs_3_.refs_4_
  20.6 2.0 %attend0.1.refs_0_ = bf16[128,512]{1,0:T(8,128)(2,1)S(1)} custom-call(s32[1]{0:T(128)} %bitcast.p_ref, f32[256,1536]{1,0:T(8,128)S(1)} %project.1.acc_ref, bf16[2,512,512]{2,1,0:T(8,128)(2,1)S(1)} %get-tuple-element.64.keys_ref, bf16[2,512,512]{2,1,0:T(8,128)(2,1)S(1)} %get-tuple-element.65.values_ref, bf16[272,1024]{1,0:T(8,128)(2,1)S(1)} %get-tuple-element.59.refs_0_, ...), custom_call_target="tpu_custom_call" | custom-call | tf_op jit(solution)/shard_map/attend0/pallas_call | solution.py:394
  22.7 1.8 %collective-permute-start.6 = (bf16[128,512]{1,0:T(8,128)(2,1)S(1)}, bf16[128,512]{1,0:T(8,128)(2,1)S(1)}, u32[]{:S(2)}, u32[]{:S(2)}) collective-permute-start(bf16[128,512]{1,0:T(8,128)(2,1)S(1)} %attend0.1.refs_0_), channel_id=1, source_target_pairs={{0,2},{1,3},{2,0},{3,1},{4,6},{5,7},{6,4},{7,5},{8,10},{9,11},{10,... | collective-permute-start | bytes 393224 | tf_op jit(solution)/shard_map/ppermute | solution.py:19
  24.5 2.0 %attend1.1.refs_1_ = bf16[128,512]{1,0:T(8,128)(2,1)S(1)} custom-call(s32[1]{0:T(128)} %bitcast.p_ref, f32[256,1536]{1,0:T(8,128)S(1)} %project.1.acc_ref, bf16[2,512,512]{2,1,0:T(8,128)(2,1)S(1)} %get-tuple-element.64.keys_ref, bf16[2,512,512]{2,1,0:T(8,128)(2,1)S(1)} %get-tuple-element.65.values_ref, bf16[272,1024]{1,0:T(8,128)(2,1)S(1)} %get-tuple-element.59.refs_0_, ...), custom_call_target="tpu_custom_call" | custom-call | tf_op jit(solution)/shard_map/attend1/pallas_call | solution.py:394
  26.5 0.6 collective-permute-start.4
  27.1 1.2 collective-permute-done.6.refs_0_
  28.3 1.7 %collective-permute-start.5 = (bf16[128,512]{1,0:T(8,128)(2,1)S(1)}, bf16[128,512]{1,0:T(8,128)(2,1)S(1)}, u32[]{:S(2)}, u32[]{:S(2)}) collective-permute-start(bf16[128,512]{1,0:T(8,128)(2,1)S(1)} %attend1.1.refs_1_), channel_id=1, source_target_pairs={{0,2},{1,3},{2,0},{3,1},{4,6},{5,7},{6,4},{7,5},{8,10},{9,11},{10,... | collective-permute-start | bytes 393224 | tf_op jit(solution)/shard_map/ppermute | solution.py:19
  30.0 1.0 update_near.1.acc_ref
  31.0 1.8 %update0.1 = (bf16[256,1024]{1,0:T(8,128)(2,1)}, f32[256,512]{1,0:T(8,128)S(1)}, bf16[256,512]{1,0:T(8,128)(2,1)S(1)}, f32[8,256]{1,0:T(8,128)S(1)}, bf16[1024,128]{1,0:T(8,128)(2,1)S(1)}) custom-call(s32[1]{0:T(128)} %bitcast.p_ref, f32[256,1024]{1,0:T(8,128)S(1)} %update_near.1.acc_ref, f32[1,1024]{1,0:T(1,128)S(1)} %bitcast.7, ...), custom_call_target="tpu_custom_call" | custom-call | flops 536870912 | bytes 9187328 | tf_op jit(solution)/shard_map/update0/pallas_call | solution.py:394
  32.8 1.6 %collective-permute-start.9 = (bf16[1024,128]{1,0:T(8,128)(2,1)S(1)}, bf16[1024,128]{1,0:T(8,128)(2,1)S(1)}, u32[]{:S(2)}, u32[]{:S(2)}) collective-permute-start(bf16[1024,128]{1,0:T(8,128)(2,1)S(1)} %get-tuple-element.70.refs_0_), channel_id=1, source_target_pairs={{0,8},{8,16},{16,24},{24,28},{28,20},{20,12},{12,4},{4,0},{1,9},{9... | collective-permute-start | bytes 786440 | tf_op jit(solution)/shard_map/ppermute | solution.py:52
  34.4 0.5 collective-permute-start.10
  34.8 1.3 %collective-permute-done.8.refs_1_ = bf16[128,512]{1,0:T(8,128)(2,1)S(1)} collective-permute-done((bf16[128,512]{1,0:T(8,128)(2,1)S(1)}, bf16[128,512]{1,0:T(8,128)(2,1)S(1)}, u32[]{:S(2)}, u32[]{:S(2)}) %collective-permute-start.8) | collective-permute-done | bytes 131104 | tf_op jit(solution)/shard_map/ppermute | solution.py:19
  36.2 1.8 %update1.1 = (bf16[256,1024]{1,0:T(8,128)(2,1)}, f32[256,512]{1,0:T(8,128)S(1)}, bf16[256,512]{1,0:T(8,128)(2,1)S(1)}, f32[8,256]{1,0:T(8,128)S(1)}, bf16[1024,128]{1,0:T(8,128)(2,1)S(1)}) custom-call(s32[1]{0:T(128)} %bitcast.p_ref, f32[256,1024]{1,0:T(8,128)S(1)} %update_near.1.acc_ref, ...), custom_call_target="tpu_custom_call", output_to_operand_aliasing={{0}: (8, {}), {1}: (9, {}), {2}: (10, {}), {3}: (11, {})} | custom-call | flops 536870912 | bytes 10506240 | tf_op jit(solution)/shard_map/update1/pallas_call | solution.py:394
  38.0 3.3 %collective-permute-done.9.refs_2_ = bf16[1024,128]{1,0:T(8,128)(2,1)S(1)} collective-permute-done((bf16[1024,128]{1,0:T(8,128)(2,1)S(1)}, bf16[1024,128]{1,0:T(8,128)(2,1)S(1)}, u32[]{:S(2)}, u32[]{:S(2)}) %collective-permute-start.9) | collective-permute-done | bytes 262176 | tf_op jit(solution)/shard_map/ppermute | solution.py:52
  41.3 1.3 %collective-permute-done.10.refs_4_ = bf16[1024,128]{1,0:T(8,128)(2,1)S(1)} collective-permute-done((bf16[1024,128]{1,0:T(8,128)(2,1)S(1)}, bf16[1024,128]{1,0:T(8,128)(2,1)S(1)}, u32[]{:S(2)}, u32[]{:S(2)}) %collective-permute-start.10) | collective-permute-done | bytes 262176 | tf_op jit(solution)/shard_map/ppermute | solution.py:52
  42.6 0.5 collective-permute-start.17
  43.1 1.6 %collective-permute-start.15 = (bf16[1024,128]{1,0:T(8,128)(2,1)S(1)}, bf16[1024,128]{1,0:T(8,128)(2,1)S(1)}, u32[]{:S(2)}, u32[]{:S(2)}) collective-permute-start(bf16[1024,128]{1,0:T(8,128)(2,1)S(1)} %get-tuple-element.82.refs_1_), channel_id=1, source_target_pairs={{0,8},{8,16},{16,24},{24,28},{28,20},{20,12},{12,4},{4,0},{1,9},{9... | collective-permute-start | bytes 786440 | tf_op jit(solution)/shard_map/ppermute | solution.py:52
  45.1 0.5 collective-permute-start.18
  45.6 1.6 %collective-permute-start.13 = (bf16[1024,128]{1,0:T(8,128)(2,1)S(1)}, bf16[1024,128]{1,0:T(8,128)(2,1)S(1)}, u32[]{:S(2)}, u32[]{:S(2)}) collective-permute-start(bf16[1024,128]{1,0:T(8,128)(2,1)S(1)} %collective-permute-done.9.refs_2_), channel_id=1, source_target_pairs={{0,8},{8,16},{16,24},{24,28},{28,20},{20,12},{12,4},{4,0},{1,9},{9... | collective-permute-start | bytes 786440 | tf_op jit(solution)/shard_map/ppermute | solution.py:52
  47.7 1.0 collective-permute-done.18
  48.8 0.6 collective-permute-start.12
  49.3 2.9 %collective-permute-done.15.refs_3_ = bf16[1024,128]{1,0:T(8,128)(2,1)S(1)} collective-permute-done((bf16[1024,128]{1,0:T(8,128)(2,1)S(1)}, bf16[1024,128]{1,0:T(8,128)(2,1)S(1)}, u32[]{:S(2)}, u32[]{:S(2)}) %collective-permute-start.15) | collective-permute-done | bytes 262176 | tf_op jit(solution)/shard_map/ppermute | solution.py:52
  52.2 1.6 %collective-permute-done.16.refs_5_ = bf16[1024,128]{1,0:T(8,128)(2,1)S(1)} collective-permute-done((bf16[1024,128]{1,0:T(8,128)(2,1)S(1)}, bf16[1024,128]{1,0:T(8,128)(2,1)S(1)}, u32[]{:S(2)}, u32[]{:S(2)}) %collective-permute-start.16) | collective-permute-done | bytes 262176 | tf_op jit(solution)/shard_map/ppermute | solution.py:52
  53.9 3.0 %collective-permute-done.13.refs_6_ = bf16[1024,128]{1,0:T(8,128)(2,1)S(1)} collective-permute-done((bf16[1024,128]{1,0:T(8,128)(2,1)S(1)}, bf16[1024,128]{1,0:T(8,128)(2,1)S(1)}, u32[]{:S(2)}, u32[]{:S(2)}) %collective-permute-start.13) | collective-permute-done | bytes 262176 | tf_op jit(solution)/shard_map/ppermute | solution.py:52
  56.9 1.3 %collective-permute-done.14.refs_8_ = bf16[1024,128]{1,0:T(8,128)(2,1)S(1)} collective-permute-done((bf16[1024,128]{1,0:T(8,128)(2,1)S(1)}, bf16[1024,128]{1,0:T(8,128)(2,1)S(1)}, u32[]{:S(2)}, u32[]{:S(2)}) %collective-permute-start.14) | collective-permute-done | bytes 262176 | tf_op jit(solution)/shard_map/ppermute | solution.py:52
  58.2 1.1 heads.1
  59.4 1.2 collective-permute-done.19
  60.7 1.6 %collective-permute-start.20 = (bf16[336,512]{1,0:T(8,128)(2,1)S(1)}, bf16[336,512]{1,0:T(8,128)(2,1)S(1)}, u32[]{:S(2)}, u32[]{:S(2)}) collective-permute-start(bf16[336,512]{1,0:T(8,128)(2,1)S(1)} %select_dynamic-update-slice_fusion.refs_0_.refs_18_.refs_10_), channel_id=1, source_target_pairs={{0,8},{8,16},{16,24},{24,28},{28,20},{20,12},{12,4},{4,0},{1,9},{9... | collective-permute-start | bytes 1032200 | tf_op jit(solution)/shard_map/ppermute | solution.py:52
  62.8 1.6 %collective-permute-start.37 = (bf16[1024,128]{1,0:T(8,128)(2,1)S(1)}, bf16[1024,128]{1,0:T(8,128)(2,1)S(1)}, u32[]{:S(2)}, u32[]{:S(2)}) collective-permute-start(bf16[1024,128]{1,0:T(8,128)(2,1)S(1)} %collective-permute-done.15.refs_3_), channel_id=1, source_target_pairs={{0,8},{8,16},{16,24},{24,28},{28,20},{20,12},{12,4},{4,0},{1,9},{9... | collective-permute-start | bytes 786440 | tf_op jit(solution)/shard_map/ppermute | solution.py:52
  64.8 11.7 %collective-permute-done.37.refs_7_ = bf16[1024,128]{1,0:T(8,128)(2,1)S(1)} collective-permute-done((bf16[1024,128]{1,0:T(8,128)(2,1)S(1)}, bf16[1024,128]{1,0:T(8,128)(2,1)S(1)}, u32[]{:S(2)}, u32[]{:S(2)}) %collective-permute-start.37) | collective-permute-done | bytes 262176 | tf_op jit(solution)/shard_map/ppermute | solution.py:52
  76.5 1.6 %collective-permute-start.39 = (bf16[1024,128]{1,0:T(8,128)(2,1)S(1)}, bf16[1024,128]{1,0:T(8,128)(2,1)S(1)}, u32[]{:S(2)}, u32[]{:S(2)}) collective-permute-start(bf16[1024,128]{1,0:T(8,128)(2,1)S(1)} %collective-permute-done.13.refs_6_), channel_id=1, source_target_pairs={{0,8},{8,16},{16,24},{24,28},{28,20},{20,12},{12,4},{4,0},{1,9},{9... | collective-permute-start | bytes 786440 | tf_op jit(solution)/shard_map/ppermute | solution.py:52
  78.1 1.5 %collective-permute-start.22 = (bf16[336,512]{1,0:T(8,128)(2,1)S(1)}, bf16[336,512]{1,0:T(8,128)(2,1)S(1)}, u32[]{:S(2)}, u32[]{:S(2)}) collective-permute-start(bf16[336,512]{1,0:T(8,128)(2,1)S(1)} %collective-permute-done.20.refs_1_.refs_19_.refs_11_), channel_id=1, source_target_pairs={{0,8},{8,16},{16,24},{24,28},{28,20},{20,12},{12,4},{4,0},{1,9},{9... | collective-permute-start | bytes 1032200 | tf_op jit(solution)/shard_map/ppermute | solution.py:52
  79.6 0.5 collective-permute-start.41
  80.6 5.2 %collective-permute-done.39.refs_2_ = bf16[1024,128]{1,0:T(8,128)(2,1)S(1)} collective-permute-done((bf16[1024,128]{1,0:T(8,128)(2,1)S(1)}, bf16[1024,128]{1,0:T(8,128)(2,1)S(1)}, u32[]{:S(2)}, u32[]{:S(2)}) %collective-permute-start.39) | collective-permute-done | bytes 262176 | tf_op jit(solution)/shard_map/ppermute | solution.py:52
  85.7 1.6 %collective-permute-start.40 = (bf16[1024,128]{1,0:T(8,128)(2,1)S(1)}, bf16[1024,128]{1,0:T(8,128)(2,1)S(1)}, u32[]{:S(2)}, u32[]{:S(2)}) collective-permute-start(bf16[1024,128]{1,0:T(8,128)(2,1)S(1)} %collective-permute-done.37.refs_7_), channel_id=1, source_target_pairs={{0,8},{8,16},{16,24},{24,28},{28,20},{20,12},{12,4},{4,0},{1,9},{9... | collective-permute-start | bytes 786440 | tf_op jit(solution)/shard_map/ppermute | solution.py:52
  87.3 1.5 %collective-permute-done.41.refs_4_ = bf16[1024,128]{1,0:T(8,128)(2,1)S(1)} collective-permute-done((bf16[1024,128]{1,0:T(8,128)(2,1)S(1)}, bf16[1024,128]{1,0:T(8,128)(2,1)S(1)}, u32[]{:S(2)}, u32[]{:S(2)}) %collective-permute-start.41) | collective-permute-done | bytes 262176 | tf_op jit(solution)/shard_map/ppermute | solution.py:52
  88.8 0.5 collective-permute-start.42
  89.4 3.8 %collective-permute-done.22.refs_3_.refs_21_.refs_13_ = bf16[336,512]{1,0:T(8,128)(2,1)S(1)} collective-permute-done((bf16[336,512]{1,0:T(8,128)(2,1)S(1)}, bf16[336,512]{1,0:T(8,128)(2,1)S(1)}, u32[]{:S(2)}, u32[]{:S(2)}) %collective-permute-start.22) | collective-permute-done | bytes 344096 | tf_op jit(solution)/shard_map/ppermute | solution.py:52
  93.1 3.1 %collective-permute-done.23.refs_4_.refs_22_.refs_14_ = bf16[336,512]{1,0:T(8,128)(2,1)S(1)} collective-permute-done((bf16[336,512]{1,0:T(8,128)(2,1)S(1)}, bf16[336,512]{1,0:T(8,128)(2,1)S(1)}, u32[]{:S(2)}, u32[]{:S(2)}) %collective-permute-start.23) | collective-permute-done | bytes 344096 | tf_op jit(solution)/shard_map/ppermute | solution.py:52
  96.2 0.5 collective-permute-start.24
  96.7 1.1 collective-permute-done.40.refs_3_
  97.8 0.5 collective-permute-start.25
  98.2 2.8 %collective-permute-done.42.refs_5_ = bf16[1024,128]{1,0:T(8,128)(2,1)S(1)} collective-permute-done((bf16[1024,128]{1,0:T(8,128)(2,1)S(1)}, bf16[1024,128]{1,0:T(8,128)(2,1)S(1)}, u32[]{:S(2)}, u32[]{:S(2)}) %collective-permute-start.42) | collective-permute-done | bytes 262176 | tf_op jit(solution)/shard_map/ppermute | solution.py:52
  101.0 0.5 collective-permute-start.31
  101.6 2.8 %collective-permute-done.24.refs_5_.refs_23_.refs_8_ = bf16[336,512]{1,0:T(8,128)(2,1)S(1)} collective-permute-done((bf16[336,512]{1,0:T(8,128)(2,1)S(1)}, bf16[336,512]{1,0:T(8,128)(2,1)S(1)}, u32[]{:S(2)}, u32[]{:S(2)}) %collective-permute-start.24) | collective-permute-done | bytes 344096 | tf_op jit(solution)/shard_map/ppermute | solution.py:52
  104.4 2.5 %collective-permute-done.25.refs_6_.refs_24_.refs_9_ = bf16[336,512]{1,0:T(8,128)(2,1)S(1)} collective-permute-done((bf16[336,512]{1,0:T(8,128)(2,1)S(1)}, bf16[336,512]{1,0:T(8,128)(2,1)S(1)}, u32[]{:S(2)}, u32[]{:S(2)}) %collective-permute-start.25) | collective-permute-done | bytes 344096 | tf_op jit(solution)/shard_map/ppermute | solution.py:52
  106.9 0.5 collective-permute-start.26
  107.4 1.6 %collective-permute-start.27 = (bf16[336,256]{1,0:T(8,128)(2,1)S(1)}, bf16[336,256]{1,0:T(8,128)(2,1)S(1)}, u32[]{:S(2)}, u32[]{:S(2)}) collective-permute-start(bf16[336,256]{1,0:T(8,128)(2,1)S(1)} %slice.13), channel_id=1, source_target_pairs={{0,4},{8,0},{16,8},{24,16},{28,24},{20,28},{12,20},{4,12},{1,5},{9... | collective-permute-start | bytes 516104 | tf_op jit(solution)/shard_map/ppermute | solution.py:52
  109.0 0.5 collective-permute-start.43
  109.5 2.9 %collective-permute-done.26.refs_7_.refs_25_.refs_10_ = bf16[336,256]{1,0:T(8,128)(2,1)S(1)} collective-permute-done((bf16[336,256]{1,0:T(8,128)(2,1)S(1)}, bf16[336,256]{1,0:T(8,128)(2,1)S(1)}, u32[]{:S(2)}, u32[]{:S(2)}) %collective-permute-start.26) | collective-permute-done | bytes 172064 | tf_op jit(solution)/shard_map/ppermute | solution.py:52
  112.4 0.5 collective-permute-start.44
  113.4 0.5 collective-permute-start.36
  113.9 3.4 %gradients_start.1 = (f32[1024,512]{1,0:T(8,128)S(1)}, f32[1024,512]{1,0:T(8,128)S(1)}) custom-call(s32[1]{0:T(128)} %bitcast.p_ref, bf16[1024,128]{1,0:T(8,128)(2,1)S(1)} %get-tuple-element.70.refs_0_, bf16[1024,128]{1,0:T(8,128)(2,1)S(1)} %get-tuple-element.82.refs_1_, bf16[1024,128]{1,0:T(8,128)(2,1)S(1)} %collective-permute-done.9.refs_2_, ...), custom_call_target="tpu_custom_call" | custom-call | flops 2684354560 | bytes 10256384 | tf_op jit(solution)/shard_map/gradients_start/pallas_call | solution.py:394
  117.4 0.8 sums.1
  118.2 0.5 collective-permute-start.45
  118.8 3.5 %gradients_end.1 = (bf16[1024,512]{1,0:T(8,128)(2,1)}, bf16[1024,512]{1,0:T(8,128)(2,1)}) custom-call(s32[1]{0:T(128)} %bitcast.p_ref, f32[1024,512]{1,0:T(8,128)S(1)} %get-tuple-element.98.refs_0_, f32[1024,512]{1,0:T(8,128)S(1)} %get-tuple-element.99.refs_1_, bf16[1024,128]{1,0:T(8,128)(2,1)S(1)} %collective-permute-done.39.refs_2_, ...), custom_call_target="tpu_custom_call" | custom-call | flops 1610612736 | bytes 9928704 | tf_op jit(solution)/shard_map/gradients_end/pallas_call | solution.py:394
  122.3 1.3 %collective-permute-done.45.refs_1_ = bf16[256,256]{1,0:T(8,128)(2,1)S(1)} collective-permute-done((bf16[256,256]{1,0:T(8,128)(2,1)S(1)}, bf16[256,256]{1,0:T(8,128)(2,1)S(1)}, u32[]{:S(2)}, u32[]{:S(2)}) %collective-permute-start.45) | collective-permute-done | bytes 131104 | tf_op jit(solution)/shard_map/ppermute | solution.py:19
  123.6 0.7 join.1
  (64 shorter events, 3.1 us)
Async XLA Ops:
  2.4 3.1 %collective-permute-start = (bf16[272,1024]{1,0:T(8,128)(2,1)S(1)}, bf16[272,1024]{1,0:T(8,128)(2,1)S(1)}, u32[]{:S(2)}, u32[]{:S(2)}) collective-permute-start(bf16[272,1024]{1,0:T(8,128)(2,1)S(1)} %get-tuple-element.59.refs_0_), channel_id=1, source_target_pairs={{0,1},{1,0},{2,3},{3,2},{4,5},{5,4},{6,7},{7,6},{8,9},{9,8},{10,11... | collective-permute-start | bytes 1671176 | tf_op jit(solution)/shard_map/ppermute | solution.py:19
  2.9 15.8 %collective-permute-start.1 = (bf16[272,1024]{1,0:T(8,128)(2,1)S(1)}, bf16[272,1024]{1,0:T(8,128)(2,1)S(1)}, u32[]{:S(2)}, u32[]{:S(2)}) collective-permute-start(bf16[272,1024]{1,0:T(8,128)(2,1)S(1)} %get-tuple-element.59.refs_0_), channel_id=1, source_target_pairs={{0,2},{1,3},{2,0},{3,1},{4,6},{5,7},{6,4},{7,5},{8,10},{9,11},{10,... | collective-permute-start | bytes 1671176 | tf_op jit(solution)/shard_map/ppermute | solution.py:19
  18.7 2.0 %collective-permute-start.2 = (bf16[272,1024]{1,0:T(8,128)(2,1)S(1)}, bf16[272,1024]{1,0:T(8,128)(2,1)S(1)}, u32[]{:S(2)}, u32[]{:S(2)}) collective-permute-start(bf16[272,1024]{1,0:T(8,128)(2,1)S(1)} %collective-permute-done.1.refs_0_.refs_1_), channel_id=1, source_target_pairs={{0,1},{1,0},{2,3},{3,2},{4,5},{5,4},{6,7},{7,6},{8,9},{9,8},{10,11... | collective-permute-start | bytes 1671176 | tf_op jit(solution)/shard_map/ppermute | solution.py:19
  22.7 7.4 %copy-start = (bf16[2048,1024]{1,0:T(8,128)(2,1)S(1)}, bf16[2048,1024]{1,0:T(8,128)(2,1)}, u32[]{:S(2)}) copy-start(bf16[2048,1024]{1,0:T(8,128)(2,1)} %refs_2_.5) | copy-start | bytes 12582916
  22.7 5.6 %collective-permute-start.6 = (bf16[128,512]{1,0:T(8,128)(2,1)S(1)}, bf16[128,512]{1,0:T(8,128)(2,1)S(1)}, u32[]{:S(2)}, u32[]{:S(2)}) collective-permute-start(bf16[128,512]{1,0:T(8,128)(2,1)S(1)} %attend0.1.refs_0_), channel_id=1, source_target_pairs={{0,2},{1,3},{2,0},{3,1},{4,6},{5,7},{6,4},{7,5},{8,10},{9,11},{10,... | collective-permute-start | bytes 393224 | tf_op jit(solution)/shard_map/ppermute | solution.py:19
  24.5 5.5 %collective-permute-start.3 = (bf16[128,512]{1,0:T(8,128)(2,1)S(1)}, bf16[128,512]{1,0:T(8,128)(2,1)S(1)}, u32[]{:S(2)}, u32[]{:S(2)}) collective-permute-start(bf16[128,512]{1,0:T(8,128)(2,1)S(1)} %attend0.1.refs_0_), channel_id=1, source_target_pairs={{0,1},{1,0},{2,3},{3,2},{4,5},{5,4},{6,7},{7,6},{8,9},{9,8},{10,11... | collective-permute-start | bytes 393224 | tf_op jit(solution)/shard_map/ppermute | solution.py:19
  26.5 4.5 %copy-start.1 = (bf16[1024,512]{1,0:T(8,128)(2,1)S(1)}, bf16[1024,512]{1,0:T(8,128)(2,1)}, u32[]{:S(2)}) copy-start(bf16[1024,512]{1,0:T(8,128)(2,1)} %policy_ref.3) | copy-start | bytes 3145732
  26.5 4.5 %copy-start.2 = (bf16[1024,512]{1,0:T(8,128)(2,1)S(1)}, bf16[1024,512]{1,0:T(8,128)(2,1)}, u32[]{:S(2)}) copy-start(bf16[1024,512]{1,0:T(8,128)(2,1)} %value_ref.3) | copy-start | bytes 3145732
  26.5 4.5 %copy-start.4 = (f32[1024]{0:T(1024)S(1)}, f32[1024]{0:T(1024)}, u32[]{:S(2)}) copy-start(f32[1024]{0:T(1024)} %param.27) | copy-start | bytes 12292
  26.5 3.5 %collective-permute-start.4 = (bf16[128,512]{1,0:T(8,128)(2,1)S(1)}, bf16[128,512]{1,0:T(8,128)(2,1)S(1)}, u32[]{:S(2)}, u32[]{:S(2)}) collective-permute-start(bf16[128,512]{1,0:T(8,128)(2,1)S(1)} %attend1.1.refs_1_), channel_id=1, source_target_pairs={{0,1},{1,0},{2,3},{3,2},{4,5},{5,4},{6,7},{7,6},{8,9},{9,8},{10,11... | collective-permute-start | bytes 393224 | tf_op jit(solution)/shard_map/ppermute | solution.py:19
  28.3 2.7 %collective-permute-start.7 = (bf16[128,512]{1,0:T(8,128)(2,1)S(1)}, bf16[128,512]{1,0:T(8,128)(2,1)S(1)}, u32[]{:S(2)}, u32[]{:S(2)}) collective-permute-start(bf16[128,512]{1,0:T(8,128)(2,1)S(1)} %collective-permute-done.6.refs_0_), channel_id=1, source_target_pairs={{0,1},{1,0},{2,3},{3,2},{4,5},{5,4},{6,7},{7,6},{8,9},{9,8},{10,11... | collective-permute-start | bytes 393224 | tf_op jit(solution)/shard_map/ppermute | solution.py:19
  28.3 6.6 %collective-permute-start.5 = (bf16[128,512]{1,0:T(8,128)(2,1)S(1)}, bf16[128,512]{1,0:T(8,128)(2,1)S(1)}, u32[]{:S(2)}, u32[]{:S(2)}) collective-permute-start(bf16[128,512]{1,0:T(8,128)(2,1)S(1)} %attend1.1.refs_1_), channel_id=1, source_target_pairs={{0,2},{1,3},{2,0},{3,1},{4,6},{5,7},{6,4},{7,5},{8,10},{9,11},{10,... | collective-permute-start | bytes 393224 | tf_op jit(solution)/shard_map/ppermute | solution.py:19
  32.8 8.5 %collective-permute-start.9 = (bf16[1024,128]{1,0:T(8,128)(2,1)S(1)}, bf16[1024,128]{1,0:T(8,128)(2,1)S(1)}, u32[]{:S(2)}, u32[]{:S(2)}) collective-permute-start(bf16[1024,128]{1,0:T(8,128)(2,1)S(1)} %get-tuple-element.70.refs_0_), channel_id=1, source_target_pairs={{0,8},{8,16},{16,24},{24,28},{28,20},{20,12},{12,4},{4,0},{1,9},{9... | collective-permute-start | bytes 786440 | tf_op jit(solution)/shard_map/ppermute | solution.py:52
  34.4 8.2 %collective-permute-start.10 = (bf16[1024,128]{1,0:T(8,128)(2,1)S(1)}, bf16[1024,128]{1,0:T(8,128)(2,1)S(1)}, u32[]{:S(2)}, u32[]{:S(2)}) collective-permute-start(bf16[1024,128]{1,0:T(8,128)(2,1)S(1)} %get-tuple-element.70.refs_0_), channel_id=1, source_target_pairs={{0,4},{8,0},{16,8},{24,16},{28,24},{20,28},{12,20},{4,12},{1,5},{9... | collective-permute-start | bytes 786440 | tf_op jit(solution)/shard_map/ppermute | solution.py:52
  34.8 1.3 %collective-permute-start.8 = (bf16[128,512]{1,0:T(8,128)(2,1)S(1)}, bf16[128,512]{1,0:T(8,128)(2,1)S(1)}, u32[]{:S(2)}, u32[]{:S(2)}) collective-permute-start(bf16[128,512]{1,0:T(8,128)(2,1)S(1)} %collective-permute-done.5.refs_0_), channel_id=1, source_target_pairs={{0,1},{1,0},{2,3},{3,2},{4,5},{5,4},{6,7},{7,6},{8,9},{9,8},{10,11... | collective-permute-start | bytes 393224 | tf_op jit(solution)/shard_map/ppermute | solution.py:19
  36.2 13.1 %copy-start.7 = (bf16[512]{0:T(512)(128)(2,1)S(1)}, bf16[512]{0:T(512)(128)(2,1)}, u32[]{:S(2)}) copy-start(bf16[512]{0:T(512)(128)(2,1)} %param.31) | copy-start | bytes 3076
  36.2 22.0 %copy-start.3 = (bf16[512,256]{1,0:T(8,128)(2,1)S(1)}, bf16[512,256]{1,0:T(8,128)(2,1)}, u32[]{:S(2)}) copy-start(bf16[512,256]{1,0:T(8,128)(2,1)} %policy_out_ref.1) | copy-start | bytes 786436
  36.2 22.0 %copy-start.5 = (s32[256]{0:T(256)S(1)}, s32[256]{0:T(256)}, u32[]{:S(2)}) copy-start(s32[256]{0:T(256)} %param.32) | copy-start | bytes 3076
  36.2 22.0 %copy-start.6 = (f32[256]{0:T(256)S(1)}, f32[256]{0:T(256)}, u32[]{:S(2)}) copy-start(f32[256]{0:T(256)} %param.33) | copy-start | bytes 3076
  42.6 4.6 %collective-permute-start.11 = (bf16[256,512]{1,0:T(8,128)(2,1)S(1)}, bf16[256,512]{1,0:T(8,128)(2,1)S(1)}, u32[]{:S(2)}, u32[]{:S(2)}) collective-permute-start(bf16[256,512]{1,0:T(8,128)(2,1)S(1)} %get-tuple-element.79), channel_id=1, source_target_pairs={{0,1},{1,0},{2,3},{3,2},{4,5},{5,4},{6,7},{7,6},{8,9},{9,8},{10,11... | collective-permute-start | bytes 786440 | tf_op jit(solution)/shard_map/ppermute | solution.py:19
  42.6 2.5 %collective-permute-start.17 = (f32[8,256]{1,0:T(8,128)S(1)}, f32[8,256]{1,0:T(8,128)S(1)}, u32[]{:S(2)}, u32[]{:S(2)}) collective-permute-start(f32[8,256]{1,0:T(8,128)S(1)} %get-tuple-element.84), channel_id=1, source_target_pairs={{0,1},{1,0},{2,3},{3,2},{4,5},{5,4},{6,7},{7,6},{8,9},{9,8},{10,11... | collective-permute-start | bytes 24584 | tf_op jit(solution)/shard_map/ppermute | solution.py:19
  43.1 9.2 %collective-permute-start.15 = (bf16[1024,128]{1,0:T(8,128)(2,1)S(1)}, bf16[1024,128]{1,0:T(8,128)(2,1)S(1)}, u32[]{:S(2)}, u32[]{:S(2)}) collective-permute-start(bf16[1024,128]{1,0:T(8,128)(2,1)S(1)} %get-tuple-element.82.refs_1_), channel_id=1, source_target_pairs={{0,8},{8,16},{16,24},{24,28},{28,20},{20,12},{12,4},{4,0},{1,9},{9... | collective-permute-start | bytes 786440 | tf_op jit(solution)/shard_map/ppermute | solution.py:52
  44.6 9.2 %collective-permute-start.16 = (bf16[1024,128]{1,0:T(8,128)(2,1)S(1)}, bf16[1024,128]{1,0:T(8,128)(2,1)S(1)}, u32[]{:S(2)}, u32[]{:S(2)}) collective-permute-start(bf16[1024,128]{1,0:T(8,128)(2,1)S(1)} %get-tuple-element.82.refs_1_), channel_id=1, source_target_pairs={{0,4},{8,0},{16,8},{24,16},{28,24},{20,28},{12,20},{4,12},{1,5},{9... | collective-permute-start | bytes 786440 | tf_op jit(solution)/shard_map/ppermute | solution.py:52
  45.1 3.7 %collective-permute-start.18 = (f32[8,256]{1,0:T(8,128)S(1)}, f32[8,256]{1,0:T(8,128)S(1)}, u32[]{:S(2)}, u32[]{:S(2)}) collective-permute-start(f32[8,256]{1,0:T(8,128)S(1)} %add.14), channel_id=1, source_target_pairs={{0,2},{1,3},{2,0},{3,1},{4,6},{5,7},{6,4},{7,5},{8,10},{9,11},{10,... | collective-permute-start | bytes 24584 | tf_op jit(solution)/shard_map/ppermute | solution.py:19
  45.6 11.3 %collective-permute-start.13 = (bf16[1024,128]{1,0:T(8,128)(2,1)S(1)}, bf16[1024,128]{1,0:T(8,128)(2,1)S(1)}, u32[]{:S(2)}, u32[]{:S(2)}) collective-permute-start(bf16[1024,128]{1,0:T(8,128)(2,1)S(1)} %collective-permute-done.9.refs_2_), channel_id=1, source_target_pairs={{0,8},{8,16},{16,24},{24,28},{28,20},{20,12},{12,4},{4,0},{1,9},{9... | collective-permute-start | bytes 786440 | tf_op jit(solution)/shard_map/ppermute | solution.py:52
  47.2 11.0 %collective-permute-start.14 = (bf16[1024,128]{1,0:T(8,128)(2,1)S(1)}, bf16[1024,128]{1,0:T(8,128)(2,1)S(1)}, u32[]{:S(2)}, u32[]{:S(2)}) collective-permute-start(bf16[1024,128]{1,0:T(8,128)(2,1)S(1)} %collective-permute-done.10.refs_4_), channel_id=1, source_target_pairs={{0,4},{8,0},{16,8},{24,16},{28,24},{20,28},{12,20},{4,12},{1,5},{9... | collective-permute-start | bytes 786440 | tf_op jit(solution)/shard_map/ppermute | solution.py:52
  48.8 9.4 %collective-permute-start.12 = (bf16[256,512]{1,0:T(8,128)(2,1)S(1)}, bf16[256,512]{1,0:T(8,128)(2,1)S(1)}, u32[]{:S(2)}, u32[]{:S(2)}) collective-permute-start(bf16[256,512]{1,0:T(8,128)(2,1)S(1)} %add_convert_fusion.mine_ref), channel_id=1, source_target_pairs={{0,2},{1,3},{2,0},{3,1},{4,6},{5,7},{6,4},{7,5},{8,10},{9,11},{10,... | collective-permute-start | bytes 786440 | tf_op jit(solution)/shard_map/ppermute | solution.py:19
  59.4 1.3 %collective-permute-start.19 = (bf16[64,512]{1,0:T(8,128)(2,1)S(1)}, bf16[64,512]{1,0:T(8,128)(2,1)S(1)}, u32[]{:S(2)}, u32[]{:S(2)}) collective-permute-start(bf16[64,512]{1,0:T(8,128)(2,1)S(1)} %get-tuple-element.86), channel_id=1, source_target_pairs={{0,1},{1,0},{2,3},{3,2},{4,5},{5,4},{6,7},{7,6},{8,9},{9,8},{10,11... | collective-permute-start | bytes 196616 | tf_op jit(solution)/shard_map/ppermute | solution.py:19
  60.7 17.4 %collective-permute-start.20 = (bf16[336,512]{1,0:T(8,128)(2,1)S(1)}, bf16[336,512]{1,0:T(8,128)(2,1)S(1)}, u32[]{:S(2)}, u32[]{:S(2)}) collective-permute-start(bf16[336,512]{1,0:T(8,128)(2,1)S(1)} %select_dynamic-update-slice_fusion.refs_0_.refs_18_.refs_10_), channel_id=1, source_target_pairs={{0,8},{8,16},{16,24},{24,28},{28,20},{20,12},{12,4},{4,0},{1,9},{9... | collective-permute-start | bytes 1032200 | tf_op jit(solution)/shard_map/ppermute | solution.py:52
  62.3 17.8 %collective-permute-start.21 = (bf16[336,512]{1,0:T(8,128)(2,1)S(1)}, bf16[336,512]{1,0:T(8,128)(2,1)S(1)}, u32[]{:S(2)}, u32[]{:S(2)}) collective-permute-start(bf16[336,512]{1,0:T(8,128)(2,1)S(1)} %select_dynamic-update-slice_fusion.refs_0_.refs_18_.refs_10_), channel_id=1, source_target_pairs={{0,4},{8,0},{16,8},{24,16},{28,24},{20,28},{12,20},{4,12},{1,5},{9... | collective-permute-start | bytes 1032200 | tf_op jit(solution)/shard_map/ppermute | solution.py:52
  62.8 13.7 %collective-permute-start.37 = (bf16[1024,128]{1,0:T(8,128)(2,1)S(1)}, bf16[1024,128]{1,0:T(8,128)(2,1)S(1)}, u32[]{:S(2)}, u32[]{:S(2)}) collective-permute-start(bf16[1024,128]{1,0:T(8,128)(2,1)S(1)} %collective-permute-done.15.refs_3_), channel_id=1, source_target_pairs={{0,8},{8,16},{16,24},{24,28},{28,20},{20,12},{12,4},{4,0},{1,9},{9... | collective-permute-start | bytes 786440 | tf_op jit(solution)/shard_map/ppermute | solution.py:52
  64.4 15.2 %collective-permute-start.38 = (bf16[1024,128]{1,0:T(8,128)(2,1)S(1)}, bf16[1024,128]{1,0:T(8,128)(2,1)S(1)}, u32[]{:S(2)}, u32[]{:S(2)}) collective-permute-start(bf16[1024,128]{1,0:T(8,128)(2,1)S(1)} %collective-permute-done.16.refs_5_), channel_id=1, source_target_pairs={{0,4},{8,0},{16,8},{24,16},{28,24},{20,28},{12,20},{4,12},{1,5},{9... | collective-permute-start | bytes 786440 | tf_op jit(solution)/shard_map/ppermute | solution.py:52
  76.5 9.2 %collective-permute-start.39 = (bf16[1024,128]{1,0:T(8,128)(2,1)S(1)}, bf16[1024,128]{1,0:T(8,128)(2,1)S(1)}, u32[]{:S(2)}, u32[]{:S(2)}) collective-permute-start(bf16[1024,128]{1,0:T(8,128)(2,1)S(1)} %collective-permute-done.13.refs_6_), channel_id=1, source_target_pairs={{0,8},{8,16},{16,24},{24,28},{28,20},{20,12},{12,4},{4,0},{1,9},{9... | collective-permute-start | bytes 786440 | tf_op jit(solution)/shard_map/ppermute | solution.py:52
  78.1 15.0 %collective-permute-start.22 = (bf16[336,512]{1,0:T(8,128)(2,1)S(1)}, bf16[336,512]{1,0:T(8,128)(2,1)S(1)}, u32[]{:S(2)}, u32[]{:S(2)}) collective-permute-start(bf16[336,512]{1,0:T(8,128)(2,1)S(1)} %collective-permute-done.20.refs_1_.refs_19_.refs_11_), channel_id=1, source_target_pairs={{0,8},{8,16},{16,24},{24,28},{28,20},{20,12},{12,4},{4,0},{1,9},{9... | collective-permute-start | bytes 1032200 | tf_op jit(solution)/shard_map/ppermute | solution.py:52
  79.6 9.2 %collective-permute-start.41 = (bf16[1024,128]{1,0:T(8,128)(2,1)S(1)}, bf16[1024,128]{1,0:T(8,128)(2,1)S(1)}, u32[]{:S(2)}, u32[]{:S(2)}) collective-permute-start(bf16[1024,128]{1,0:T(8,128)(2,1)S(1)} %collective-permute-done.14.refs_8_), channel_id=1, source_target_pairs={{0,4},{8,0},{16,8},{24,16},{28,24},{20,28},{12,20},{4,12},{1,5},{9... | collective-permute-start | bytes 786440 | tf_op jit(solution)/shard_map/ppermute | solution.py:52
  80.1 16.1 %collective-permute-start.23 = (bf16[336,512]{1,0:T(8,128)(2,1)S(1)}, bf16[336,512]{1,0:T(8,128)(2,1)S(1)}, u32[]{:S(2)}, u32[]{:S(2)}) collective-permute-start(bf16[336,512]{1,0:T(8,128)(2,1)S(1)} %collective-permute-done.21.refs_2_.refs_20_.refs_12_), channel_id=1, source_target_pairs={{0,4},{8,0},{16,8},{24,16},{28,24},{20,28},{12,20},{4,12},{1,5},{9... | collective-permute-start | bytes 1032200 | tf_op jit(solution)/shard_map/ppermute | solution.py:52
  85.7 12.0 %collective-permute-start.40 = (bf16[1024,128]{1,0:T(8,128)(2,1)S(1)}, bf16[1024,128]{1,0:T(8,128)(2,1)S(1)}, u32[]{:S(2)}, u32[]{:S(2)}) collective-permute-start(bf16[1024,128]{1,0:T(8,128)(2,1)S(1)} %collective-permute-done.37.refs_7_), channel_id=1, source_target_pairs={{0,8},{8,16},{16,24},{24,28},{28,20},{20,12},{12,4},{4,0},{1,9},{9... | collective-permute-start | bytes 786440 | tf_op jit(solution)/shard_map/ppermute | solution.py:52
  87.3 13.7 %collective-permute-start.28 = (bf16[336,512]{1,0:T(8,128)(2,1)S(1)}, bf16[336,512]{1,0:T(8,128)(2,1)S(1)}, u32[]{:S(2)}, u32[]{:S(2)}) collective-permute-start(bf16[336,512]{1,0:T(8,128)(2,1)S(1)} %select_dynamic-update-slice_fusion.refs_0_.refs_18_.refs_10_), channel_id=1, source_target_pairs={{0,1},{1,0},{2,3},{3,2},{4,5},{5,4},{6,7},{7,6},{8,9},{9,8},{10,11... | collective-permute-start | bytes 1032200 | tf_op jit(solution)/shard_map/ppermute | solution.py:19
  88.8 12.2 %collective-permute-start.42 = (bf16[1024,128]{1,0:T(8,128)(2,1)S(1)}, bf16[1024,128]{1,0:T(8,128)(2,1)S(1)}, u32[]{:S(2)}, u32[]{:S(2)}) collective-permute-start(bf16[1024,128]{1,0:T(8,128)(2,1)S(1)} %collective-permute-done.38.refs_9_), channel_id=1, source_target_pairs={{0,4},{8,0},{16,8},{24,16},{28,24},{20,28},{12,20},{4,12},{1,5},{9... | collective-permute-start | bytes 786440 | tf_op jit(solution)/shard_map/ppermute | solution.py:52
  93.1 8.4 %collective-permute-start.29 = (bf16[336,512]{1,0:T(8,128)(2,1)S(1)}, bf16[336,512]{1,0:T(8,128)(2,1)S(1)}, u32[]{:S(2)}, u32[]{:S(2)}) collective-permute-start(bf16[336,512]{1,0:T(8,128)(2,1)S(1)} %collective-permute-done.20.refs_1_.refs_19_.refs_11_), channel_id=1, source_target_pairs={{0,1},{1,0},{2,3},{3,2},{4,5},{5,4},{6,7},{7,6},{8,9},{9,8},{10,11... | collective-permute-start | bytes 1032200 | tf_op jit(solution)/shard_map/ppermute | solution.py:19
  96.2 8.2 %collective-permute-start.24 = (bf16[336,512]{1,0:T(8,128)(2,1)S(1)}, bf16[336,512]{1,0:T(8,128)(2,1)S(1)}, u32[]{:S(2)}, u32[]{:S(2)}) collective-permute-start(bf16[336,512]{1,0:T(8,128)(2,1)S(1)} %collective-permute-done.22.refs_3_.refs_21_.refs_13_), channel_id=1, source_target_pairs={{0,8},{8,16},{16,24},{24,28},{28,20},{20,12},{12,4},{4,0},{1,9},{9... | collective-permute-start | bytes 1032200 | tf_op jit(solution)/shard_map/ppermute | solution.py:52
  97.8 9.2 %collective-permute-start.25 = (bf16[336,512]{1,0:T(8,128)(2,1)S(1)}, bf16[336,512]{1,0:T(8,128)(2,1)S(1)}, u32[]{:S(2)}, u32[]{:S(2)}) collective-permute-start(bf16[336,512]{1,0:T(8,128)(2,1)S(1)} %collective-permute-done.23.refs_4_.refs_22_.refs_14_), channel_id=1, source_target_pairs={{0,4},{8,0},{16,8},{24,16},{28,24},{20,28},{12,20},{4,12},{1,5},{9... | collective-permute-start | bytes 1032200 | tf_op jit(solution)/shard_map/ppermute | solution.py:52
  101.0 6.4 %collective-permute-start.30 = (bf16[336,512]{1,0:T(8,128)(2,1)S(1)}, bf16[336,512]{1,0:T(8,128)(2,1)S(1)}, u32[]{:S(2)}, u32[]{:S(2)}) collective-permute-start(bf16[336,512]{1,0:T(8,128)(2,1)S(1)} %collective-permute-done.21.refs_2_.refs_20_.refs_12_), channel_id=1, source_target_pairs={{0,1},{1,0},{2,3},{3,2},{4,5},{5,4},{6,7},{7,6},{8,9},{9,8},{10,11... | collective-permute-start | bytes 1032200 | tf_op jit(solution)/shard_map/ppermute | solution.py:19
  101.0 8.0 %collective-permute-start.31 = (bf16[336,512]{1,0:T(8,128)(2,1)S(1)}, bf16[336,512]{1,0:T(8,128)(2,1)S(1)}, u32[]{:S(2)}, u32[]{:S(2)}) collective-permute-start(bf16[336,512]{1,0:T(8,128)(2,1)S(1)} %collective-permute-done.22.refs_3_.refs_21_.refs_13_), channel_id=1, source_target_pairs={{0,1},{1,0},{2,3},{3,2},{4,5},{5,4},{6,7},{7,6},{8,9},{9,8},{10,11... | collective-permute-start | bytes 1032200 | tf_op jit(solution)/shard_map/ppermute | solution.py:19
  101.5 7.5 %collective-permute-start.32 = (bf16[336,512]{1,0:T(8,128)(2,1)S(1)}, bf16[336,512]{1,0:T(8,128)(2,1)S(1)}, u32[]{:S(2)}, u32[]{:S(2)}) collective-permute-start(bf16[336,512]{1,0:T(8,128)(2,1)S(1)} %collective-permute-done.23.refs_4_.refs_22_.refs_14_), channel_id=1, source_target_pairs={{0,1},{1,0},{2,3},{3,2},{4,5},{5,4},{6,7},{7,6},{8,9},{9,8},{10,11... | collective-permute-start | bytes 1032200 | tf_op jit(solution)/shard_map/ppermute | solution.py:19
  104.4 9.0 %collective-permute-start.33 = (bf16[336,512]{1,0:T(8,128)(2,1)S(1)}, bf16[336,512]{1,0:T(8,128)(2,1)S(1)}, u32[]{:S(2)}, u32[]{:S(2)}) collective-permute-start(bf16[336,512]{1,0:T(8,128)(2,1)S(1)} %collective-permute-done.24.refs_5_.refs_23_.refs_8_), channel_id=1, source_target_pairs={{0,1},{1,0},{2,3},{3,2},{4,5},{5,4},{6,7},{7,6},{8,9},{9,8},{10,11... | collective-permute-start | bytes 1032200 | tf_op jit(solution)/shard_map/ppermute | solution.py:19
  106.9 5.5 %collective-permute-start.26 = (bf16[336,256]{1,0:T(8,128)(2,1)S(1)}, bf16[336,256]{1,0:T(8,128)(2,1)S(1)}, u32[]{:S(2)}, u32[]{:S(2)}) collective-permute-start(bf16[336,256]{1,0:T(8,128)(2,1)S(1)} %slice.12), channel_id=1, source_target_pairs={{0,8},{8,16},{16,24},{24,28},{28,20},{20,12},{12,4},{4,0},{1,9},{9... | collective-permute-start | bytes 516104 | tf_op jit(solution)/shard_map/ppermute | solution.py:52
  107.4 6.0 %collective-permute-start.27 = (bf16[336,256]{1,0:T(8,128)(2,1)S(1)}, bf16[336,256]{1,0:T(8,128)(2,1)S(1)}, u32[]{:S(2)}, u32[]{:S(2)}) collective-permute-start(bf16[336,256]{1,0:T(8,128)(2,1)S(1)} %slice.13), channel_id=1, source_target_pairs={{0,4},{8,0},{16,8},{24,16},{28,24},{20,28},{12,20},{4,12},{1,5},{9... | collective-permute-start | bytes 516104 | tf_op jit(solution)/shard_map/ppermute | solution.py:52
  109.0 8.3 %collective-permute-start.34 = (bf16[336,512]{1,0:T(8,128)(2,1)S(1)}, bf16[336,512]{1,0:T(8,128)(2,1)S(1)}, u32[]{:S(2)}, u32[]{:S(2)}) collective-permute-start(bf16[336,512]{1,0:T(8,128)(2,1)S(1)} %collective-permute-done.25.refs_6_.refs_24_.refs_9_), channel_id=1, source_target_pairs={{0,1},{1,0},{2,3},{3,2},{4,5},{5,4},{6,7},{7,6},{8,9},{9,8},{10,11... | collective-permute-start | bytes 1032200 | tf_op jit(solution)/shard_map/ppermute | solution.py:19
  109.0 9.7 %collective-permute-start.43 = (bf16[1024,128]{1,0:T(8,128)(2,1)S(1)}, bf16[1024,128]{1,0:T(8,128)(2,1)S(1)}, u32[]{:S(2)}, u32[]{:S(2)}) collective-permute-start(bf16[1024,128]{1,0:T(8,128)(2,1)S(1)} %collective-permute-done.39.refs_2_), channel_id=1, source_target_pairs={{0,8},{8,16},{16,24},{24,28},{28,20},{20,12},{12,4},{4,0},{1,9},{9... | collective-permute-start | bytes 786440 | tf_op jit(solution)/shard_map/ppermute | solution.py:52
  112.4 6.4 %collective-permute-start.44 = (bf16[1024,128]{1,0:T(8,128)(2,1)S(1)}, bf16[1024,128]{1,0:T(8,128)(2,1)S(1)}, u32[]{:S(2)}, u32[]{:S(2)}) collective-permute-start(bf16[1024,128]{1,0:T(8,128)(2,1)S(1)} %collective-permute-done.42.refs_5_), channel_id=1, source_target_pairs={{0,4},{8,0},{16,8},{24,16},{28,24},{20,28},{12,20},{4,12},{1,5},{9... | collective-permute-start | bytes 786440 | tf_op jit(solution)/shard_map/ppermute | solution.py:52
  113.4 4.0 %collective-permute-start.35 = (bf16[336,256]{1,0:T(8,128)(2,1)S(1)}, bf16[336,256]{1,0:T(8,128)(2,1)S(1)}, u32[]{:S(2)}, u32[]{:S(2)}) collective-permute-start(bf16[336,256]{1,0:T(8,128)(2,1)S(1)} %collective-permute-done.26.refs_7_.refs_25_.refs_10_), channel_id=1, source_target_pairs={{0,1},{1,0},{2,3},{3,2},{4,5},{5,4},{6,7},{7,6},{8,9},{9,8},{10,11... | collective-permute-start | bytes 516104 | tf_op jit(solution)/shard_map/ppermute | solution.py:19
  113.4 4.0 %collective-permute-start.36 = (bf16[336,256]{1,0:T(8,128)(2,1)S(1)}, bf16[336,256]{1,0:T(8,128)(2,1)S(1)}, u32[]{:S(2)}, u32[]{:S(2)}) collective-permute-start(bf16[336,256]{1,0:T(8,128)(2,1)S(1)} %collective-permute-done.27.refs_8_.refs_26_.refs_11_), channel_id=1, source_target_pairs={{0,1},{1,0},{2,3},{3,2},{4,5},{5,4},{6,7},{7,6},{8,9},{9,8},{10,11... | collective-permute-start | bytes 516104 | tf_op jit(solution)/shard_map/ppermute | solution.py:19
  118.2 5.4 %collective-permute-start.45 = (bf16[256,256]{1,0:T(8,128)(2,1)S(1)}, bf16[256,256]{1,0:T(8,128)(2,1)S(1)}, u32[]{:S(2)}, u32[]{:S(2)}) collective-permute-start(bf16[256,256]{1,0:T(8,128)(2,1)S(1)} %get-tuple-element.108.refs_0_), channel_id=1, source_target_pairs={{0,2},{1,3},{2,0},{3,1},{4,6},{5,7},{6,4},{7,5},{8,10},{9,11},{10,... | collective-permute-start | bytes 393224 | tf_op jit(solution)/shard_map/ppermute | solution.py:19
where the time goes:
time: 124 us
  waiting for transfers between devices  66.2 us (53%)
  starting transfers between devices  30.8 us (25%)
  Pallas kernels  26.2 us (21%)
    ppermute x22, waiting for transfers between devices, ring_step(): return lax.ppermute(block, 'wide', pairs)  51.3 us
    pallas_call x13, Pallas kernels, call(): pl.pallas_call(body, name=name, out_shape=outs, input_output_aliases=alia...  26.2 us
    ppermute x22, starting transfers between devices, ring_step(): return lax.ppermute(block, 'wide', pairs)  20.4 us
    ppermute x24, waiting for transfers between devices, swap(): return lax.ppermute(block, 'narrow', [(n, n ^ bit) for n in range(size)])  15 us
    ppermute x24, starting transfers between devices, swap(): return lax.ppermute(block, 'narrow', [(n, n ^ bit) for n in range(size)])  10.5 us
  transfers between devices with their start and end apart: 46, of which 25 were waited for; matrix products, arithmetic and copies ran while one was open for 0% of the time, Pallas kernels for 17%

commit v1 on v0

--- a/solution.py
+++ b/solution.py
@@ -616,22 +616,26 @@
         [whole(payload_shape), whole((quarter, hidden_count))],
         6 * rows * hidden_count * action_count, 16 * MIB, [pltpu.VMEM(half, BF16)],
     )
-    taken = jnp.where(first, payload[rows : rows + quarter], swap(give, 1))
+    shards[0].append(ring.step(*shards[0][-1]))
+    given = swap(after(give, *shards[-1][-1]), 1)
+    taken = jnp.where(first, payload[rows : rows + quarter], given)
     payload = lax.dynamic_update_slice(payload, taken, (rows, 0))
 
     payload_rounds = [[payload, payload]]
+    payload_rounds.append(ring.step(*payload_rounds[-1]))
     for step in range(2, rounds - 1):
         for shard in shards:
-            if len(payload_rounds) < rounds:
-                payload_rounds.append(ring.step(*payload_rounds[-1]))
-            shard.append(ring.step(*shard[-1]))
-    while len(payload_rounds) < rounds:
-        payload_rounds.append(ring.step(*payload_rounds[-1]))
+            if len(shard) == step:
+                shard.append(ring.step(*shard[-1]))
+                if len(payload_rounds) < rounds - 1:
+                    payload_rounds.append(ring.step(*payload_rounds[-1]))
     cut = scenes // 2
     for one, other in zip(shards[:cut], shards[cut:]):
         up, down = ring.step(one[-1][0], other[-1][1])
         one.append([up])
         other.append([down])
+    while len(payload_rounds) < rounds:
+        payload_rounds.append(ring.step(*payload_rounds[-1]))
     size = hidden_count // 2
     up, down = payload_rounds[-1]
     payload_rounds.append(ring.step(up[:, :size], down[:, size:]))
@@ -640,37 +644,12 @@
         for way in range(len(shards[0][step])):
             turned_all += [shard[step][way] for shard in shards]
     payload_own = [payload, *(b for pair in payload_rounds[1:] for b in pair)]
-    payload_other = [swap(b, 1) for b in payload_own]
-
-    pieces = [*payload_own, *payload_other]
-    share_shape = (4 * quarter, action_count)
-    share, losses, value_out_grad = call(
-        functools.partial(sums, total_rows), "sums", place, 1, [*pieces, *pieces],
-        [
-            pl.BlockSpec((count, b.shape[1]), functools.partial(lambda at, i, p: (at, 0), start // count))
-            for start, count in ((rows, quarter), (rows + quarter, 16))
-            for b in pieces
-        ],
-        [
-            jax.ShapeDtypeStruct(share_shape, BF16),
-            jax.ShapeDtypeStruct((1, 2), F32),
-            jax.ShapeDtypeStruct((hidden_count,), BF16),
-        ],
-        [whole(share_shape), whole((1, 2)), whole((hidden_count,))], 0, 8 * MIB,
-    )
-    losses = losses.reshape(2)
-    shares = far_blocks(share)
-    policy_out_grad = call(
-        functools.partial(join, list(shares)), "join", place, 1, list(shares.values()),
-        [whole(share_shape)] * len(shares),
-        [jax.ShapeDtypeStruct((hidden_count, action_count), BF16)],
-        [whole((hidden_count, action_count))], 0, 8 * MIB,
-    )[0]
+    split = wide_size - 3
+    payload_other = [swap(b, 1) for b in payload_own[:split]]
 
     block = 256
     grad_spec = pl.BlockSpec((block, hidden_count), lambda i, p: (i, 0))
     grad_flops = 4 * rows * width * hidden_count
-    split = wide_size - 3
 
     def gradient(body, name, operands, specs, count, turned, own, other, dtype):
         return call(
@@ -694,6 +673,34 @@
         gradients_start, "gradients_start", [], [], split, turned_all[: scenes * split],
         payload_own[:split], payload_other[:split], F32,
     )
+    payload_other += [swap(b, 1) for b in payload_own[split:-2]]
+    payload_other += [swap(after(b, *starts), 1) for b in payload_own[-2:]]
+
+    pieces = [*payload_own, *payload_other]
+    share_shape = (4 * quarter, action_count)
+    share, losses, value_out_grad = call(
+        functools.partial(sums, total_rows), "sums", place, 1, [*pieces, *pieces],
+        [
+            pl.BlockSpec((count, b.shape[1]), functools.partial(lambda at, i, p: (at, 0), start // count))
+            for start, count in ((rows, quarter), (rows + quarter, 16))
+            for b in pieces
+        ],
+        [
+            jax.ShapeDtypeStruct(share_shape, BF16),
+            jax.ShapeDtypeStruct((1, 2), F32),
+            jax.ShapeDtypeStruct((hidden_count,), BF16),
+        ],
+        [whole(share_shape), whole((1, 2)), whole((hidden_count,))], 0, 8 * MIB,
+    )
+    losses = losses.reshape(2)
+    shares = far_blocks(share)
+    policy_out_grad = call(
+        functools.partial(join, list(shares)), "join", place, 1, list(shares.values()),
+        [whole(share_shape)] * len(shares),
+        [jax.ShapeDtypeStruct((hidden_count, action_count), BF16)],
+        [whole((hidden_count, action_count))], 0, 8 * MIB,
+    )[0]
+
     policy_in_grad, value_in_grad = gradient(
         gradients_end, "gradients_end", starts, [grad_spec] * 2, wide_size - split,
         turned_all[scenes * split :], payload_own[split:], payload_other[split:], BF16,

time: 124 us -> 125 us (level)
  starting transfers between devices: 30.8 us -> 32.3 us
    ppermute x22, starting transfers between devices: 20.4 us -> 22.4 us  [ring_step(): return lax.ppermute(block, 'wide', pairs)]
    ppermute x22, waiting for transfers between devices: 51.3 us -> 49.7 us  [ring_step(): return lax.ppermute(block, 'wide', pairs)]
where the time goes in v1:
time: 125 us
  waiting for transfers between devices  65.8 us (53%)
  starting transfers between devices  32.3 us (26%)
  Pallas kernels  26.2 us (21%)
    ppermute x22, waiting for transfers between devices, ring_step(): return lax.ppermute(block, 'wide', pairs)  49.7 us
    pallas_call x13, Pallas kernels, call(): pl.pallas_call(body, name=name, out_shape=outs, input_output_aliases=alia...  26.2 us
    ppermute x22, starting transfers between devices, ring_step(): return lax.ppermute(block, 'wide', pairs)  22.4 us
    ppermute x24, waiting for transfers between devices, swap(): return lax.ppermute(block, 'narrow', [(n, n ^ bit) for n in range(size)])  16 us
    ppermute x24, starting transfers between devices, swap(): return lax.ppermute(block, 'narrow', [(n, n ^ bit) for n in range(size)])  9.91 us
  transfers between devices with their start and end apart: 46, of which 25 were waited for; matrix products, arithmetic and copies ran while one was open for 0% of the time, Pallas kernels for 17%

profile of v1, /device:TPU:0, one launch (start us, length us, event | category | flops | bytes accessed | tf_op | source)
XLA Modules:
  0.0 125.3 jit_solution(12872308357380972527)
XLA Ops:
  0.6 1.7 %embed.1 = (f32[256,1024]{1,0:T(8,128)S(1)}, bf16[272,1024]{1,0:T(8,128)(2,1)S(1)}) custom-call(s32[1]{0:T(128)} %bitcast.p_ref, bf16[256,1024]{1,0:T(8,128)(2,1)} %latent_ref.1, s32[1,256]{1,0:T(1,128)} %bitcast.12, bf16[256,1024]{1,0:T(8,128)(2,1)} %table_ref.1, f32[1,1024]{1,0:T(1,128)} %bitcast.11), custom_call_target="tpu_custom_call" | custom-call | flops 134217728 | bytes 2659328 | tf_op jit(solution)/shard_map/embed/pallas_call | solution.py:394
  2.4 0.5 collective-permute-start
  2.9 2.6 %collective-permute-start.1 = (bf16[272,1024]{1,0:T(8,128)(2,1)S(1)}, bf16[272,1024]{1,0:T(8,128)(2,1)S(1)}, u32[]{:S(2)}, u32[]{:S(2)}) collective-permute-start(bf16[272,1024]{1,0:T(8,128)(2,1)S(1)} %get-tuple-element.62.refs_0_), channel_id=1, source_target_pairs={{0,2},{1,3},{2,0},{3,1},{4,6},{5,7},{6,4},{7,5},{8,10},{9,11},{10,... | collective-permute-start | bytes 1671176 | tf_op jit(solution)/shard_map/ppermute | solution.py:19
  5.5 5.3 %begin.1 = (f32[256,1536]{1,0:T(8,128)S(1)}, bf16[1024,512]{1,0:T(8,128)(2,1)S(1)}, bf16[1024,512]{1,0:T(8,128)(2,1)S(1)}, bf16[1024,512]{1,0:T(8,128)(2,1)S(1)}...) custom-call(s32[1]{0:T(128)} %bitcast.p_ref, ...), custom_call_target="tpu_custom_call" | custom-call | flops 1610612736 | bytes 25755648 | tf_op jit(solution)/shard_map/begin/pallas_call | solution.py:394
  10.8 7.9 %collective-permute-done.1.refs_0_.refs_1_ = bf16[272,1024]{1,0:T(8,128)(2,1)S(1)} collective-permute-done((bf16[272,1024]{1,0:T(8,128)(2,1)S(1)}, bf16[272,1024]{1,0:T(8,128)(2,1)S(1)}, u32[]{:S(2)}, u32[]{:S(2)}) %collective-permute-start.1) | collective-permute-done | bytes 557088 | tf_op jit(solution)/shard_map/ppermute | solution.py:19
  18.7 1.0 project.1.acc_ref
  19.7 1.0 collective-permute-done.2.refs_3_.refs_4_
  20.6 2.0 %attend0.1.refs_0_ = bf16[128,512]{1,0:T(8,128)(2,1)S(1)} custom-call(s32[1]{0:T(128)} %bitcast.p_ref, f32[256,1536]{1,0:T(8,128)S(1)} %project.1.acc_ref, bf16[2,512,512]{2,1,0:T(8,128)(2,1)S(1)} %get-tuple-element.67.keys_ref, bf16[2,512,512]{2,1,0:T(8,128)(2,1)S(1)} %get-tuple-element.68.values_ref, bf16[272,1024]{1,0:T(8,128)(2,1)S(1)} %get-tuple-element.62.refs_0_, ...), custom_call_target="tpu_custom_call" | custom-call | tf_op jit(solution)/shard_map/attend0/pallas_call | solution.py:394
  22.7 1.8 %collective-permute-start.6 = (bf16[128,512]{1,0:T(8,128)(2,1)S(1)}, bf16[128,512]{1,0:T(8,128)(2,1)S(1)}, u32[]{:S(2)}, u32[]{:S(2)}) collective-permute-start(bf16[128,512]{1,0:T(8,128)(2,1)S(1)} %attend0.1.refs_0_), channel_id=1, source_target_pairs={{0,2},{1,3},{2,0},{3,1},{4,6},{5,7},{6,4},{7,5},{8,10},{9,11},{10,... | collective-permute-start | bytes 393224 | tf_op jit(solution)/shard_map/ppermute | solution.py:19
  24.5 2.0 %attend1.1.refs_1_ = bf16[128,512]{1,0:T(8,128)(2,1)S(1)} custom-call(s32[1]{0:T(128)} %bitcast.p_ref, f32[256,1536]{1,0:T(8,128)S(1)} %project.1.acc_ref, bf16[2,512,512]{2,1,0:T(8,128)(2,1)S(1)} %get-tuple-element.67.keys_ref, bf16[2,512,512]{2,1,0:T(8,128)(2,1)S(1)} %get-tuple-element.68.values_ref, bf16[272,1024]{1,0:T(8,128)(2,1)S(1)} %get-tuple-element.62.refs_0_, ...), custom_call_target="tpu_custom_call" | custom-call | tf_op jit(solution)/shard_map/attend1/pallas_call | solution.py:394
  26.5 0.6 collective-permute-start.4
  27.1 1.2 collective-permute-done.6.refs_0_
  28.3 1.7 %collective-permute-start.5 = (bf16[128,512]{1,0:T(8,128)(2,1)S(1)}, bf16[128,512]{1,0:T(8,128)(2,1)S(1)}, u32[]{:S(2)}, u32[]{:S(2)}) collective-permute-start(bf16[128,512]{1,0:T(8,128)(2,1)S(1)} %attend1.1.refs_1_), channel_id=1, source_target_pairs={{0,2},{1,3},{2,0},{3,1},{4,6},{5,7},{6,4},{7,5},{8,10},{9,11},{10,... | collective-permute-start | bytes 393224 | tf_op jit(solution)/shard_map/ppermute | solution.py:19
  30.0 1.0 update_near.1.acc_ref
  31.0 1.8 %update0.1 = (bf16[256,1024]{1,0:T(8,128)(2,1)}, f32[256,512]{1,0:T(8,128)S(1)}, bf16[256,512]{1,0:T(8,128)(2,1)S(1)}, f32[8,256]{1,0:T(8,128)S(1)}, bf16[1024,128]{1,0:T(8,128)(2,1)S(1)}) custom-call(s32[1]{0:T(128)} %bitcast.p_ref, f32[256,1024]{1,0:T(8,128)S(1)} %update_near.1.acc_ref, f32[1,1024]{1,0:T(1,128)S(1)} %bitcast.7, ...), custom_call_target="tpu_custom_call" | custom-call | flops 536870912 | bytes 9187328 | tf_op jit(solution)/shard_map/update0/pallas_call | solution.py:394
  32.8 1.6 %collective-permute-start.9 = (bf16[1024,128]{1,0:T(8,128)(2,1)S(1)}, bf16[1024,128]{1,0:T(8,128)(2,1)S(1)}, u32[]{:S(2)}, u32[]{:S(2)}) collective-permute-start(bf16[1024,128]{1,0:T(8,128)(2,1)S(1)} %get-tuple-element.73.refs_0_), channel_id=1, source_target_pairs={{0,8},{8,16},{16,24},{24,28},{28,20},{20,12},{12,4},{4,0},{1,9},{9... | collective-permute-start | bytes 786440 | tf_op jit(solution)/shard_map/ppermute | solution.py:52
  34.4 0.5 collective-permute-start.10
  34.8 1.3 %collective-permute-done.8.refs_1_ = bf16[128,512]{1,0:T(8,128)(2,1)S(1)} collective-permute-done((bf16[128,512]{1,0:T(8,128)(2,1)S(1)}, bf16[128,512]{1,0:T(8,128)(2,1)S(1)}, u32[]{:S(2)}, u32[]{:S(2)}) %collective-permute-start.8) | collective-permute-done | bytes 131104 | tf_op jit(solution)/shard_map/ppermute | solution.py:19
  36.2 1.8 %update1.1 = (bf16[256,1024]{1,0:T(8,128)(2,1)}, f32[256,512]{1,0:T(8,128)S(1)}, bf16[256,512]{1,0:T(8,128)(2,1)S(1)}, f32[8,256]{1,0:T(8,128)S(1)}, bf16[1024,128]{1,0:T(8,128)(2,1)S(1)}) custom-call(s32[1]{0:T(128)} %bitcast.p_ref, f32[256,1024]{1,0:T(8,128)S(1)} %update_near.1.acc_ref, ...), custom_call_target="tpu_custom_call", output_to_operand_aliasing={{0}: (8, {}), {1}: (9, {}), {2}: (10, {}), {3}: (11, {})} | custom-call | flops 536870912 | bytes 10506240 | tf_op jit(solution)/shard_map/update1/pallas_call | solution.py:394
  38.0 3.3 %collective-permute-done.9.refs_2_ = bf16[1024,128]{1,0:T(8,128)(2,1)S(1)} collective-permute-done((bf16[1024,128]{1,0:T(8,128)(2,1)S(1)}, bf16[1024,128]{1,0:T(8,128)(2,1)S(1)}, u32[]{:S(2)}, u32[]{:S(2)}) %collective-permute-start.9) | collective-permute-done | bytes 262176 | tf_op jit(solution)/shard_map/ppermute | solution.py:52
  41.3 1.3 %collective-permute-done.10.refs_4_ = bf16[1024,128]{1,0:T(8,128)(2,1)S(1)} collective-permute-done((bf16[1024,128]{1,0:T(8,128)(2,1)S(1)}, bf16[1024,128]{1,0:T(8,128)(2,1)S(1)}, u32[]{:S(2)}, u32[]{:S(2)}) %collective-permute-start.10) | collective-permute-done | bytes 262176 | tf_op jit(solution)/shard_map/ppermute | solution.py:52
  42.6 1.6 %collective-permute-start.15 = (bf16[1024,128]{1,0:T(8,128)(2,1)S(1)}, bf16[1024,128]{1,0:T(8,128)(2,1)S(1)}, u32[]{:S(2)}, u32[]{:S(2)}) collective-permute-start(bf16[1024,128]{1,0:T(8,128)(2,1)S(1)} %get-tuple-element.85.refs_1_), channel_id=1, source_target_pairs={{0,8},{8,16},{16,24},{24,28},{28,20},{20,12},{12,4},{4,0},{1,9},{9... | collective-permute-start | bytes 786440 | tf_op jit(solution)/shard_map/ppermute | solution.py:52
  44.1 0.4 collective-permute-start.16
  44.6 1.6 %collective-permute-start.13 = (bf16[1024,128]{1,0:T(8,128)(2,1)S(1)}, bf16[1024,128]{1,0:T(8,128)(2,1)S(1)}, u32[]{:S(2)}, u32[]{:S(2)}) collective-permute-start(bf16[1024,128]{1,0:T(8,128)(2,1)S(1)} %collective-permute-done.9.refs_2_), channel_id=1, source_target_pairs={{0,8},{8,16},{16,24},{24,28},{28,20},{20,12},{12,4},{4,0},{1,9},{9... | collective-permute-start | bytes 786440 | tf_op jit(solution)/shard_map/ppermute | solution.py:52
  46.2 0.4 collective-permute-start.14
  46.7 0.6 collective-permute-start.12
  47.3 4.4 %collective-permute-done.15.refs_3_ = bf16[1024,128]{1,0:T(8,128)(2,1)S(1)} collective-permute-done((bf16[1024,128]{1,0:T(8,128)(2,1)S(1)}, bf16[1024,128]{1,0:T(8,128)(2,1)S(1)}, u32[]{:S(2)}, u32[]{:S(2)}) %collective-permute-start.15) | collective-permute-done | bytes 262176 | tf_op jit(solution)/shard_map/ppermute | solution.py:52
  51.7 0.5 collective-permute-start.18
  52.2 1.1 collective-permute-done.16.refs_5_
  53.3 1.6 %collective-permute-start.19 = (bf16[1024,128]{1,0:T(8,128)(2,1)S(1)}, bf16[1024,128]{1,0:T(8,128)(2,1)S(1)}, u32[]{:S(2)}, u32[]{:S(2)}) collective-permute-start(bf16[1024,128]{1,0:T(8,128)(2,1)S(1)} %collective-permute-done.15.refs_3_), channel_id=1, source_target_pairs={{0,8},{8,16},{16,24},{24,28},{28,20},{20,12},{12,4},{4,0},{1,9},{9... | collective-permute-start | bytes 786440 | tf_op jit(solution)/shard_map/ppermute | solution.py:52
  54.9 0.5 collective-permute-done.18
  55.3 0.5 collective-permute-start.20
  55.8 1.5 %collective-permute-done.13.refs_6_ = bf16[1024,128]{1,0:T(8,128)(2,1)S(1)} collective-permute-done((bf16[1024,128]{1,0:T(8,128)(2,1)S(1)}, bf16[1024,128]{1,0:T(8,128)(2,1)S(1)}, u32[]{:S(2)}, u32[]{:S(2)}) %collective-permute-start.13) | collective-permute-done | bytes 262176 | tf_op jit(solution)/shard_map/ppermute | solution.py:52
  57.3 1.6 %collective-permute-done.14.refs_8_ = bf16[1024,128]{1,0:T(8,128)(2,1)S(1)} collective-permute-done((bf16[1024,128]{1,0:T(8,128)(2,1)S(1)}, bf16[1024,128]{1,0:T(8,128)(2,1)S(1)}, u32[]{:S(2)}, u32[]{:S(2)}) %collective-permute-start.14) | collective-permute-done | bytes 262176 | tf_op jit(solution)/shard_map/ppermute | solution.py:52
  58.9 1.1 heads.1
  60.1 2.5 %collective-permute-done.19.refs_7_ = bf16[1024,128]{1,0:T(8,128)(2,1)S(1)} collective-permute-done((bf16[1024,128]{1,0:T(8,128)(2,1)S(1)}, bf16[1024,128]{1,0:T(8,128)(2,1)S(1)}, u32[]{:S(2)}, u32[]{:S(2)}) %collective-permute-start.19) | collective-permute-done | bytes 262176 | tf_op jit(solution)/shard_map/ppermute | solution.py:52
  62.5 1.3 %collective-permute-done.20.refs_9_ = bf16[1024,128]{1,0:T(8,128)(2,1)S(1)} collective-permute-done((bf16[1024,128]{1,0:T(8,128)(2,1)S(1)}, bf16[1024,128]{1,0:T(8,128)(2,1)S(1)}, u32[]{:S(2)}, u32[]{:S(2)}) %collective-permute-start.20) | collective-permute-done | bytes 262176 | tf_op jit(solution)/shard_map/ppermute | solution.py:52
  63.8 1.3 collective-permute-done.21
  65.1 1.6 %collective-permute-start.22 = (bf16[336,512]{1,0:T(8,128)(2,1)S(1)}, bf16[336,512]{1,0:T(8,128)(2,1)S(1)}, u32[]{:S(2)}, u32[]{:S(2)}) collective-permute-start(bf16[336,512]{1,0:T(8,128)(2,1)S(1)} %select_dynamic-update-slice_fusion.refs_10_.refs_0_.refs_18_), channel_id=1, source_target_pairs={{0,8},{8,16},{16,24},{24,28},{28,20},{20,12},{12,4},{4,0},{1,9},{9... | collective-permute-start | bytes 1032200 | tf_op jit(solution)/shard_map/ppermute | solution.py:52
  67.2 1.6 %collective-permute-start.28 = (bf16[1024,128]{1,0:T(8,128)(2,1)S(1)}, bf16[1024,128]{1,0:T(8,128)(2,1)S(1)}, u32[]{:S(2)}, u32[]{:S(2)}) collective-permute-start(bf16[1024,128]{1,0:T(8,128)(2,1)S(1)} %collective-permute-done.13.refs_6_), channel_id=1, source_target_pairs={{0,8},{8,16},{16,24},{24,28},{28,20},{20,12},{12,4},{4,0},{1,9},{9... | collective-permute-start | bytes 786440 | tf_op jit(solution)/shard_map/ppermute | solution.py:52
  69.2 6.9 %collective-permute-done.22.refs_11_.refs_1_.refs_19_ = bf16[336,512]{1,0:T(8,128)(2,1)S(1)} collective-permute-done((bf16[336,512]{1,0:T(8,128)(2,1)S(1)}, bf16[336,512]{1,0:T(8,128)(2,1)S(1)}, u32[]{:S(2)}, u32[]{:S(2)}) %collective-permute-start.22) | collective-permute-done | bytes 344096 | tf_op jit(solution)/shard_map/ppermute | solution.py:52
  76.1 1.6 %collective-permute-start.24 = (bf16[336,512]{1,0:T(8,128)(2,1)S(1)}, bf16[336,512]{1,0:T(8,128)(2,1)S(1)}, u32[]{:S(2)}, u32[]{:S(2)}) collective-permute-start(bf16[336,512]{1,0:T(8,128)(2,1)S(1)} %collective-permute-done.22.refs_11_.refs_1_.refs_19_), channel_id=1, source_target_pairs={{0,8},{8,16},{16,24},{24,28},{28,20},{20,12},{12,4},{4,0},{1,9},{9... | collective-permute-start | bytes 1032200 | tf_op jit(solution)/shard_map/ppermute | solution.py:52
  78.1 3.6 %collective-permute-done.28.refs_2_ = bf16[1024,128]{1,0:T(8,128)(2,1)S(1)} collective-permute-done((bf16[1024,128]{1,0:T(8,128)(2,1)S(1)}, bf16[1024,128]{1,0:T(8,128)(2,1)S(1)}, u32[]{:S(2)}, u32[]{:S(2)}) %collective-permute-start.28) | collective-permute-done | bytes 262176 | tf_op jit(solution)/shard_map/ppermute | solution.py:52
  81.7 1.6 %collective-permute-start.29 = (bf16[1024,128]{1,0:T(8,128)(2,1)S(1)}, bf16[1024,128]{1,0:T(8,128)(2,1)S(1)}, u32[]{:S(2)}, u32[]{:S(2)}) collective-permute-start(bf16[1024,128]{1,0:T(8,128)(2,1)S(1)} %collective-permute-done.19.refs_7_), channel_id=1, source_target_pairs={{0,8},{8,16},{16,24},{24,28},{28,20},{20,12},{12,4},{4,0},{1,9},{9... | collective-permute-start | bytes 786440 | tf_op jit(solution)/shard_map/ppermute | solution.py:52
  83.3 0.4 collective-permute-start.33
  83.7 5.3 %collective-permute-done.24.refs_13_.refs_3_.refs_21_ = bf16[336,512]{1,0:T(8,128)(2,1)S(1)} collective-permute-done((bf16[336,512]{1,0:T(8,128)(2,1)S(1)}, bf16[336,512]{1,0:T(8,128)(2,1)S(1)}, u32[]{:S(2)}, u32[]{:S(2)}) %collective-permute-start.24) | collective-permute-done | bytes 344096 | tf_op jit(solution)/shard_map/ppermute | solution.py:52
  89.0 1.6 %collective-permute-start.26 = (bf16[336,512]{1,0:T(8,128)(2,1)S(1)}, bf16[336,512]{1,0:T(8,128)(2,1)S(1)}, u32[]{:S(2)}, u32[]{:S(2)}) collective-permute-start(bf16[336,512]{1,0:T(8,128)(2,1)S(1)} %collective-permute-done.24.refs_13_.refs_3_.refs_21_), channel_id=1, source_target_pairs={{0,8},{8,16},{16,24},{24,28},{28,20},{20,12},{12,4},{4,0},{1,9},{9... | collective-permute-start | bytes 1032200 | tf_op jit(solution)/shard_map/ppermute | solution.py:52
  91.1 3.6 %collective-permute-done.29.refs_3_ = bf16[1024,128]{1,0:T(8,128)(2,1)S(1)} collective-permute-done((bf16[1024,128]{1,0:T(8,128)(2,1)S(1)}, bf16[1024,128]{1,0:T(8,128)(2,1)S(1)}, u32[]{:S(2)}, u32[]{:S(2)}) %collective-permute-start.29) | collective-permute-done | bytes 262176 | tf_op jit(solution)/shard_map/ppermute | solution.py:52
  94.7 1.6 %collective-permute-start.30 = (bf16[1024,128]{1,0:T(8,128)(2,1)S(1)}, bf16[1024,128]{1,0:T(8,128)(2,1)S(1)}, u32[]{:S(2)}, u32[]{:S(2)}) collective-permute-start(bf16[1024,128]{1,0:T(8,128)(2,1)S(1)} %collective-permute-done.28.refs_2_), channel_id=1, source_target_pairs={{0,8},{8,16},{16,24},{24,28},{28,20},{20,12},{12,4},{4,0},{1,9},{9... | collective-permute-start | bytes 786440 | tf_op jit(solution)/shard_map/ppermute | solution.py:52
  96.7 10.1 %collective-permute-done.30.refs_6_ = bf16[1024,128]{1,0:T(8,128)(2,1)S(1)} collective-permute-done((bf16[1024,128]{1,0:T(8,128)(2,1)S(1)}, bf16[1024,128]{1,0:T(8,128)(2,1)S(1)}, u32[]{:S(2)}, u32[]{:S(2)}) %collective-permute-start.30) | collective-permute-done | bytes 262176 | tf_op jit(solution)/shard_map/ppermute | solution.py:52
  106.9 1.3 %collective-permute-done.34.refs_7_ = bf16[1024,128]{1,0:T(8,128)(2,1)S(1)} collective-permute-done((bf16[1024,128]{1,0:T(8,128)(2,1)S(1)}, bf16[1024,128]{1,0:T(8,128)(2,1)S(1)}, u32[]{:S(2)}, u32[]{:S(2)}) %collective-permute-start.34) | collective-permute-done | bytes 262176 | tf_op jit(solution)/shard_map/ppermute | solution.py:52
  108.2 0.5 collective-permute-start.39
  108.8 1.5 %collective-permute-start.31 = (bf16[336,256]{1,0:T(8,128)(2,1)S(1)}, bf16[336,256]{1,0:T(8,128)(2,1)S(1)}, u32[]{:S(2)}, u32[]{:S(2)}) collective-permute-start(bf16[336,256]{1,0:T(8,128)(2,1)S(1)} %slice.12), channel_id=1, source_target_pairs={{0,8},{8,16},{16,24},{24,28},{28,20},{20,12},{12,4},{4,0},{1,9},{9... | collective-permute-start | bytes 516104 | tf_op jit(solution)/shard_map/ppermute | solution.py:52
  110.4 0.5 collective-permute-start.35
  110.9 0.5 collective-permute-start.42
  111.4 3.5 %gradients_start.1 = (f32[1024,512]{1,0:T(8,128)S(1)}, f32[1024,512]{1,0:T(8,128)S(1)}) custom-call(s32[1]{0:T(128)} %bitcast.p_ref, bf16[1024,128]{1,0:T(8,128)(2,1)S(1)} %get-tuple-element.73.refs_0_, bf16[1024,128]{1,0:T(8,128)(2,1)S(1)} %get-tuple-element.85.refs_1_, bf16[1024,128]{1,0:T(8,128)(2,1)S(1)} %collective-permute-done.9.refs_2_, ...), custom_call_target="tpu_custom_call" | custom-call | flops 2684354560 | bytes 10256384 | tf_op jit(solution)/shard_map/gradients_start/pallas_call | solution.py:394
  114.9 0.7 collective-permute-done.31.refs_7_.refs_25_.refs_10_
  115.6 1.2 collective-permute-done.35.refs_8_.refs_26_.refs_11_
  117.0 1.2 collective-permute-done.44.refs_17_.refs_35_.refs_15_
  118.2 0.8 sums.1
  119.0 0.5 collective-permute-start.45
  119.5 3.5 %gradients_end.1 = (bf16[1024,512]{1,0:T(8,128)(2,1)}, bf16[1024,512]{1,0:T(8,128)(2,1)}) custom-call(s32[1]{0:T(128)} %bitcast.p_ref, f32[1024,512]{1,0:T(8,128)S(1)} %get-tuple-element.107.refs_0_, f32[1024,512]{1,0:T(8,128)S(1)} %get-tuple-element.108.refs_1_, bf16[1024,128]{1,0:T(8,128)(2,1)S(1)} %collective-permute-done.28.refs_2_, ...), custom_call_target="tpu_custom_call" | custom-call | flops 1610612736 | bytes 9928704 | tf_op jit(solution)/shard_map/gradients_end/pallas_call | solution.py:394
  123.0 1.5 %collective-permute-done.45.refs_1_ = bf16[256,256]{1,0:T(8,128)(2,1)S(1)} collective-permute-done((bf16[256,256]{1,0:T(8,128)(2,1)S(1)}, bf16[256,256]{1,0:T(8,128)(2,1)S(1)}, u32[]{:S(2)}, u32[]{:S(2)}) %collective-permute-start.45) | collective-permute-done | bytes 131104 | tf_op jit(solution)/shard_map/ppermute | solution.py:19
  124.5 0.7 join.1
  (64 shorter events, 2.9 us)
Async XLA Ops:
  2.4 3.1 %collective-permute-start = (bf16[272,1024]{1,0:T(8,128)(2,1)S(1)}, bf16[272,1024]{1,0:T(8,128)(2,1)S(1)}, u32[]{:S(2)}, u32[]{:S(2)}) collective-permute-start(bf16[272,1024]{1,0:T(8,128)(2,1)S(1)} %get-tuple-element.62.refs_0_), channel_id=1, source_target_pairs={{0,1},{1,0},{2,3},{3,2},{4,5},{5,4},{6,7},{7,6},{8,9},{9,8},{10,11... | collective-permute-start | bytes 1671176 | tf_op jit(solution)/shard_map/ppermute | solution.py:19
  2.9 15.8 %collective-permute-start.1 = (bf16[272,1024]{1,0:T(8,128)(2,1)S(1)}, bf16[272,1024]{1,0:T(8,128)(2,1)S(1)}, u32[]{:S(2)}, u32[]{:S(2)}) collective-permute-start(bf16[272,1024]{1,0:T(8,128)(2,1)S(1)} %get-tuple-element.62.refs_0_), channel_id=1, source_target_pairs={{0,2},{1,3},{2,0},{3,1},{4,6},{5,7},{6,4},{7,5},{8,10},{9,11},{10,... | collective-permute-start | bytes 1671176 | tf_op jit(solution)/shard_map/ppermute | solution.py:19
  18.7 2.0 %collective-permute-start.2 = (bf16[272,1024]{1,0:T(8,128)(2,1)S(1)}, bf16[272,1024]{1,0:T(8,128)(2,1)S(1)}, u32[]{:S(2)}, u32[]{:S(2)}) collective-permute-start(bf16[272,1024]{1,0:T(8,128)(2,1)S(1)} %collective-permute-done.1.refs_0_.refs_1_), channel_id=1, source_target_pairs={{0,1},{1,0},{2,3},{3,2},{4,5},{5,4},{6,7},{7,6},{8,9},{9,8},{10,11... | collective-permute-start | bytes 1671176 | tf_op jit(solution)/shard_map/ppermute | solution.py:19
  22.7 7.4 %copy-start = (bf16[2048,1024]{1,0:T(8,128)(2,1)S(1)}, bf16[2048,1024]{1,0:T(8,128)(2,1)}, u32[]{:S(2)}) copy-start(bf16[2048,1024]{1,0:T(8,128)(2,1)} %refs_2_.5) | copy-start | bytes 12582916
  22.7 5.6 %collective-permute-start.6 = (bf16[128,512]{1,0:T(8,128)(2,1)S(1)}, bf16[128,512]{1,0:T(8,128)(2,1)S(1)}, u32[]{:S(2)}, u32[]{:S(2)}) collective-permute-start(bf16[128,512]{1,0:T(8,128)(2,1)S(1)} %attend0.1.refs_0_), channel_id=1, source_target_pairs={{0,2},{1,3},{2,0},{3,1},{4,6},{5,7},{6,4},{7,5},{8,10},{9,11},{10,... | collective-permute-start | bytes 393224 | tf_op jit(solution)/shard_map/ppermute | solution.py:19
  24.5 5.5 %collective-permute-start.3 = (bf16[128,512]{1,0:T(8,128)(2,1)S(1)}, bf16[128,512]{1,0:T(8,128)(2,1)S(1)}, u32[]{:S(2)}, u32[]{:S(2)}) collective-permute-start(bf16[128,512]{1,0:T(8,128)(2,1)S(1)} %attend0.1.refs_0_), channel_id=1, source_target_pairs={{0,1},{1,0},{2,3},{3,2},{4,5},{5,4},{6,7},{7,6},{8,9},{9,8},{10,11... | collective-permute-start | bytes 393224 | tf_op jit(solution)/shard_map/ppermute | solution.py:19
  26.5 4.5 %copy-start.1 = (bf16[1024,512]{1,0:T(8,128)(2,1)S(1)}, bf16[1024,512]{1,0:T(8,128)(2,1)}, u32[]{:S(2)}) copy-start(bf16[1024,512]{1,0:T(8,128)(2,1)} %policy_ref.3) | copy-start | bytes 3145732
  26.5 4.5 %copy-start.2 = (bf16[1024,512]{1,0:T(8,128)(2,1)S(1)}, bf16[1024,512]{1,0:T(8,128)(2,1)}, u32[]{:S(2)}) copy-start(bf16[1024,512]{1,0:T(8,128)(2,1)} %value_ref.3) | copy-start | bytes 3145732
  26.5 4.5 %copy-start.4 = (f32[1024]{0:T(1024)S(1)}, f32[1024]{0:T(1024)}, u32[]{:S(2)}) copy-start(f32[1024]{0:T(1024)} %param.27) | copy-start | bytes 12292
  26.5 3.5 %collective-permute-start.4 = (bf16[128,512]{1,0:T(8,128)(2,1)S(1)}, bf16[128,512]{1,0:T(8,128)(2,1)S(1)}, u32[]{:S(2)}, u32[]{:S(2)}) collective-permute-start(bf16[128,512]{1,0:T(8,128)(2,1)S(1)} %attend1.1.refs_1_), channel_id=1, source_target_pairs={{0,1},{1,0},{2,3},{3,2},{4,5},{5,4},{6,7},{7,6},{8,9},{9,8},{10,11... | collective-permute-start | bytes 393224 | tf_op jit(solution)/shard_map/ppermute | solution.py:19
  28.3 2.7 %collective-permute-start.7 = (bf16[128,512]{1,0:T(8,128)(2,1)S(1)}, bf16[128,512]{1,0:T(8,128)(2,1)S(1)}, u32[]{:S(2)}, u32[]{:S(2)}) collective-permute-start(bf16[128,512]{1,0:T(8,128)(2,1)S(1)} %collective-permute-done.6.refs_0_), channel_id=1, source_target_pairs={{0,1},{1,0},{2,3},{3,2},{4,5},{5,4},{6,7},{7,6},{8,9},{9,8},{10,11... | collective-permute-start | bytes 393224 | tf_op jit(solution)/shard_map/ppermute | solution.py:19
  28.3 6.6 %collective-permute-start.5 = (bf16[128,512]{1,0:T(8,128)(2,1)S(1)}, bf16[128,512]{1,0:T(8,128)(2,1)S(1)}, u32[]{:S(2)}, u32[]{:S(2)}) collective-permute-start(bf16[128,512]{1,0:T(8,128)(2,1)S(1)} %attend1.1.refs_1_), channel_id=1, source_target_pairs={{0,2},{1,3},{2,0},{3,1},{4,6},{5,7},{6,4},{7,5},{8,10},{9,11},{10,... | collective-permute-start | bytes 393224 | tf_op jit(solution)/shard_map/ppermute | solution.py:19
  32.8 8.5 %collective-permute-start.9 = (bf16[1024,128]{1,0:T(8,128)(2,1)S(1)}, bf16[1024,128]{1,0:T(8,128)(2,1)S(1)}, u32[]{:S(2)}, u32[]{:S(2)}) collective-permute-start(bf16[1024,128]{1,0:T(8,128)(2,1)S(1)} %get-tuple-element.73.refs_0_), channel_id=1, source_target_pairs={{0,8},{8,16},{16,24},{24,28},{28,20},{20,12},{12,4},{4,0},{1,9},{9... | collective-permute-start | bytes 786440 | tf_op jit(solution)/shard_map/ppermute | solution.py:52
  34.4 8.2 %collective-permute-start.10 = (bf16[1024,128]{1,0:T(8,128)(2,1)S(1)}, bf16[1024,128]{1,0:T(8,128)(2,1)S(1)}, u32[]{:S(2)}, u32[]{:S(2)}) collective-permute-start(bf16[1024,128]{1,0:T(8,128)(2,1)S(1)} %get-tuple-element.73.refs_0_), channel_id=1, source_target_pairs={{0,4},{8,0},{16,8},{24,16},{28,24},{20,28},{12,20},{4,12},{1,5},{9... | collective-permute-start | bytes 786440 | tf_op jit(solution)/shard_map/ppermute | solution.py:52
  34.8 1.3 %collective-permute-start.8 = (bf16[128,512]{1,0:T(8,128)(2,1)S(1)}, bf16[128,512]{1,0:T(8,128)(2,1)S(1)}, u32[]{:S(2)}, u32[]{:S(2)}) collective-permute-start(bf16[128,512]{1,0:T(8,128)(2,1)S(1)} %collective-permute-done.5.refs_0_), channel_id=1, source_target_pairs={{0,1},{1,0},{2,3},{3,2},{4,5},{5,4},{6,7},{7,6},{8,9},{9,8},{10,11... | collective-permute-start | bytes 393224 | tf_op jit(solution)/shard_map/ppermute | solution.py:19
  36.2 19.6 %copy-start.7 = (bf16[512]{0:T(512)(128)(2,1)S(1)}, bf16[512]{0:T(512)(128)(2,1)}, u32[]{:S(2)}) copy-start(bf16[512]{0:T(512)(128)(2,1)} %param.31) | copy-start | bytes 3076
  36.2 22.7 %copy-start.3 = (bf16[512,256]{1,0:T(8,128)(2,1)S(1)}, bf16[512,256]{1,0:T(8,128)(2,1)}, u32[]{:S(2)}) copy-start(bf16[512,256]{1,0:T(8,128)(2,1)} %policy_out_ref.1) | copy-start | bytes 786436
  36.2 22.7 %copy-start.5 = (s32[256]{0:T(256)S(1)}, s32[256]{0:T(256)}, u32[]{:S(2)}) copy-start(s32[256]{0:T(256)} %param.32) | copy-start | bytes 3076
  36.2 22.7 %copy-start.6 = (f32[256]{0:T(256)S(1)}, f32[256]{0:T(256)}, u32[]{:S(2)}) copy-start(f32[256]{0:T(256)} %param.33) | copy-start | bytes 3076
  42.6 3.6 %collective-permute-start.11 = (bf16[256,512]{1,0:T(8,128)(2,1)S(1)}, bf16[256,512]{1,0:T(8,128)(2,1)S(1)}, u32[]{:S(2)}, u32[]{:S(2)}) collective-permute-start(bf16[256,512]{1,0:T(8,128)(2,1)S(1)} %get-tuple-element.82), channel_id=1, source_target_pairs={{0,1},{1,0},{2,3},{3,2},{4,5},{5,4},{6,7},{7,6},{8,9},{9,8},{10,11... | collective-permute-start | bytes 786440 | tf_op jit(solution)/shard_map/ppermute | solution.py:19
  42.6 9.1 %collective-permute-start.15 = (bf16[1024,128]{1,0:T(8,128)(2,1)S(1)}, bf16[1024,128]{1,0:T(8,128)(2,1)S(1)}, u32[]{:S(2)}, u32[]{:S(2)}) collective-permute-start(bf16[1024,128]{1,0:T(8,128)(2,1)S(1)} %get-tuple-element.85.refs_1_), channel_id=1, source_target_pairs={{0,8},{8,16},{16,24},{24,28},{28,20},{20,12},{12,4},{4,0},{1,9},{9... | collective-permute-start | bytes 786440 | tf_op jit(solution)/shard_map/ppermute | solution.py:52
  44.1 9.1 %collective-permute-start.16 = (bf16[1024,128]{1,0:T(8,128)(2,1)S(1)}, bf16[1024,128]{1,0:T(8,128)(2,1)S(1)}, u32[]{:S(2)}, u32[]{:S(2)}) collective-permute-start(bf16[1024,128]{1,0:T(8,128)(2,1)S(1)} %get-tuple-element.85.refs_1_), channel_id=1, source_target_pairs={{0,4},{8,0},{16,8},{24,16},{28,24},{20,28},{12,20},{4,12},{1,5},{9... | collective-permute-start | bytes 786440 | tf_op jit(solution)/shard_map/ppermute | solution.py:52
  44.6 2.1 %collective-permute-start.17 = (f32[8,256]{1,0:T(8,128)S(1)}, f32[8,256]{1,0:T(8,128)S(1)}, u32[]{:S(2)}, u32[]{:S(2)}) collective-permute-start(f32[8,256]{1,0:T(8,128)S(1)} %get-tuple-element.87), channel_id=1, source_target_pairs={{0,1},{1,0},{2,3},{3,2},{4,5},{5,4},{6,7},{7,6},{8,9},{9,8},{10,11... | collective-permute-start | bytes 24584 | tf_op jit(solution)/shard_map/ppermute | solution.py:19
  44.6 12.7 %collective-permute-start.13 = (bf16[1024,128]{1,0:T(8,128)(2,1)S(1)}, bf16[1024,128]{1,0:T(8,128)(2,1)S(1)}, u32[]{:S(2)}, u32[]{:S(2)}) collective-permute-start(bf16[1024,128]{1,0:T(8,128)(2,1)S(1)} %collective-permute-done.9.refs_2_), channel_id=1, source_target_pairs={{0,8},{8,16},{16,24},{24,28},{28,20},{20,12},{12,4},{4,0},{1,9},{9... | collective-permute-start | bytes 786440 | tf_op jit(solution)/shard_map/ppermute | solution.py:52
  46.2 12.7 %collective-permute-start.14 = (bf16[1024,128]{1,0:T(8,128)(2,1)S(1)}, bf16[1024,128]{1,0:T(8,128)(2,1)S(1)}, u32[]{:S(2)}, u32[]{:S(2)}) collective-permute-start(bf16[1024,128]{1,0:T(8,128)(2,1)S(1)} %collective-permute-done.10.refs_4_), channel_id=1, source_target_pairs={{0,4},{8,0},{16,8},{24,16},{28,24},{20,28},{12,20},{4,12},{1,5},{9... | collective-permute-start | bytes 786440 | tf_op jit(solution)/shard_map/ppermute | solution.py:52
  46.7 12.2 %collective-permute-start.12 = (bf16[256,512]{1,0:T(8,128)(2,1)S(1)}, bf16[256,512]{1,0:T(8,128)(2,1)S(1)}, u32[]{:S(2)}, u32[]{:S(2)}) collective-permute-start(bf16[256,512]{1,0:T(8,128)(2,1)S(1)} %add_convert_fusion.mine_ref), channel_id=1, source_target_pairs={{0,2},{1,3},{2,0},{3,1},{4,6},{5,7},{6,4},{7,5},{8,10},{9,11},{10,... | collective-permute-start | bytes 786440 | tf_op jit(solution)/shard_map/ppermute | solution.py:19
  51.7 3.7 %collective-permute-start.18 = (f32[8,256]{1,0:T(8,128)S(1)}, f32[8,256]{1,0:T(8,128)S(1)}, u32[]{:S(2)}, u32[]{:S(2)}) collective-permute-start(f32[8,256]{1,0:T(8,128)S(1)} %add.14), channel_id=1, source_target_pairs={{0,2},{1,3},{2,0},{3,1},{4,6},{5,7},{6,4},{7,5},{8,10},{9,11},{10,... | collective-permute-start | bytes 24584 | tf_op jit(solution)/shard_map/ppermute | solution.py:19
  53.3 9.2 %collective-permute-start.19 = (bf16[1024,128]{1,0:T(8,128)(2,1)S(1)}, bf16[1024,128]{1,0:T(8,128)(2,1)S(1)}, u32[]{:S(2)}, u32[]{:S(2)}) collective-permute-start(bf16[1024,128]{1,0:T(8,128)(2,1)S(1)} %collective-permute-done.15.refs_3_), channel_id=1, source_target_pairs={{0,8},{8,16},{16,24},{24,28},{28,20},{20,12},{12,4},{4,0},{1,9},{9... | collective-permute-start | bytes 786440 | tf_op jit(solution)/shard_map/ppermute | solution.py:52
  55.3 8.5 %collective-permute-start.20 = (bf16[1024,128]{1,0:T(8,128)(2,1)S(1)}, bf16[1024,128]{1,0:T(8,128)(2,1)S(1)}, u32[]{:S(2)}, u32[]{:S(2)}) collective-permute-start(bf16[1024,128]{1,0:T(8,128)(2,1)S(1)} %collective-permute-done.16.refs_5_), channel_id=1, source_target_pairs={{0,4},{8,0},{16,8},{24,16},{28,24},{20,28},{12,20},{4,12},{1,5},{9... | collective-permute-start | bytes 786440 | tf_op jit(solution)/shard_map/ppermute | solution.py:52
  63.8 1.3 %collective-permute-start.21 = (bf16[64,512]{1,0:T(8,128)(2,1)S(1)}, bf16[64,512]{1,0:T(8,128)(2,1)S(1)}, u32[]{:S(2)}, u32[]{:S(2)}) collective-permute-start(bf16[64,512]{1,0:T(8,128)(2,1)S(1)} %get-tuple-element.92), channel_id=1, source_target_pairs={{0,1},{1,0},{2,3},{3,2},{4,5},{5,4},{6,7},{7,6},{8,9},{9,8},{10,11... | collective-permute-start | bytes 196616 | tf_op jit(solution)/shard_map/ppermute | solution.py:19
  65.1 11.0 %collective-permute-start.22 = (bf16[336,512]{1,0:T(8,128)(2,1)S(1)}, bf16[336,512]{1,0:T(8,128)(2,1)S(1)}, u32[]{:S(2)}, u32[]{:S(2)}) collective-permute-start(bf16[336,512]{1,0:T(8,128)(2,1)S(1)} %select_dynamic-update-slice_fusion.refs_10_.refs_0_.refs_18_), channel_id=1, source_target_pairs={{0,8},{8,16},{16,24},{24,28},{28,20},{20,12},{12,4},{4,0},{1,9},{9... | collective-permute-start | bytes 1032200 | tf_op jit(solution)/shard_map/ppermute | solution.py:52
  66.7 10.9 %collective-permute-start.23 = (bf16[336,512]{1,0:T(8,128)(2,1)S(1)}, bf16[336,512]{1,0:T(8,128)(2,1)S(1)}, u32[]{:S(2)}, u32[]{:S(2)}) collective-permute-start(bf16[336,512]{1,0:T(8,128)(2,1)S(1)} %select_dynamic-update-slice_fusion.refs_10_.refs_0_.refs_18_), channel_id=1, source_target_pairs={{0,4},{8,0},{16,8},{24,16},{28,24},{20,28},{12,20},{4,12},{1,5},{9... | collective-permute-start | bytes 1032200 | tf_op jit(solution)/shard_map/ppermute | solution.py:52
  67.2 14.5 %collective-permute-start.28 = (bf16[1024,128]{1,0:T(8,128)(2,1)S(1)}, bf16[1024,128]{1,0:T(8,128)(2,1)S(1)}, u32[]{:S(2)}, u32[]{:S(2)}) collective-permute-start(bf16[1024,128]{1,0:T(8,128)(2,1)S(1)} %collective-permute-done.13.refs_6_), channel_id=1, source_target_pairs={{0,8},{8,16},{16,24},{24,28},{28,20},{20,12},{12,4},{4,0},{1,9},{9... | collective-permute-start | bytes 786440 | tf_op jit(solution)/shard_map/ppermute | solution.py:52
  68.8 14.5 %collective-permute-start.32 = (bf16[1024,128]{1,0:T(8,128)(2,1)S(1)}, bf16[1024,128]{1,0:T(8,128)(2,1)S(1)}, u32[]{:S(2)}, u32[]{:S(2)}) collective-permute-start(bf16[1024,128]{1,0:T(8,128)(2,1)S(1)} %collective-permute-done.14.refs_8_), channel_id=1, source_target_pairs={{0,4},{8,0},{16,8},{24,16},{28,24},{20,28},{12,20},{4,12},{1,5},{9... | collective-permute-start | bytes 786440 | tf_op jit(solution)/shard_map/ppermute | solution.py:52
  76.1 13.0 %collective-permute-start.24 = (bf16[336,512]{1,0:T(8,128)(2,1)S(1)}, bf16[336,512]{1,0:T(8,128)(2,1)S(1)}, u32[]{:S(2)}, u32[]{:S(2)}) collective-permute-start(bf16[336,512]{1,0:T(8,128)(2,1)S(1)} %collective-permute-done.22.refs_11_.refs_1_.refs_19_), channel_id=1, source_target_pairs={{0,8},{8,16},{16,24},{24,28},{28,20},{20,12},{12,4},{4,0},{1,9},{9... | collective-permute-start | bytes 1032200 | tf_op jit(solution)/shard_map/ppermute | solution.py:52
  77.7 13.0 %collective-permute-start.25 = (bf16[336,512]{1,0:T(8,128)(2,1)S(1)}, bf16[336,512]{1,0:T(8,128)(2,1)S(1)}, u32[]{:S(2)}, u32[]{:S(2)}) collective-permute-start(bf16[336,512]{1,0:T(8,128)(2,1)S(1)} %collective-permute-done.23.refs_12_.refs_2_.refs_20_), channel_id=1, source_target_pairs={{0,4},{8,0},{16,8},{24,16},{28,24},{20,28},{12,20},{4,12},{1,5},{9... | collective-permute-start | bytes 1032200 | tf_op jit(solution)/shard_map/ppermute | solution.py:52
  81.7 13.0 %collective-permute-start.29 = (bf16[1024,128]{1,0:T(8,128)(2,1)S(1)}, bf16[1024,128]{1,0:T(8,128)(2,1)S(1)}, u32[]{:S(2)}, u32[]{:S(2)}) collective-permute-start(bf16[1024,128]{1,0:T(8,128)(2,1)S(1)} %collective-permute-done.19.refs_7_), channel_id=1, source_target_pairs={{0,8},{8,16},{16,24},{24,28},{28,20},{20,12},{12,4},{4,0},{1,9},{9... | collective-permute-start | bytes 786440 | tf_op jit(solution)/shard_map/ppermute | solution.py:52
  83.3 13.0 %collective-permute-start.33 = (bf16[1024,128]{1,0:T(8,128)(2,1)S(1)}, bf16[1024,128]{1,0:T(8,128)(2,1)S(1)}, u32[]{:S(2)}, u32[]{:S(2)}) collective-permute-start(bf16[1024,128]{1,0:T(8,128)(2,1)S(1)} %collective-permute-done.20.refs_9_), channel_id=1, source_target_pairs={{0,4},{8,0},{16,8},{24,16},{28,24},{20,28},{12,20},{4,12},{1,5},{9... | collective-permute-start | bytes 786440 | tf_op jit(solution)/shard_map/ppermute | solution.py:52
  89.0 19.1 %collective-permute-start.26 = (bf16[336,512]{1,0:T(8,128)(2,1)S(1)}, bf16[336,512]{1,0:T(8,128)(2,1)S(1)}, u32[]{:S(2)}, u32[]{:S(2)}) collective-permute-start(bf16[336,512]{1,0:T(8,128)(2,1)S(1)} %collective-permute-done.24.refs_13_.refs_3_.refs_21_), channel_id=1, source_target_pairs={{0,8},{8,16},{16,24},{24,28},{28,20},{20,12},{12,4},{4,0},{1,9},{9... | collective-permute-start | bytes 1032200 | tf_op jit(solution)/shard_map/ppermute | solution.py:52
  90.7 18.0 %collective-permute-start.27 = (bf16[336,512]{1,0:T(8,128)(2,1)S(1)}, bf16[336,512]{1,0:T(8,128)(2,1)S(1)}, u32[]{:S(2)}, u32[]{:S(2)}) collective-permute-start(bf16[336,512]{1,0:T(8,128)(2,1)S(1)} %collective-permute-done.25.refs_14_.refs_4_.refs_22_), channel_id=1, source_target_pairs={{0,4},{8,0},{16,8},{24,16},{28,24},{20,28},{12,20},{4,12},{1,5},{9... | collective-permute-start | bytes 1032200 | tf_op jit(solution)/shard_map/ppermute | solution.py:52
  94.7 12.2 %collective-permute-start.30 = (bf16[1024,128]{1,0:T(8,128)(2,1)S(1)}, bf16[1024,128]{1,0:T(8,128)(2,1)S(1)}, u32[]{:S(2)}, u32[]{:S(2)}) collective-permute-start(bf16[1024,128]{1,0:T(8,128)(2,1)S(1)} %collective-permute-done.28.refs_2_), channel_id=1, source_target_pairs={{0,8},{8,16},{16,24},{24,28},{28,20},{20,12},{12,4},{4,0},{1,9},{9... | collective-permute-start | bytes 786440 | tf_op jit(solution)/shard_map/ppermute | solution.py:52
  96.3 11.9 %collective-permute-start.34 = (bf16[1024,128]{1,0:T(8,128)(2,1)S(1)}, bf16[1024,128]{1,0:T(8,128)(2,1)S(1)}, u32[]{:S(2)}, u32[]{:S(2)}) collective-permute-start(bf16[1024,128]{1,0:T(8,128)(2,1)S(1)} %collective-permute-done.33.refs_5_), channel_id=1, source_target_pairs={{0,4},{8,0},{16,8},{24,16},{28,24},{20,28},{12,20},{4,12},{1,5},{9... | collective-permute-start | bytes 786440 | tf_op jit(solution)/shard_map/ppermute | solution.py:52
  96.7 12.1 %collective-permute-start.36 = (bf16[336,512]{1,0:T(8,128)(2,1)S(1)}, bf16[336,512]{1,0:T(8,128)(2,1)S(1)}, u32[]{:S(2)}, u32[]{:S(2)}) collective-permute-start(bf16[336,512]{1,0:T(8,128)(2,1)S(1)} %select_dynamic-update-slice_fusion.refs_10_.refs_0_.refs_18_), channel_id=1, source_target_pairs={{0,1},{1,0},{2,3},{3,2},{4,5},{5,4},{6,7},{7,6},{8,9},{9,8},{10,11... | collective-permute-start | bytes 1032200 | tf_op jit(solution)/shard_map/ppermute | solution.py:19
  106.9 3.5 %collective-permute-start.37 = (bf16[336,512]{1,0:T(8,128)(2,1)S(1)}, bf16[336,512]{1,0:T(8,128)(2,1)S(1)}, u32[]{:S(2)}, u32[]{:S(2)}) collective-permute-start(bf16[336,512]{1,0:T(8,128)(2,1)S(1)} %collective-permute-done.22.refs_11_.refs_1_.refs_19_), channel_id=1, source_target_pairs={{0,1},{1,0},{2,3},{3,2},{4,5},{5,4},{6,7},{7,6},{8,9},{9,8},{10,11... | collective-permute-start | bytes 1032200 | tf_op jit(solution)/shard_map/ppermute | solution.py:19
  108.2 2.7 %collective-permute-start.38 = (bf16[336,512]{1,0:T(8,128)(2,1)S(1)}, bf16[336,512]{1,0:T(8,128)(2,1)S(1)}, u32[]{:S(2)}, u32[]{:S(2)}) collective-permute-start(bf16[336,512]{1,0:T(8,128)(2,1)S(1)} %collective-permute-done.23.refs_12_.refs_2_.refs_20_), channel_id=1, source_target_pairs={{0,1},{1,0},{2,3},{3,2},{4,5},{5,4},{6,7},{7,6},{8,9},{9,8},{10,11... | collective-permute-start | bytes 1032200 | tf_op jit(solution)/shard_map/ppermute | solution.py:19
  108.2 2.7 %collective-permute-start.39 = (bf16[336,512]{1,0:T(8,128)(2,1)S(1)}, bf16[336,512]{1,0:T(8,128)(2,1)S(1)}, u32[]{:S(2)}, u32[]{:S(2)}) collective-permute-start(bf16[336,512]{1,0:T(8,128)(2,1)S(1)} %collective-permute-done.24.refs_13_.refs_3_.refs_21_), channel_id=1, source_target_pairs={{0,1},{1,0},{2,3},{3,2},{4,5},{5,4},{6,7},{7,6},{8,9},{9,8},{10,11... | collective-permute-start | bytes 1032200 | tf_op jit(solution)/shard_map/ppermute | solution.py:19
  108.7 2.7 %collective-permute-start.40 = (bf16[336,512]{1,0:T(8,128)(2,1)S(1)}, bf16[336,512]{1,0:T(8,128)(2,1)S(1)}, u32[]{:S(2)}, u32[]{:S(2)}) collective-permute-start(bf16[336,512]{1,0:T(8,128)(2,1)S(1)} %collective-permute-done.25.refs_14_.refs_4_.refs_22_), channel_id=1, source_target_pairs={{0,1},{1,0},{2,3},{3,2},{4,5},{5,4},{6,7},{7,6},{8,9},{9,8},{10,11... | collective-permute-start | bytes 1032200 | tf_op jit(solution)/shard_map/ppermute | solution.py:19
  108.8 6.8 %collective-permute-start.31 = (bf16[336,256]{1,0:T(8,128)(2,1)S(1)}, bf16[336,256]{1,0:T(8,128)(2,1)S(1)}, u32[]{:S(2)}, u32[]{:S(2)}) collective-permute-start(bf16[336,256]{1,0:T(8,128)(2,1)S(1)} %slice.12), channel_id=1, source_target_pairs={{0,8},{8,16},{16,24},{24,28},{28,20},{20,12},{12,4},{4,0},{1,9},{9... | collective-permute-start | bytes 516104 | tf_op jit(solution)/shard_map/ppermute | solution.py:52
  110.4 6.4 %collective-permute-start.35 = (bf16[336,256]{1,0:T(8,128)(2,1)S(1)}, bf16[336,256]{1,0:T(8,128)(2,1)S(1)}, u32[]{:S(2)}, u32[]{:S(2)}) collective-permute-start(bf16[336,256]{1,0:T(8,128)(2,1)S(1)} %slice.13), channel_id=1, source_target_pairs={{0,4},{8,0},{16,8},{24,16},{28,24},{20,28},{12,20},{4,12},{1,5},{9... | collective-permute-start | bytes 516104 | tf_op jit(solution)/shard_map/ppermute | solution.py:52
  110.9 5.9 %collective-permute-start.41 = (bf16[336,512]{1,0:T(8,128)(2,1)S(1)}, bf16[336,512]{1,0:T(8,128)(2,1)S(1)}, u32[]{:S(2)}, u32[]{:S(2)}) collective-permute-start(bf16[336,512]{1,0:T(8,128)(2,1)S(1)} %collective-permute-done.26.refs_5_.refs_23_.refs_8_), channel_id=1, source_target_pairs={{0,1},{1,0},{2,3},{3,2},{4,5},{5,4},{6,7},{7,6},{8,9},{9,8},{10,11... | collective-permute-start | bytes 1032200 | tf_op jit(solution)/shard_map/ppermute | solution.py:19
  110.9 5.9 %collective-permute-start.42 = (bf16[336,512]{1,0:T(8,128)(2,1)S(1)}, bf16[336,512]{1,0:T(8,128)(2,1)S(1)}, u32[]{:S(2)}, u32[]{:S(2)}) collective-permute-start(bf16[336,512]{1,0:T(8,128)(2,1)S(1)} %collective-permute-done.27.refs_6_.refs_24_.refs_9_), channel_id=1, source_target_pairs={{0,1},{1,0},{2,3},{3,2},{4,5},{5,4},{6,7},{7,6},{8,9},{9,8},{10,11... | collective-permute-start | bytes 1032200 | tf_op jit(solution)/shard_map/ppermute | solution.py:19
  115.6 1.4 %collective-permute-start.43 = (bf16[336,256]{1,0:T(8,128)(2,1)S(1)}, bf16[336,256]{1,0:T(8,128)(2,1)S(1)}, u32[]{:S(2)}, u32[]{:S(2)}) collective-permute-start(bf16[336,256]{1,0:T(8,128)(2,1)S(1)} %collective-permute-done.31.refs_7_.refs_25_.refs_10_), channel_id=1, source_target_pairs={{0,1},{1,0},{2,3},{3,2},{4,5},{5,4},{6,7},{7,6},{8,9},{9,8},{10,11... | collective-permute-start | bytes 516104 | tf_op jit(solution)/shard_map/ppermute | solution.py:19
  116.8 1.4 %collective-permute-start.44 = (bf16[336,256]{1,0:T(8,128)(2,1)S(1)}, bf16[336,256]{1,0:T(8,128)(2,1)S(1)}, u32[]{:S(2)}, u32[]{:S(2)}) collective-permute-start(bf16[336,256]{1,0:T(8,128)(2,1)S(1)} %collective-permute-done.35.refs_8_.refs_26_.refs_11_), channel_id=1, source_target_pairs={{0,1},{1,0},{2,3},{3,2},{4,5},{5,4},{6,7},{7,6},{8,9},{9,8},{10,11... | collective-permute-start | bytes 516104 | tf_op jit(solution)/shard_map/ppermute | solution.py:19
  119.0 5.5 %collective-permute-start.45 = (bf16[256,256]{1,0:T(8,128)(2,1)S(1)}, bf16[256,256]{1,0:T(8,128)(2,1)S(1)}, u32[]{:S(2)}, u32[]{:S(2)}) collective-permute-start(bf16[256,256]{1,0:T(8,128)(2,1)S(1)} %get-tuple-element.114.refs_0_), channel_id=1, source_target_pairs={{0,2},{1,3},{2,0},{3,1},{4,6},{5,7},{6,4},{7,5},{8,10},{9,11},{10,... | collective-permute-start | bytes 393224 | tf_op jit(solution)/shard_map/ppermute | solution.py:19

commit v2 on v1

--- a/solution.py
+++ b/solution.py
@@ -12,6 +12,16 @@
 F32 = jnp.float32
 BF16 = jnp.bfloat16
 MIB = 1 << 20
+HOLDS = {
+    "give": ("s0t1",),
+    "heads": ("s0t2", "s1t1", "s1t2"),
+    "share": ("s1t2",),
+    "s0t3": ("s1t2",),
+    "s1t3": ("s0t3",),
+    "s0t4": ("s1t3",),
+    "p4": ("s1t3",),
+}
+EARLY = ("s0t2", "s1t2", "s0t3")
 
 
 def swap(block, bit):
@@ -54,13 +64,16 @@
 
 class Ring:
     def __init__(self):
-        self.arrived = []
-
-    def step(self, *pair):
-        held = self.arrived[-2] if len(self.arrived) > 1 else ((), ())
-        up, down = (after(b, *h) for b, h in zip(pair, held))
-        self.arrived.append(((ring_step(up, 1),), (ring_step(down, -1),)))
-        return [self.arrived[-1][0][0], self.arrived[-1][1][0]]
+        self.at = {}
+
+    def arrived(self, names):
+        return [b for name in names for b in self.at.get(name, ())]
+
+    def step(self, name, up, down):
+        held = HOLDS.get(name, ())
+        up, down = after(up, *self.arrived(held)), after(down, *self.arrived(held))
+        self.at[name] = [ring_step(up, 1), ring_step(down, -1)]
+        return self.at[name]
 
 
 def dot(a, b):
@@ -582,21 +595,23 @@
         )
         turned.append(one)
         if s == 0:
-            shards.append([ring.step(one, one)])
+            shards.append([ring.step("s0t1", one, one)])
     new_latent, keep, give, squares = filled
 
     for bit in (1, *far_bits()):
         squares = squares + swap(squares, bit)
-    pre = keep + swap(after(give, *shards[0][0]), 1).astype(F32)
+    shards += [[ring.step(f"s{k + 1}t1", one, one)] for k, one in enumerate(turned[1:])]
+    pre = keep + swap(after(give, *ring.arrived(HOLDS["give"])), 1).astype(F32)
     mine = pre.astype(BF16)
     *upper, last = far_bits()
     for bit in upper:
         mine = (mine.astype(F32) + swap(mine, bit).astype(F32)).astype(BF16)
     rounds = wide_size // 2
-    shards += [[ring.step(one, one)] for one in turned[1:]]
-    for shard in shards:
-        shard.append(ring.step(*shard[-1]))
-    theirs = after(swap(mine, last), *shards[0][-1], *(b for one in shards for b in one[0]))
+    for step in range(2, rounds):
+        for k, shard in enumerate(shards):
+            if f"s{k}t{step}" in EARLY:
+                shard.append(ring.step(f"s{k}t{step}", *shard[-1]))
+    theirs = after(swap(mine, last), *ring.arrived(HOLDS["heads"]))
     quarter = hidden_count // chips // 4
     payload_shape = (rows + quarter + 16, hidden_count)
     payload, give = call(
@@ -616,29 +631,24 @@
         [whole(payload_shape), whole((quarter, hidden_count))],
         6 * rows * hidden_count * action_count, 16 * MIB, [pltpu.VMEM(half, BF16)],
     )
-    shards[0].append(ring.step(*shards[0][-1]))
-    given = swap(after(give, *shards[-1][-1]), 1)
-    taken = jnp.where(first, payload[rows : rows + quarter], given)
+    taken = jnp.where(first, payload[rows : rows + quarter], swap(after(give, *ring.arrived(HOLDS["share"])), 1))
     payload = lax.dynamic_update_slice(payload, taken, (rows, 0))
 
     payload_rounds = [[payload, payload]]
-    payload_rounds.append(ring.step(*payload_rounds[-1]))
-    for step in range(2, rounds - 1):
-        for shard in shards:
-            if len(shard) == step:
-                shard.append(ring.step(*shard[-1]))
-                if len(payload_rounds) < rounds - 1:
-                    payload_rounds.append(ring.step(*payload_rounds[-1]))
-    cut = scenes // 2
-    for one, other in zip(shards[:cut], shards[cut:]):
-        up, down = ring.step(one[-1][0], other[-1][1])
-        one.append([up])
-        other.append([down])
-    while len(payload_rounds) < rounds:
-        payload_rounds.append(ring.step(*payload_rounds[-1]))
-    size = hidden_count // 2
-    up, down = payload_rounds[-1]
-    payload_rounds.append(ring.step(up[:, :size], down[:, size:]))
+    cut, size = scenes // 2, hidden_count // 2
+    for step in range(1, rounds + 1):
+        up, down = payload_rounds[-1]
+        if step == rounds:
+            up, down = up[:, :size], down[:, size:]
+        payload_rounds.append(ring.step(f"p{step}", up, down))
+        for k, shard in enumerate(shards):
+            if len(shard) == step and step < rounds - 1:
+                shard.append(ring.step(f"s{k}t{step + 1}", *shard[-1]))
+        if step == rounds - 1:
+            for k, (one, other) in enumerate(zip(shards[:cut], shards[cut:])):
+                up, down = ring.step(f"s{k}t{rounds}", one[-1][0], other[-1][1])
+                one.append([up])
+                other.append([down])
     turned_all = list(turned)
     for step in range(rounds):
         for way in range(len(shards[0][step])):
@@ -670,7 +680,7 @@
         )
 
     starts = gradient(
-        gradients_start, "gradients_start", [], [], split, turned_all[: scenes * split],
+        gradients_start, "gradients_start", [], [], 0, turned_all[: scenes * split],
         payload_own[:split], payload_other[:split], F32,
     )
     payload_other += [swap(b, 1) for b in payload_own[split:-2]]

time: 125 us -> 120 us (0.960)
  waiting for transfers between devices: 65.8 us -> 57.7 us
  starting transfers between devices: 32.3 us -> 35.4 us
    ppermute x22, waiting for transfers between devices: 49.7 us -> 41 us  [ring_step(): return lax.ppermute(block, 'wide', pairs)]
    ppermute x22, starting transfers between devices: 22.4 us -> 26 us  [ring_step(): return lax.ppermute(block, 'wide', pairs)]
where the time goes in v2:
time: 120 us
  waiting for transfers between devices  57.7 us (48%)
  starting transfers between devices  35.4 us (30%)
  Pallas kernels  26.2 us (22%)
    ppermute x22, waiting for transfers between devices, ring_step(): return lax.ppermute(block, 'wide', pairs)  41 us
    pallas_call x13, Pallas kernels, call(): pl.pallas_call(body, name=name, out_shape=outs, input_output_aliases=alia...  26.2 us
    ppermute x22, starting transfers between devices, ring_step(): return lax.ppermute(block, 'wide', pairs)  26 us
    ppermute x24, waiting for transfers between devices, swap(): return lax.ppermute(block, 'narrow', [(n, n ^ bit) for n in range(size)])  16.7 us
    ppermute x24, starting transfers between devices, swap(): return lax.ppermute(block, 'narrow', [(n, n ^ bit) for n in range(size)])  9.33 us
  transfers between devices with their start and end apart: 46, of which 25 were waited for; matrix products, arithmetic and copies ran while one was open for 0% of the time, Pallas kernels for 17%

profile of v2, /device:TPU:0, one launch (start us, length us, event | category | flops | bytes accessed | tf_op | source)
XLA Modules:
  0.0 120.3 jit_solution(5035677475676385857)
XLA Ops:
  0.6 1.7 %embed.1 = (f32[256,1024]{1,0:T(8,128)S(1)}, bf16[272,1024]{1,0:T(8,128)(2,1)S(1)}) custom-call(s32[1]{0:T(128)} %bitcast.p_ref, bf16[256,1024]{1,0:T(8,128)(2,1)} %latent_ref.1, s32[1,256]{1,0:T(1,128)} %bitcast.12, bf16[256,1024]{1,0:T(8,128)(2,1)} %table_ref.1, f32[1,1024]{1,0:T(1,128)} %bitcast.11), custom_call_target="tpu_custom_call" | custom-call | flops 134217728 | bytes 2659328 | tf_op jit(solution)/shard_map/embed/pallas_call | solution.py:407
  2.4 0.5 collective-permute-start
  2.9 2.6 %collective-permute-start.1 = (bf16[272,1024]{1,0:T(8,128)(2,1)S(1)}, bf16[272,1024]{1,0:T(8,128)(2,1)S(1)}, u32[]{:S(2)}, u32[]{:S(2)}) collective-permute-start(bf16[272,1024]{1,0:T(8,128)(2,1)S(1)} %get-tuple-element.52.refs_0_), channel_id=1, source_target_pairs={{0,2},{1,3},{2,0},{3,1},{4,6},{5,7},{6,4},{7,5},{8,10},{9,11},{10,... | collective-permute-start | bytes 1671176 | tf_op jit(solution)/shard_map/ppermute | solution.py:29
  5.5 5.3 %begin.1 = (f32[256,1536]{1,0:T(8,128)S(1)}, bf16[1024,512]{1,0:T(8,128)(2,1)S(1)}, bf16[1024,512]{1,0:T(8,128)(2,1)S(1)}, bf16[1024,512]{1,0:T(8,128)(2,1)S(1)}...) custom-call(s32[1]{0:T(128)} %bitcast.p_ref, ...), custom_call_target="tpu_custom_call" | custom-call | flops 1610612736 | bytes 25755648 | tf_op jit(solution)/shard_map/begin/pallas_call | solution.py:407
  10.8 7.9 %collective-permute-done.1.refs_0_.refs_1_ = bf16[272,1024]{1,0:T(8,128)(2,1)S(1)} collective-permute-done((bf16[272,1024]{1,0:T(8,128)(2,1)S(1)}, bf16[272,1024]{1,0:T(8,128)(2,1)S(1)}, u32[]{:S(2)}, u32[]{:S(2)}) %collective-permute-start.1) | collective-permute-done | bytes 557088 | tf_op jit(solution)/shard_map/ppermute | solution.py:29
  18.7 1.0 project.1.acc_ref
  19.7 1.0 collective-permute-done.2.refs_3_.refs_4_
  20.6 2.0 %attend0.1.refs_0_ = bf16[128,512]{1,0:T(8,128)(2,1)S(1)} custom-call(s32[1]{0:T(128)} %bitcast.p_ref, f32[256,1536]{1,0:T(8,128)S(1)} %project.1.acc_ref, bf16[2,512,512]{2,1,0:T(8,128)(2,1)S(1)} %get-tuple-element.57.keys_ref, bf16[2,512,512]{2,1,0:T(8,128)(2,1)S(1)} %get-tuple-element.58.values_ref, bf16[272,1024]{1,0:T(8,128)(2,1)S(1)} %get-tuple-element.52.refs_0_, ...), custom_call_target="tpu_custom_call" | custom-call | tf_op jit(solution)/shard_map/attend0/pallas_call | solution.py:407
  22.7 1.8 %collective-permute-start.6 = (bf16[128,512]{1,0:T(8,128)(2,1)S(1)}, bf16[128,512]{1,0:T(8,128)(2,1)S(1)}, u32[]{:S(2)}, u32[]{:S(2)}) collective-permute-start(bf16[128,512]{1,0:T(8,128)(2,1)S(1)} %attend0.1.refs_0_), channel_id=1, source_target_pairs={{0,2},{1,3},{2,0},{3,1},{4,6},{5,7},{6,4},{7,5},{8,10},{9,11},{10,... | collective-permute-start | bytes 393224 | tf_op jit(solution)/shard_map/ppermute | solution.py:29
  24.5 2.0 %attend1.1.refs_1_ = bf16[128,512]{1,0:T(8,128)(2,1)S(1)} custom-call(s32[1]{0:T(128)} %bitcast.p_ref, f32[256,1536]{1,0:T(8,128)S(1)} %project.1.acc_ref, bf16[2,512,512]{2,1,0:T(8,128)(2,1)S(1)} %get-tuple-element.57.keys_ref, bf16[2,512,512]{2,1,0:T(8,128)(2,1)S(1)} %get-tuple-element.58.values_ref, bf16[272,1024]{1,0:T(8,128)(2,1)S(1)} %get-tuple-element.52.refs_0_, ...), custom_call_target="tpu_custom_call" | custom-call | tf_op jit(solution)/shard_map/attend1/pallas_call | solution.py:407
  26.5 0.6 collective-permute-start.4
  27.1 1.2 collective-permute-done.6.refs_0_
  28.3 1.7 %collective-permute-start.5 = (bf16[128,512]{1,0:T(8,128)(2,1)S(1)}, bf16[128,512]{1,0:T(8,128)(2,1)S(1)}, u32[]{:S(2)}, u32[]{:S(2)}) collective-permute-start(bf16[128,512]{1,0:T(8,128)(2,1)S(1)} %attend1.1.refs_1_), channel_id=1, source_target_pairs={{0,2},{1,3},{2,0},{3,1},{4,6},{5,7},{6,4},{7,5},{8,10},{9,11},{10,... | collective-permute-start | bytes 393224 | tf_op jit(solution)/shard_map/ppermute | solution.py:29
  30.0 1.0 update_near.1.acc_ref
  31.0 1.8 %update0.1 = (bf16[256,1024]{1,0:T(8,128)(2,1)}, f32[256,512]{1,0:T(8,128)S(1)}, bf16[256,512]{1,0:T(8,128)(2,1)S(1)}, f32[8,256]{1,0:T(8,128)S(1)}, bf16[1024,128]{1,0:T(8,128)(2,1)S(1)}) custom-call(s32[1]{0:T(128)} %bitcast.p_ref, f32[256,1024]{1,0:T(8,128)S(1)} %update_near.1.acc_ref, f32[1,1024]{1,0:T(1,128)S(1)} %bitcast.7, ...), custom_call_target="tpu_custom_call" | custom-call | flops 536870912 | bytes 9187328 | tf_op jit(solution)/shard_map/update0/pallas_call | solution.py:407
  32.8 1.6 %collective-permute-start.9 = (bf16[1024,128]{1,0:T(8,128)(2,1)S(1)}, bf16[1024,128]{1,0:T(8,128)(2,1)S(1)}, u32[]{:S(2)}, u32[]{:S(2)}) collective-permute-start(bf16[1024,128]{1,0:T(8,128)(2,1)S(1)} %get-tuple-element.63.refs_0_), channel_id=1, source_target_pairs={{0,8},{8,16},{16,24},{24,28},{28,20},{20,12},{12,4},{4,0},{1,9},{9... | collective-permute-start | bytes 786440 | tf_op jit(solution)/shard_map/ppermute | solution.py:62
  34.4 0.5 collective-permute-start.10
  34.8 1.3 %collective-permute-done.8.refs_1_ = bf16[128,512]{1,0:T(8,128)(2,1)S(1)} collective-permute-done((bf16[128,512]{1,0:T(8,128)(2,1)S(1)}, bf16[128,512]{1,0:T(8,128)(2,1)S(1)}, u32[]{:S(2)}, u32[]{:S(2)}) %collective-permute-start.8) | collective-permute-done | bytes 131104 | tf_op jit(solution)/shard_map/ppermute | solution.py:29
  36.2 1.8 %update1.1 = (bf16[256,1024]{1,0:T(8,128)(2,1)}, f32[256,512]{1,0:T(8,128)S(1)}, bf16[256,512]{1,0:T(8,128)(2,1)S(1)}, f32[8,256]{1,0:T(8,128)S(1)}, bf16[1024,128]{1,0:T(8,128)(2,1)S(1)}) custom-call(s32[1]{0:T(128)} %bitcast.p_ref, f32[256,1024]{1,0:T(8,128)S(1)} %update_near.1.acc_ref, ...), custom_call_target="tpu_custom_call", output_to_operand_aliasing={{0}: (8, {}), {1}: (9, {}), {2}: (10, {}), {3}: (11, {})} | custom-call | flops 536870912 | bytes 10506240 | tf_op jit(solution)/shard_map/update1/pallas_call | solution.py:407
  38.0 1.6 %collective-permute-start.15 = (bf16[1024,128]{1,0:T(8,128)(2,1)S(1)}, bf16[1024,128]{1,0:T(8,128)(2,1)S(1)}, u32[]{:S(2)}, u32[]{:S(2)}) collective-permute-start(bf16[1024,128]{1,0:T(8,128)(2,1)S(1)} %get-tuple-element.73.refs_1_), channel_id=1, source_target_pairs={{0,8},{8,16},{16,24},{24,28},{28,20},{20,12},{12,4},{4,0},{1,9},{9... | collective-permute-start | bytes 786440 | tf_op jit(solution)/shard_map/ppermute | solution.py:62
  39.5 0.5 collective-permute-start.16
  40.0 1.8 %collective-permute-done.9.refs_2_ = bf16[1024,128]{1,0:T(8,128)(2,1)S(1)} collective-permute-done((bf16[1024,128]{1,0:T(8,128)(2,1)S(1)}, bf16[1024,128]{1,0:T(8,128)(2,1)S(1)}, u32[]{:S(2)}, u32[]{:S(2)}) %collective-permute-start.9) | collective-permute-done | bytes 262176 | tf_op jit(solution)/shard_map/ppermute | solution.py:62
  41.8 1.3 %collective-permute-done.10.refs_4_ = bf16[1024,128]{1,0:T(8,128)(2,1)S(1)} collective-permute-done((bf16[1024,128]{1,0:T(8,128)(2,1)S(1)}, bf16[1024,128]{1,0:T(8,128)(2,1)S(1)}, u32[]{:S(2)}, u32[]{:S(2)}) %collective-permute-start.10) | collective-permute-done | bytes 262176 | tf_op jit(solution)/shard_map/ppermute | solution.py:62
  43.1 0.5 collective-permute-start.19
  43.6 1.0 collective-permute-done.19
  44.6 1.6 %collective-permute-start.13 = (bf16[1024,128]{1,0:T(8,128)(2,1)S(1)}, bf16[1024,128]{1,0:T(8,128)(2,1)S(1)}, u32[]{:S(2)}, u32[]{:S(2)}) collective-permute-start(bf16[1024,128]{1,0:T(8,128)(2,1)S(1)} %collective-permute-done.9.refs_2_), channel_id=1, source_target_pairs={{0,8},{8,16},{16,24},{24,28},{28,20},{20,12},{12,4},{4,0},{1,9},{9... | collective-permute-start | bytes 786440 | tf_op jit(solution)/shard_map/ppermute | solution.py:62
  46.2 0.7 collective-permute-done.15.refs_3_
  46.9 2.0 %collective-permute-start.14 = (bf16[1024,128]{1,0:T(8,128)(2,1)S(1)}, bf16[1024,128]{1,0:T(8,128)(2,1)S(1)}, u32[]{:S(2)}, u32[]{:S(2)}) collective-permute-start(bf16[1024,128]{1,0:T(8,128)(2,1)S(1)} %collective-permute-done.10.refs_4_), channel_id=1, source_target_pairs={{0,4},{8,0},{16,8},{24,16},{28,24},{20,28},{12,20},{4,12},{1,5},{9... | collective-permute-start | bytes 786440 | tf_op jit(solution)/shard_map/ppermute | solution.py:62
  48.9 0.9 collective-permute-start.17
  49.8 1.1 collective-permute-start.18
  51.1 2.7 %collective-permute-done.13.refs_6_ = bf16[1024,128]{1,0:T(8,128)(2,1)S(1)} collective-permute-done((bf16[1024,128]{1,0:T(8,128)(2,1)S(1)}, bf16[1024,128]{1,0:T(8,128)(2,1)S(1)}, u32[]{:S(2)}, u32[]{:S(2)}) %collective-permute-start.13) | collective-permute-done | bytes 262176 | tf_op jit(solution)/shard_map/ppermute | solution.py:62
  53.8 2.3 %collective-permute-done.14.refs_8_ = bf16[1024,128]{1,0:T(8,128)(2,1)S(1)} collective-permute-done((bf16[1024,128]{1,0:T(8,128)(2,1)S(1)}, bf16[1024,128]{1,0:T(8,128)(2,1)S(1)}, u32[]{:S(2)}, u32[]{:S(2)}) %collective-permute-start.14) | collective-permute-done | bytes 262176 | tf_op jit(solution)/shard_map/ppermute | solution.py:62
  56.1 2.5 %collective-permute-done.17.refs_7_ = bf16[1024,128]{1,0:T(8,128)(2,1)S(1)} collective-permute-done((bf16[1024,128]{1,0:T(8,128)(2,1)S(1)}, bf16[1024,128]{1,0:T(8,128)(2,1)S(1)}, u32[]{:S(2)}, u32[]{:S(2)}) %collective-permute-start.17) | collective-permute-done | bytes 262176 | tf_op jit(solution)/shard_map/ppermute | solution.py:62
  58.6 1.8 %collective-permute-done.18.refs_9_ = bf16[1024,128]{1,0:T(8,128)(2,1)S(1)} collective-permute-done((bf16[1024,128]{1,0:T(8,128)(2,1)S(1)}, bf16[1024,128]{1,0:T(8,128)(2,1)S(1)}, u32[]{:S(2)}, u32[]{:S(2)}) %collective-permute-start.18) | collective-permute-done | bytes 262176 | tf_op jit(solution)/shard_map/ppermute | solution.py:62
  60.4 1.1 heads.1
  61.6 1.2 %collective-permute-done.21 = bf16[64,512]{1,0:T(8,128)(2,1)S(1)} collective-permute-done((bf16[64,512]{1,0:T(8,128)(2,1)S(1)}, bf16[64,512]{1,0:T(8,128)(2,1)S(1)}, u32[]{:S(2)}, u32[]{:S(2)}) %collective-permute-start.21) | collective-permute-done | bytes 65568 | tf_op jit(solution)/shard_map/ppermute | solution.py:29
  62.8 1.6 %collective-permute-start.22 = (bf16[336,512]{1,0:T(8,128)(2,1)S(1)}, bf16[336,512]{1,0:T(8,128)(2,1)S(1)}, u32[]{:S(2)}, u32[]{:S(2)}) collective-permute-start(bf16[336,512]{1,0:T(8,128)(2,1)S(1)} %select_dynamic-update-slice_fusion.refs_10_.refs_0_.refs_18_), channel_id=1, source_target_pairs={{0,8},{8,16},{16,24},{24,28},{28,20},{20,12},{12,4},{4,0},{1,9},{9... | collective-permute-start | bytes 1032200 | tf_op jit(solution)/shard_map/ppermute | solution.py:62
  64.5 0.5 collective-permute-start.23
  64.9 1.6 %collective-permute-start.28 = (bf16[1024,128]{1,0:T(8,128)(2,1)S(1)}, bf16[1024,128]{1,0:T(8,128)(2,1)S(1)}, u32[]{:S(2)}, u32[]{:S(2)}) collective-permute-start(bf16[1024,128]{1,0:T(8,128)(2,1)S(1)} %collective-permute-done.13.refs_6_), channel_id=1, source_target_pairs={{0,8},{8,16},{16,24},{24,28},{28,20},{20,12},{12,4},{4,0},{1,9},{9... | collective-permute-start | bytes 786440 | tf_op jit(solution)/shard_map/ppermute | solution.py:62
  66.9 6.9 %collective-permute-done.22.refs_11_.refs_1_.refs_19_ = bf16[336,512]{1,0:T(8,128)(2,1)S(1)} collective-permute-done((bf16[336,512]{1,0:T(8,128)(2,1)S(1)}, bf16[336,512]{1,0:T(8,128)(2,1)S(1)}, u32[]{:S(2)}, u32[]{:S(2)}) %collective-permute-start.22) | collective-permute-done | bytes 344096 | tf_op jit(solution)/shard_map/ppermute | solution.py:62
  73.8 1.6 %collective-permute-start.24 = (bf16[336,512]{1,0:T(8,128)(2,1)S(1)}, bf16[336,512]{1,0:T(8,128)(2,1)S(1)}, u32[]{:S(2)}, u32[]{:S(2)}) collective-permute-start(bf16[336,512]{1,0:T(8,128)(2,1)S(1)} %collective-permute-done.22.refs_11_.refs_1_.refs_19_), channel_id=1, source_target_pairs={{0,8},{8,16},{16,24},{24,28},{28,20},{20,12},{12,4},{4,0},{1,9},{9... | collective-permute-start | bytes 1032200 | tf_op jit(solution)/shard_map/ppermute | solution.py:62
  75.9 3.6 %collective-permute-done.28.refs_2_ = bf16[1024,128]{1,0:T(8,128)(2,1)S(1)} collective-permute-done((bf16[1024,128]{1,0:T(8,128)(2,1)S(1)}, bf16[1024,128]{1,0:T(8,128)(2,1)S(1)}, u32[]{:S(2)}, u32[]{:S(2)}) %collective-permute-start.28) | collective-permute-done | bytes 262176 | tf_op jit(solution)/shard_map/ppermute | solution.py:62
  79.4 1.6 %collective-permute-done.29.refs_4_ = bf16[1024,128]{1,0:T(8,128)(2,1)S(1)} collective-permute-done((bf16[1024,128]{1,0:T(8,128)(2,1)S(1)}, bf16[1024,128]{1,0:T(8,128)(2,1)S(1)}, u32[]{:S(2)}, u32[]{:S(2)}) %collective-permute-start.29) | collective-permute-done | bytes 262176 | tf_op jit(solution)/shard_map/ppermute | solution.py:62
  81.0 1.6 %collective-permute-start.30 = (bf16[1024,128]{1,0:T(8,128)(2,1)S(1)}, bf16[1024,128]{1,0:T(8,128)(2,1)S(1)}, u32[]{:S(2)}, u32[]{:S(2)}) collective-permute-start(bf16[1024,128]{1,0:T(8,128)(2,1)S(1)} %collective-permute-done.17.refs_7_), channel_id=1, source_target_pairs={{0,8},{8,16},{16,24},{24,28},{28,20},{20,12},{12,4},{4,0},{1,9},{9... | collective-permute-start | bytes 786440 | tf_op jit(solution)/shard_map/ppermute | solution.py:62
  83.1 3.7 %collective-permute-done.24.refs_13_.refs_3_.refs_21_ = bf16[336,512]{1,0:T(8,128)(2,1)S(1)} collective-permute-done((bf16[336,512]{1,0:T(8,128)(2,1)S(1)}, bf16[336,512]{1,0:T(8,128)(2,1)S(1)}, u32[]{:S(2)}, u32[]{:S(2)}) %collective-permute-start.24) | collective-permute-done | bytes 344096 | tf_op jit(solution)/shard_map/ppermute | solution.py:62
  86.8 1.6 %collective-permute-done.25.refs_14_.refs_4_.refs_22_ = bf16[336,512]{1,0:T(8,128)(2,1)S(1)} collective-permute-done((bf16[336,512]{1,0:T(8,128)(2,1)S(1)}, bf16[336,512]{1,0:T(8,128)(2,1)S(1)}, u32[]{:S(2)}, u32[]{:S(2)}) %collective-permute-start.25) | collective-permute-done | bytes 344096 | tf_op jit(solution)/shard_map/ppermute | solution.py:62
  88.4 1.6 %collective-permute-start.26 = (bf16[336,512]{1,0:T(8,128)(2,1)S(1)}, bf16[336,512]{1,0:T(8,128)(2,1)S(1)}, u32[]{:S(2)}, u32[]{:S(2)}) collective-permute-start(bf16[336,512]{1,0:T(8,128)(2,1)S(1)} %collective-permute-done.24.refs_13_.refs_3_.refs_21_), channel_id=1, source_target_pairs={{0,8},{8,16},{16,24},{24,28},{28,20},{20,12},{12,4},{4,0},{1,9},{9... | collective-permute-start | bytes 1032200 | tf_op jit(solution)/shard_map/ppermute | solution.py:62
  90.0 2.4 %collective-permute-done.30.refs_3_ = bf16[1024,128]{1,0:T(8,128)(2,1)S(1)} collective-permute-done((bf16[1024,128]{1,0:T(8,128)(2,1)S(1)}, bf16[1024,128]{1,0:T(8,128)(2,1)S(1)}, u32[]{:S(2)}, u32[]{:S(2)}) %collective-permute-start.30) | collective-permute-done | bytes 262176 | tf_op jit(solution)/shard_map/ppermute | solution.py:62
  92.4 1.5 %collective-permute-start.27 = (bf16[336,512]{1,0:T(8,128)(2,1)S(1)}, bf16[336,512]{1,0:T(8,128)(2,1)S(1)}, u32[]{:S(2)}, u32[]{:S(2)}) collective-permute-start(bf16[336,512]{1,0:T(8,128)(2,1)S(1)} %collective-permute-done.25.refs_14_.refs_4_.refs_22_), channel_id=1, source_target_pairs={{0,4},{8,0},{16,8},{24,16},{28,24},{20,28},{12,20},{4,12},{1,5},{9... | collective-permute-start | bytes 1032200 | tf_op jit(solution)/shard_map/ppermute | solution.py:62
  93.9 0.5 collective-permute-start.37
  94.5 4.5 %collective-permute-done.26.refs_5_.refs_23_.refs_8_ = bf16[336,512]{1,0:T(8,128)(2,1)S(1)} collective-permute-done((bf16[336,512]{1,0:T(8,128)(2,1)S(1)}, bf16[336,512]{1,0:T(8,128)(2,1)S(1)}, u32[]{:S(2)}, u32[]{:S(2)}) %collective-permute-start.26) | collective-permute-done | bytes 344096 | tf_op jit(solution)/shard_map/ppermute | solution.py:62
  99.0 1.9 %collective-permute-done.27.refs_6_.refs_24_.refs_9_ = bf16[336,512]{1,0:T(8,128)(2,1)S(1)} collective-permute-done((bf16[336,512]{1,0:T(8,128)(2,1)S(1)}, bf16[336,512]{1,0:T(8,128)(2,1)S(1)}, u32[]{:S(2)}, u32[]{:S(2)}) %collective-permute-start.27) | collective-permute-done | bytes 344096 | tf_op jit(solution)/shard_map/ppermute | solution.py:62
  100.9 1.6 %collective-permute-start.32 = (bf16[336,256]{1,0:T(8,128)(2,1)S(1)}, bf16[336,256]{1,0:T(8,128)(2,1)S(1)}, u32[]{:S(2)}, u32[]{:S(2)}) collective-permute-start(bf16[336,256]{1,0:T(8,128)(2,1)S(1)} %slice.12), channel_id=1, source_target_pairs={{0,8},{8,16},{16,24},{24,28},{28,20},{20,12},{12,4},{4,0},{1,9},{9... | collective-permute-start | bytes 516104 | tf_op jit(solution)/shard_map/ppermute | solution.py:62
  102.5 0.5 collective-permute-start.33
  103.0 1.6 %collective-permute-start.43 = (bf16[1024,128]{1,0:T(8,128)(2,1)S(1)}, bf16[1024,128]{1,0:T(8,128)(2,1)S(1)}, u32[]{:S(2)}, u32[]{:S(2)}) collective-permute-start(bf16[1024,128]{1,0:T(8,128)(2,1)S(1)} %collective-permute-done.28.refs_2_), channel_id=1, source_target_pairs={{0,8},{8,16},{16,24},{24,28},{28,20},{20,12},{12,4},{4,0},{1,9},{9... | collective-permute-start | bytes 786440 | tf_op jit(solution)/shard_map/ppermute | solution.py:62
  104.7 1.8 %collective-permute-done.32.refs_7_.refs_25_.refs_10_ = bf16[336,256]{1,0:T(8,128)(2,1)S(1)} collective-permute-done((bf16[336,256]{1,0:T(8,128)(2,1)S(1)}, bf16[336,256]{1,0:T(8,128)(2,1)S(1)}, u32[]{:S(2)}, u32[]{:S(2)}) %collective-permute-start.32) | collective-permute-done | bytes 172064 | tf_op jit(solution)/shard_map/ppermute | solution.py:62
  106.4 1.5 %collective-permute-start.44 = (bf16[1024,128]{1,0:T(8,128)(2,1)S(1)}, bf16[1024,128]{1,0:T(8,128)(2,1)S(1)}, u32[]{:S(2)}, u32[]{:S(2)}) collective-permute-start(bf16[1024,128]{1,0:T(8,128)(2,1)S(1)} %collective-permute-done.31.refs_5_), channel_id=1, source_target_pairs={{0,4},{8,0},{16,8},{24,16},{28,24},{20,28},{12,20},{4,12},{1,5},{9... | collective-permute-start | bytes 786440 | tf_op jit(solution)/shard_map/ppermute | solution.py:62
  107.9 3.5 %gradients_start.1 = (f32[1024,512]{1,0:T(8,128)S(1)}, f32[1024,512]{1,0:T(8,128)S(1)}) custom-call(s32[1]{0:T(128)} %bitcast.p_ref, bf16[1024,128]{1,0:T(8,128)(2,1)S(1)} %get-tuple-element.63.refs_0_, bf16[1024,128]{1,0:T(8,128)(2,1)S(1)} %get-tuple-element.73.refs_1_, bf16[1024,128]{1,0:T(8,128)(2,1)S(1)} %collective-permute-done.9.refs_2_, ...), custom_call_target="tpu_custom_call" | custom-call | tf_op jit(solution)/shard_map/gradients_start/pallas_call | solution.py:407
  111.5 0.5 collective-permute-start.42
  112.0 0.9 collective-permute-done.41.refs_16_.refs_34_.refs_14_
  113.1 0.8 sums.1
  114.2 3.6 %gradients_end.1 = (bf16[1024,512]{1,0:T(8,128)(2,1)}, bf16[1024,512]{1,0:T(8,128)(2,1)}) custom-call(s32[1]{0:T(128)} %bitcast.p_ref, f32[1024,512]{1,0:T(8,128)S(1)} %get-tuple-element.85.refs_0_, f32[1024,512]{1,0:T(8,128)S(1)} %get-tuple-element.86.refs_1_, bf16[1024,128]{1,0:T(8,128)(2,1)S(1)} %collective-permute-done.28.refs_2_, ...), custom_call_target="tpu_custom_call" | custom-call | flops 1610612736 | bytes 9928704 | tf_op jit(solution)/shard_map/gradients_end/pallas_call | solution.py:407
  117.7 1.8 %collective-permute-done.45.refs_1_ = bf16[256,256]{1,0:T(8,128)(2,1)S(1)} collective-permute-done((bf16[256,256]{1,0:T(8,128)(2,1)S(1)}, bf16[256,256]{1,0:T(8,128)(2,1)S(1)}, u32[]{:S(2)}, u32[]{:S(2)}) %collective-permute-start.45) | collective-permute-done | bytes 131104 | tf_op jit(solution)/shard_map/ppermute | solution.py:29
  119.6 0.7 join.1
  (64 shorter events, 2.5 us)
Async XLA Ops:
  2.4 3.1 %collective-permute-start = (bf16[272,1024]{1,0:T(8,128)(2,1)S(1)}, bf16[272,1024]{1,0:T(8,128)(2,1)S(1)}, u32[]{:S(2)}, u32[]{:S(2)}) collective-permute-start(bf16[272,1024]{1,0:T(8,128)(2,1)S(1)} %get-tuple-element.52.refs_0_), channel_id=1, source_target_pairs={{0,1},{1,0},{2,3},{3,2},{4,5},{5,4},{6,7},{7,6},{8,9},{9,8},{10,11... | collective-permute-start | bytes 1671176 | tf_op jit(solution)/shard_map/ppermute | solution.py:29
  2.9 15.8 %collective-permute-start.1 = (bf16[272,1024]{1,0:T(8,128)(2,1)S(1)}, bf16[272,1024]{1,0:T(8,128)(2,1)S(1)}, u32[]{:S(2)}, u32[]{:S(2)}) collective-permute-start(bf16[272,1024]{1,0:T(8,128)(2,1)S(1)} %get-tuple-element.52.refs_0_), channel_id=1, source_target_pairs={{0,2},{1,3},{2,0},{3,1},{4,6},{5,7},{6,4},{7,5},{8,10},{9,11},{10,... | collective-permute-start | bytes 1671176 | tf_op jit(solution)/shard_map/ppermute | solution.py:29
  18.7 2.0 %collective-permute-start.2 = (bf16[272,1024]{1,0:T(8,128)(2,1)S(1)}, bf16[272,1024]{1,0:T(8,128)(2,1)S(1)}, u32[]{:S(2)}, u32[]{:S(2)}) collective-permute-start(bf16[272,1024]{1,0:T(8,128)(2,1)S(1)} %collective-permute-done.1.refs_0_.refs_1_), channel_id=1, source_target_pairs={{0,1},{1,0},{2,3},{3,2},{4,5},{5,4},{6,7},{7,6},{8,9},{9,8},{10,11... | collective-permute-start | bytes 1671176 | tf_op jit(solution)/shard_map/ppermute | solution.py:29
  22.7 7.4 %copy-start = (bf16[2048,1024]{1,0:T(8,128)(2,1)S(1)}, bf16[2048,1024]{1,0:T(8,128)(2,1)}, u32[]{:S(2)}) copy-start(bf16[2048,1024]{1,0:T(8,128)(2,1)} %refs_2_.5) | copy-start | bytes 12582916
  22.7 5.6 %collective-permute-start.6 = (bf16[128,512]{1,0:T(8,128)(2,1)S(1)}, bf16[128,512]{1,0:T(8,128)(2,1)S(1)}, u32[]{:S(2)}, u32[]{:S(2)}) collective-permute-start(bf16[128,512]{1,0:T(8,128)(2,1)S(1)} %attend0.1.refs_0_), channel_id=1, source_target_pairs={{0,2},{1,3},{2,0},{3,1},{4,6},{5,7},{6,4},{7,5},{8,10},{9,11},{10,... | collective-permute-start | bytes 393224 | tf_op jit(solution)/shard_map/ppermute | solution.py:29
  24.5 5.5 %collective-permute-start.3 = (bf16[128,512]{1,0:T(8,128)(2,1)S(1)}, bf16[128,512]{1,0:T(8,128)(2,1)S(1)}, u32[]{:S(2)}, u32[]{:S(2)}) collective-permute-start(bf16[128,512]{1,0:T(8,128)(2,1)S(1)} %attend0.1.refs_0_), channel_id=1, source_target_pairs={{0,1},{1,0},{2,3},{3,2},{4,5},{5,4},{6,7},{7,6},{8,9},{9,8},{10,11... | collective-permute-start | bytes 393224 | tf_op jit(solution)/shard_map/ppermute | solution.py:29
  26.5 4.5 %copy-start.1 = (bf16[1024,512]{1,0:T(8,128)(2,1)S(1)}, bf16[1024,512]{1,0:T(8,128)(2,1)}, u32[]{:S(2)}) copy-start(bf16[1024,512]{1,0:T(8,128)(2,1)} %policy_ref.3) | copy-start | bytes 3145732
  26.5 4.5 %copy-start.2 = (bf16[1024,512]{1,0:T(8,128)(2,1)S(1)}, bf16[1024,512]{1,0:T(8,128)(2,1)}, u32[]{:S(2)}) copy-start(bf16[1024,512]{1,0:T(8,128)(2,1)} %value_ref.3) | copy-start | bytes 3145732
  26.5 4.5 %copy-start.4 = (f32[1024]{0:T(1024)S(1)}, f32[1024]{0:T(1024)}, u32[]{:S(2)}) copy-start(f32[1024]{0:T(1024)} %param.27) | copy-start | bytes 12292
  26.5 3.5 %collective-permute-start.4 = (bf16[128,512]{1,0:T(8,128)(2,1)S(1)}, bf16[128,512]{1,0:T(8,128)(2,1)S(1)}, u32[]{:S(2)}, u32[]{:S(2)}) collective-permute-start(bf16[128,512]{1,0:T(8,128)(2,1)S(1)} %attend1.1.refs_1_), channel_id=1, source_target_pairs={{0,1},{1,0},{2,3},{3,2},{4,5},{5,4},{6,7},{7,6},{8,9},{9,8},{10,11... | collective-permute-start | bytes 393224 | tf_op jit(solution)/shard_map/ppermute | solution.py:29
  28.3 2.7 %collective-permute-start.7 = (bf16[128,512]{1,0:T(8,128)(2,1)S(1)}, bf16[128,512]{1,0:T(8,128)(2,1)S(1)}, u32[]{:S(2)}, u32[]{:S(2)}) collective-permute-start(bf16[128,512]{1,0:T(8,128)(2,1)S(1)} %collective-permute-done.6.refs_0_), channel_id=1, source_target_pairs={{0,1},{1,0},{2,3},{3,2},{4,5},{5,4},{6,7},{7,6},{8,9},{9,8},{10,11... | collective-permute-start | bytes 393224 | tf_op jit(solution)/shard_map/ppermute | solution.py:29
  28.3 6.6 %collective-permute-start.5 = (bf16[128,512]{1,0:T(8,128)(2,1)S(1)}, bf16[128,512]{1,0:T(8,128)(2,1)S(1)}, u32[]{:S(2)}, u32[]{:S(2)}) collective-permute-start(bf16[128,512]{1,0:T(8,128)(2,1)S(1)} %attend1.1.refs_1_), channel_id=1, source_target_pairs={{0,2},{1,3},{2,0},{3,1},{4,6},{5,7},{6,4},{7,5},{8,10},{9,11},{10,... | collective-permute-start | bytes 393224 | tf_op jit(solution)/shard_map/ppermute | solution.py:29
  32.8 9.0 %collective-permute-start.9 = (bf16[1024,128]{1,0:T(8,128)(2,1)S(1)}, bf16[1024,128]{1,0:T(8,128)(2,1)S(1)}, u32[]{:S(2)}, u32[]{:S(2)}) collective-permute-start(bf16[1024,128]{1,0:T(8,128)(2,1)S(1)} %get-tuple-element.63.refs_0_), channel_id=1, source_target_pairs={{0,8},{8,16},{16,24},{24,28},{28,20},{20,12},{12,4},{4,0},{1,9},{9... | collective-permute-start | bytes 786440 | tf_op jit(solution)/shard_map/ppermute | solution.py:62
  34.4 8.7 %collective-permute-start.10 = (bf16[1024,128]{1,0:T(8,128)(2,1)S(1)}, bf16[1024,128]{1,0:T(8,128)(2,1)S(1)}, u32[]{:S(2)}, u32[]{:S(2)}) collective-permute-start(bf16[1024,128]{1,0:T(8,128)(2,1)S(1)} %get-tuple-element.63.refs_0_), channel_id=1, source_target_pairs={{0,4},{8,0},{16,8},{24,16},{28,24},{20,28},{12,20},{4,12},{1,5},{9... | collective-permute-start | bytes 786440 | tf_op jit(solution)/shard_map/ppermute | solution.py:62
  34.8 1.3 %collective-permute-start.8 = (bf16[128,512]{1,0:T(8,128)(2,1)S(1)}, bf16[128,512]{1,0:T(8,128)(2,1)S(1)}, u32[]{:S(2)}, u32[]{:S(2)}) collective-permute-start(bf16[128,512]{1,0:T(8,128)(2,1)S(1)} %collective-permute-done.5.refs_0_), channel_id=1, source_target_pairs={{0,1},{1,0},{2,3},{3,2},{4,5},{5,4},{6,7},{7,6},{8,9},{9,8},{10,11... | collective-permute-start | bytes 393224 | tf_op jit(solution)/shard_map/ppermute | solution.py:29
  36.2 14.9 %copy-start.7 = (bf16[512]{0:T(512)(128)(2,1)S(1)}, bf16[512]{0:T(512)(128)(2,1)}, u32[]{:S(2)}) copy-start(bf16[512]{0:T(512)(128)(2,1)} %param.31) | copy-start | bytes 3076
  36.2 24.1 %copy-start.3 = (bf16[512,256]{1,0:T(8,128)(2,1)S(1)}, bf16[512,256]{1,0:T(8,128)(2,1)}, u32[]{:S(2)}) copy-start(bf16[512,256]{1,0:T(8,128)(2,1)} %policy_out_ref.1) | copy-start | bytes 786436
  36.2 24.1 %copy-start.5 = (s32[256]{0:T(256)S(1)}, s32[256]{0:T(256)}, u32[]{:S(2)}) copy-start(s32[256]{0:T(256)} %param.32) | copy-start | bytes 3076
  36.2 24.1 %copy-start.6 = (f32[256]{0:T(256)S(1)}, f32[256]{0:T(256)}, u32[]{:S(2)}) copy-start(f32[256]{0:T(256)} %param.33) | copy-start | bytes 3076
  38.0 8.9 %collective-permute-start.15 = (bf16[1024,128]{1,0:T(8,128)(2,1)S(1)}, bf16[1024,128]{1,0:T(8,128)(2,1)S(1)}, u32[]{:S(2)}, u32[]{:S(2)}) collective-permute-start(bf16[1024,128]{1,0:T(8,128)(2,1)S(1)} %get-tuple-element.73.refs_1_), channel_id=1, source_target_pairs={{0,8},{8,16},{16,24},{24,28},{28,20},{20,12},{12,4},{4,0},{1,9},{9... | collective-permute-start | bytes 786440 | tf_op jit(solution)/shard_map/ppermute | solution.py:62
  39.5 9.3 %collective-permute-start.16 = (bf16[1024,128]{1,0:T(8,128)(2,1)S(1)}, bf16[1024,128]{1,0:T(8,128)(2,1)S(1)}, u32[]{:S(2)}, u32[]{:S(2)}) collective-permute-start(bf16[1024,128]{1,0:T(8,128)(2,1)S(1)} %get-tuple-element.73.refs_1_), channel_id=1, source_target_pairs={{0,4},{8,0},{16,8},{24,16},{28,24},{20,28},{12,20},{4,12},{1,5},{9... | collective-permute-start | bytes 786440 | tf_op jit(solution)/shard_map/ppermute | solution.py:62
  43.1 6.7 %collective-permute-start.11 = (bf16[256,512]{1,0:T(8,128)(2,1)S(1)}, bf16[256,512]{1,0:T(8,128)(2,1)S(1)}, u32[]{:S(2)}, u32[]{:S(2)}) collective-permute-start(bf16[256,512]{1,0:T(8,128)(2,1)S(1)} %get-tuple-element.72), channel_id=1, source_target_pairs={{0,1},{1,0},{2,3},{3,2},{4,5},{5,4},{6,7},{7,6},{8,9},{9,8},{10,11... | collective-permute-start | bytes 786440 | tf_op jit(solution)/shard_map/ppermute | solution.py:29
  43.1 1.5 %collective-permute-start.19 = (f32[8,256]{1,0:T(8,128)S(1)}, f32[8,256]{1,0:T(8,128)S(1)}, u32[]{:S(2)}, u32[]{:S(2)}) collective-permute-start(f32[8,256]{1,0:T(8,128)S(1)} %get-tuple-element.75), channel_id=1, source_target_pairs={{0,1},{1,0},{2,3},{3,2},{4,5},{5,4},{6,7},{7,6},{8,9},{9,8},{10,11... | collective-permute-start | bytes 24584 | tf_op jit(solution)/shard_map/ppermute | solution.py:29
  44.6 6.4 %collective-permute-start.20 = (f32[8,256]{1,0:T(8,128)S(1)}, f32[8,256]{1,0:T(8,128)S(1)}, u32[]{:S(2)}, u32[]{:S(2)}) collective-permute-start(f32[8,256]{1,0:T(8,128)S(1)} %add.14), channel_id=1, source_target_pairs={{0,2},{1,3},{2,0},{3,1},{4,6},{5,7},{6,4},{7,5},{8,10},{9,11},{10,... | collective-permute-start | bytes 24584 | tf_op jit(solution)/shard_map/ppermute | solution.py:29
  44.6 9.2 %collective-permute-start.13 = (bf16[1024,128]{1,0:T(8,128)(2,1)S(1)}, bf16[1024,128]{1,0:T(8,128)(2,1)S(1)}, u32[]{:S(2)}, u32[]{:S(2)}) collective-permute-start(bf16[1024,128]{1,0:T(8,128)(2,1)S(1)} %collective-permute-done.9.refs_2_), channel_id=1, source_target_pairs={{0,8},{8,16},{16,24},{24,28},{28,20},{20,12},{12,4},{4,0},{1,9},{9... | collective-permute-start | bytes 786440 | tf_op jit(solution)/shard_map/ppermute | solution.py:62
  46.9 9.2 %collective-permute-start.14 = (bf16[1024,128]{1,0:T(8,128)(2,1)S(1)}, bf16[1024,128]{1,0:T(8,128)(2,1)S(1)}, u32[]{:S(2)}, u32[]{:S(2)}) collective-permute-start(bf16[1024,128]{1,0:T(8,128)(2,1)S(1)} %collective-permute-done.10.refs_4_), channel_id=1, source_target_pairs={{0,4},{8,0},{16,8},{24,16},{28,24},{20,28},{12,20},{4,12},{1,5},{9... | collective-permute-start | bytes 786440 | tf_op jit(solution)/shard_map/ppermute | solution.py:62
  48.9 9.7 %collective-permute-start.17 = (bf16[1024,128]{1,0:T(8,128)(2,1)S(1)}, bf16[1024,128]{1,0:T(8,128)(2,1)S(1)}, u32[]{:S(2)}, u32[]{:S(2)}) collective-permute-start(bf16[1024,128]{1,0:T(8,128)(2,1)S(1)} %collective-permute-done.15.refs_3_), channel_id=1, source_target_pairs={{0,8},{8,16},{16,24},{24,28},{28,20},{20,12},{12,4},{4,0},{1,9},{9... | collective-permute-start | bytes 786440 | tf_op jit(solution)/shard_map/ppermute | solution.py:62
  49.8 10.6 %collective-permute-start.18 = (bf16[1024,128]{1,0:T(8,128)(2,1)S(1)}, bf16[1024,128]{1,0:T(8,128)(2,1)S(1)}, u32[]{:S(2)}, u32[]{:S(2)}) collective-permute-start(bf16[1024,128]{1,0:T(8,128)(2,1)S(1)} %collective-permute-done.16.refs_5_), channel_id=1, source_target_pairs={{0,4},{8,0},{16,8},{24,16},{28,24},{20,28},{12,20},{4,12},{1,5},{9... | collective-permute-start | bytes 786440 | tf_op jit(solution)/shard_map/ppermute | solution.py:62
  51.0 9.3 %collective-permute-start.12 = (bf16[256,512]{1,0:T(8,128)(2,1)S(1)}, bf16[256,512]{1,0:T(8,128)(2,1)S(1)}, u32[]{:S(2)}, u32[]{:S(2)}) collective-permute-start(bf16[256,512]{1,0:T(8,128)(2,1)S(1)} %add_convert_fusion.mine_ref), channel_id=1, source_target_pairs={{0,2},{1,3},{2,0},{3,1},{4,6},{5,7},{6,4},{7,5},{8,10},{9,11},{10,... | collective-permute-start | bytes 786440 | tf_op jit(solution)/shard_map/ppermute | solution.py:29
  61.5 1.3 %collective-permute-start.21 = (bf16[64,512]{1,0:T(8,128)(2,1)S(1)}, bf16[64,512]{1,0:T(8,128)(2,1)S(1)}, u32[]{:S(2)}, u32[]{:S(2)}) collective-permute-start(bf16[64,512]{1,0:T(8,128)(2,1)S(1)} %get-tuple-element.78), channel_id=1, source_target_pairs={{0,1},{1,0},{2,3},{3,2},{4,5},{5,4},{6,7},{7,6},{8,9},{9,8},{10,11... | collective-permute-start | bytes 196616 | tf_op jit(solution)/shard_map/ppermute | solution.py:29
  62.8 11.0 %collective-permute-start.22 = (bf16[336,512]{1,0:T(8,128)(2,1)S(1)}, bf16[336,512]{1,0:T(8,128)(2,1)S(1)}, u32[]{:S(2)}, u32[]{:S(2)}) collective-permute-start(bf16[336,512]{1,0:T(8,128)(2,1)S(1)} %select_dynamic-update-slice_fusion.refs_10_.refs_0_.refs_18_), channel_id=1, source_target_pairs={{0,8},{8,16},{16,24},{24,28},{28,20},{20,12},{12,4},{4,0},{1,9},{9... | collective-permute-start | bytes 1032200 | tf_op jit(solution)/shard_map/ppermute | solution.py:62
  64.5 10.9 %collective-permute-start.23 = (bf16[336,512]{1,0:T(8,128)(2,1)S(1)}, bf16[336,512]{1,0:T(8,128)(2,1)S(1)}, u32[]{:S(2)}, u32[]{:S(2)}) collective-permute-start(bf16[336,512]{1,0:T(8,128)(2,1)S(1)} %select_dynamic-update-slice_fusion.refs_10_.refs_0_.refs_18_), channel_id=1, source_target_pairs={{0,4},{8,0},{16,8},{24,16},{28,24},{20,28},{12,20},{4,12},{1,5},{9... | collective-permute-start | bytes 1032200 | tf_op jit(solution)/shard_map/ppermute | solution.py:62
  64.9 14.5 %collective-permute-start.28 = (bf16[1024,128]{1,0:T(8,128)(2,1)S(1)}, bf16[1024,128]{1,0:T(8,128)(2,1)S(1)}, u32[]{:S(2)}, u32[]{:S(2)}) collective-permute-start(bf16[1024,128]{1,0:T(8,128)(2,1)S(1)} %collective-permute-done.13.refs_6_), channel_id=1, source_target_pairs={{0,8},{8,16},{16,24},{24,28},{28,20},{20,12},{12,4},{4,0},{1,9},{9... | collective-permute-start | bytes 786440 | tf_op jit(solution)/shard_map/ppermute | solution.py:62
  66.5 14.5 %collective-permute-start.29 = (bf16[1024,128]{1,0:T(8,128)(2,1)S(1)}, bf16[1024,128]{1,0:T(8,128)(2,1)S(1)}, u32[]{:S(2)}, u32[]{:S(2)}) collective-permute-start(bf16[1024,128]{1,0:T(8,128)(2,1)S(1)} %collective-permute-done.14.refs_8_), channel_id=1, source_target_pairs={{0,4},{8,0},{16,8},{24,16},{28,24},{20,28},{12,20},{4,12},{1,5},{9... | collective-permute-start | bytes 786440 | tf_op jit(solution)/shard_map/ppermute | solution.py:62
  73.8 13.0 %collective-permute-start.24 = (bf16[336,512]{1,0:T(8,128)(2,1)S(1)}, bf16[336,512]{1,0:T(8,128)(2,1)S(1)}, u32[]{:S(2)}, u32[]{:S(2)}) collective-permute-start(bf16[336,512]{1,0:T(8,128)(2,1)S(1)} %collective-permute-done.22.refs_11_.refs_1_.refs_19_), channel_id=1, source_target_pairs={{0,8},{8,16},{16,24},{24,28},{28,20},{20,12},{12,4},{4,0},{1,9},{9... | collective-permute-start | bytes 1032200 | tf_op jit(solution)/shard_map/ppermute | solution.py:62
  75.4 13.0 %collective-permute-start.25 = (bf16[336,512]{1,0:T(8,128)(2,1)S(1)}, bf16[336,512]{1,0:T(8,128)(2,1)S(1)}, u32[]{:S(2)}, u32[]{:S(2)}) collective-permute-start(bf16[336,512]{1,0:T(8,128)(2,1)S(1)} %collective-permute-done.23.refs_12_.refs_2_.refs_20_), channel_id=1, source_target_pairs={{0,4},{8,0},{16,8},{24,16},{28,24},{20,28},{12,20},{4,12},{1,5},{9... | collective-permute-start | bytes 1032200 | tf_op jit(solution)/shard_map/ppermute | solution.py:62
  81.0 11.4 %collective-permute-start.30 = (bf16[1024,128]{1,0:T(8,128)(2,1)S(1)}, bf16[1024,128]{1,0:T(8,128)(2,1)S(1)}, u32[]{:S(2)}, u32[]{:S(2)}) collective-permute-start(bf16[1024,128]{1,0:T(8,128)(2,1)S(1)} %collective-permute-done.17.refs_7_), channel_id=1, source_target_pairs={{0,8},{8,16},{16,24},{24,28},{28,20},{20,12},{12,4},{4,0},{1,9},{9... | collective-permute-start | bytes 786440 | tf_op jit(solution)/shard_map/ppermute | solution.py:62
  82.6 11.3 %collective-permute-start.34 = (bf16[336,512]{1,0:T(8,128)(2,1)S(1)}, bf16[336,512]{1,0:T(8,128)(2,1)S(1)}, u32[]{:S(2)}, u32[]{:S(2)}) collective-permute-start(bf16[336,512]{1,0:T(8,128)(2,1)S(1)} %select_dynamic-update-slice_fusion.refs_10_.refs_0_.refs_18_), channel_id=1, source_target_pairs={{0,1},{1,0},{2,3},{3,2},{4,5},{5,4},{6,7},{7,6},{8,9},{9,8},{10,11... | collective-permute-start | bytes 1032200 | tf_op jit(solution)/shard_map/ppermute | solution.py:29
  82.6 11.3 %collective-permute-start.31 = (bf16[1024,128]{1,0:T(8,128)(2,1)S(1)}, bf16[1024,128]{1,0:T(8,128)(2,1)S(1)}, u32[]{:S(2)}, u32[]{:S(2)}) collective-permute-start(bf16[1024,128]{1,0:T(8,128)(2,1)S(1)} %collective-permute-done.18.refs_9_), channel_id=1, source_target_pairs={{0,4},{8,0},{16,8},{24,16},{28,24},{20,28},{12,20},{4,12},{1,5},{9... | collective-permute-start | bytes 786440 | tf_op jit(solution)/shard_map/ppermute | solution.py:62
  86.8 7.6 %collective-permute-start.35 = (bf16[336,512]{1,0:T(8,128)(2,1)S(1)}, bf16[336,512]{1,0:T(8,128)(2,1)S(1)}, u32[]{:S(2)}, u32[]{:S(2)}) collective-permute-start(bf16[336,512]{1,0:T(8,128)(2,1)S(1)} %collective-permute-done.22.refs_11_.refs_1_.refs_19_), channel_id=1, source_target_pairs={{0,1},{1,0},{2,3},{3,2},{4,5},{5,4},{6,7},{7,6},{8,9},{9,8},{10,11... | collective-permute-start | bytes 1032200 | tf_op jit(solution)/shard_map/ppermute | solution.py:29
  88.4 10.6 %collective-permute-start.26 = (bf16[336,512]{1,0:T(8,128)(2,1)S(1)}, bf16[336,512]{1,0:T(8,128)(2,1)S(1)}, u32[]{:S(2)}, u32[]{:S(2)}) collective-permute-start(bf16[336,512]{1,0:T(8,128)(2,1)S(1)} %collective-permute-done.24.refs_13_.refs_3_.refs_21_), channel_id=1, source_target_pairs={{0,8},{8,16},{16,24},{24,28},{28,20},{20,12},{12,4},{4,0},{1,9},{9... | collective-permute-start | bytes 1032200 | tf_op jit(solution)/shard_map/ppermute | solution.py:62
  92.4 8.5 %collective-permute-start.27 = (bf16[336,512]{1,0:T(8,128)(2,1)S(1)}, bf16[336,512]{1,0:T(8,128)(2,1)S(1)}, u32[]{:S(2)}, u32[]{:S(2)}) collective-permute-start(bf16[336,512]{1,0:T(8,128)(2,1)S(1)} %collective-permute-done.25.refs_14_.refs_4_.refs_22_), channel_id=1, source_target_pairs={{0,4},{8,0},{16,8},{24,16},{28,24},{20,28},{12,20},{4,12},{1,5},{9... | collective-permute-start | bytes 1032200 | tf_op jit(solution)/shard_map/ppermute | solution.py:62
  93.9 8.6 %collective-permute-start.36 = (bf16[336,512]{1,0:T(8,128)(2,1)S(1)}, bf16[336,512]{1,0:T(8,128)(2,1)S(1)}, u32[]{:S(2)}, u32[]{:S(2)}) collective-permute-start(bf16[336,512]{1,0:T(8,128)(2,1)S(1)} %collective-permute-done.23.refs_12_.refs_2_.refs_20_), channel_id=1, source_target_pairs={{0,1},{1,0},{2,3},{3,2},{4,5},{5,4},{6,7},{7,6},{8,9},{9,8},{10,11... | collective-permute-start | bytes 1032200 | tf_op jit(solution)/shard_map/ppermute | solution.py:29
  93.9 9.1 %collective-permute-start.37 = (bf16[336,512]{1,0:T(8,128)(2,1)S(1)}, bf16[336,512]{1,0:T(8,128)(2,1)S(1)}, u32[]{:S(2)}, u32[]{:S(2)}) collective-permute-start(bf16[336,512]{1,0:T(8,128)(2,1)S(1)} %collective-permute-done.24.refs_13_.refs_3_.refs_21_), channel_id=1, source_target_pairs={{0,1},{1,0},{2,3},{3,2},{4,5},{5,4},{6,7},{7,6},{8,9},{9,8},{10,11... | collective-permute-start | bytes 1032200 | tf_op jit(solution)/shard_map/ppermute | solution.py:29
  94.4 8.6 %collective-permute-start.38 = (bf16[336,512]{1,0:T(8,128)(2,1)S(1)}, bf16[336,512]{1,0:T(8,128)(2,1)S(1)}, u32[]{:S(2)}, u32[]{:S(2)}) collective-permute-start(bf16[336,512]{1,0:T(8,128)(2,1)S(1)} %collective-permute-done.25.refs_14_.refs_4_.refs_22_), channel_id=1, source_target_pairs={{0,1},{1,0},{2,3},{3,2},{4,5},{5,4},{6,7},{7,6},{8,9},{9,8},{10,11... | collective-permute-start | bytes 1032200 | tf_op jit(solution)/shard_map/ppermute | solution.py:29
  99.0 12.5 %collective-permute-start.39 = (bf16[336,512]{1,0:T(8,128)(2,1)S(1)}, bf16[336,512]{1,0:T(8,128)(2,1)S(1)}, u32[]{:S(2)}, u32[]{:S(2)}) collective-permute-start(bf16[336,512]{1,0:T(8,128)(2,1)S(1)} %collective-permute-done.26.refs_5_.refs_23_.refs_8_), channel_id=1, source_target_pairs={{0,1},{1,0},{2,3},{3,2},{4,5},{5,4},{6,7},{7,6},{8,9},{9,8},{10,11... | collective-permute-start | bytes 1032200 | tf_op jit(solution)/shard_map/ppermute | solution.py:29
  100.9 5.5 %collective-permute-start.32 = (bf16[336,256]{1,0:T(8,128)(2,1)S(1)}, bf16[336,256]{1,0:T(8,128)(2,1)S(1)}, u32[]{:S(2)}, u32[]{:S(2)}) collective-permute-start(bf16[336,256]{1,0:T(8,128)(2,1)S(1)} %slice.12), channel_id=1, source_target_pairs={{0,8},{8,16},{16,24},{24,28},{28,20},{20,12},{12,4},{4,0},{1,9},{9... | collective-permute-start | bytes 516104 | tf_op jit(solution)/shard_map/ppermute | solution.py:62
  102.5 8.9 %collective-permute-start.33 = (bf16[336,256]{1,0:T(8,128)(2,1)S(1)}, bf16[336,256]{1,0:T(8,128)(2,1)S(1)}, u32[]{:S(2)}, u32[]{:S(2)}) collective-permute-start(bf16[336,256]{1,0:T(8,128)(2,1)S(1)} %slice.13), channel_id=1, source_target_pairs={{0,4},{8,0},{16,8},{24,16},{28,24},{20,28},{12,20},{4,12},{1,5},{9... | collective-permute-start | bytes 516104 | tf_op jit(solution)/shard_map/ppermute | solution.py:62
  103.0 9.0 %collective-permute-start.40 = (bf16[336,512]{1,0:T(8,128)(2,1)S(1)}, bf16[336,512]{1,0:T(8,128)(2,1)S(1)}, u32[]{:S(2)}, u32[]{:S(2)}) collective-permute-start(bf16[336,512]{1,0:T(8,128)(2,1)S(1)} %collective-permute-done.27.refs_6_.refs_24_.refs_9_), channel_id=1, source_target_pairs={{0,1},{1,0},{2,3},{3,2},{4,5},{5,4},{6,7},{7,6},{8,9},{9,8},{10,11... | collective-permute-start | bytes 1032200 | tf_op jit(solution)/shard_map/ppermute | solution.py:29
  103.0 11.1 %collective-permute-start.43 = (bf16[1024,128]{1,0:T(8,128)(2,1)S(1)}, bf16[1024,128]{1,0:T(8,128)(2,1)S(1)}, u32[]{:S(2)}, u32[]{:S(2)}) collective-permute-start(bf16[1024,128]{1,0:T(8,128)(2,1)S(1)} %collective-permute-done.28.refs_2_), channel_id=1, source_target_pairs={{0,8},{8,16},{16,24},{24,28},{28,20},{20,12},{12,4},{4,0},{1,9},{9... | collective-permute-start | bytes 786440 | tf_op jit(solution)/shard_map/ppermute | solution.py:62
  106.4 7.7 %collective-permute-start.44 = (bf16[1024,128]{1,0:T(8,128)(2,1)S(1)}, bf16[1024,128]{1,0:T(8,128)(2,1)S(1)}, u32[]{:S(2)}, u32[]{:S(2)}) collective-permute-start(bf16[1024,128]{1,0:T(8,128)(2,1)S(1)} %collective-permute-done.31.refs_5_), channel_id=1, source_target_pairs={{0,4},{8,0},{16,8},{24,16},{28,24},{20,28},{12,20},{4,12},{1,5},{9... | collective-permute-start | bytes 786440 | tf_op jit(solution)/shard_map/ppermute | solution.py:62
  111.4 1.5 %collective-permute-start.41 = (bf16[336,256]{1,0:T(8,128)(2,1)S(1)}, bf16[336,256]{1,0:T(8,128)(2,1)S(1)}, u32[]{:S(2)}, u32[]{:S(2)}) collective-permute-start(bf16[336,256]{1,0:T(8,128)(2,1)S(1)} %collective-permute-done.32.refs_7_.refs_25_.refs_10_), channel_id=1, source_target_pairs={{0,1},{1,0},{2,3},{3,2},{4,5},{5,4},{6,7},{7,6},{8,9},{9,8},{10,11... | collective-permute-start | bytes 516104 | tf_op jit(solution)/shard_map/ppermute | solution.py:29
  111.5 1.6 %collective-permute-start.42 = (bf16[336,256]{1,0:T(8,128)(2,1)S(1)}, bf16[336,256]{1,0:T(8,128)(2,1)S(1)}, u32[]{:S(2)}, u32[]{:S(2)}) collective-permute-start(bf16[336,256]{1,0:T(8,128)(2,1)S(1)} %collective-permute-done.33.refs_8_.refs_26_.refs_11_), channel_id=1, source_target_pairs={{0,1},{1,0},{2,3},{3,2},{4,5},{5,4},{6,7},{7,6},{8,9},{9,8},{10,11... | collective-permute-start | bytes 516104 | tf_op jit(solution)/shard_map/ppermute | solution.py:29
  113.9 5.7 %collective-permute-start.45 = (bf16[256,256]{1,0:T(8,128)(2,1)S(1)}, bf16[256,256]{1,0:T(8,128)(2,1)S(1)}, u32[]{:S(2)}, u32[]{:S(2)}) collective-permute-start(bf16[256,256]{1,0:T(8,128)(2,1)S(1)} %get-tuple-element.94.refs_0_), channel_id=1, source_target_pairs={{0,2},{1,3},{2,0},{3,1},{4,6},{5,7},{6,4},{7,5},{8,10},{9,11},{10,... | collective-permute-start | bytes 393224 | tf_op jit(solution)/shard_map/ppermute | solution.py:29

commit v3 on v2

--- a/solution.py
+++ b/solution.py
@@ -654,7 +654,7 @@
         for way in range(len(shards[0][step])):
             turned_all += [shard[step][way] for shard in shards]
     payload_own = [payload, *(b for pair in payload_rounds[1:] for b in pair)]
-    split = wide_size - 3
+    split = wide_size - 1
     payload_other = [swap(b, 1) for b in payload_own[:split]]
 
     block = 256
@@ -684,7 +684,7 @@
         payload_own[:split], payload_other[:split], F32,
     )
     payload_other += [swap(b, 1) for b in payload_own[split:-2]]
-    payload_other += [swap(after(b, *starts), 1) for b in payload_own[-2:]]
+    payload_other += [swap(b, 1) for b in payload_own[-2:]]
 
     pieces = [*payload_own, *payload_other]
     share_shape = (4 * quarter, action_count)

time: 120 us -> 120 us (level)
  waiting for transfers between devices: 57.7 us -> 56.4 us
    ppermute x24, waiting for transfers between devices: 16.7 us -> 14.8 us  [swap(): return lax.ppermute(block, 'narrow', [(n, n ^ bit) for n in range(size)])]
where the time goes in v3:
time: 120 us
  waiting for transfers between devices  56.4 us (47%)
  starting transfers between devices  36.4 us (30%)
  Pallas kernels  26.4 us (22%)
    ppermute x22, waiting for transfers between devices, ring_step(): return lax.ppermute(block, 'wide', pairs)  41.5 us
    pallas_call x13, Pallas kernels, call(): pl.pallas_call(body, name=name, out_shape=outs, input_output_aliases=alia...  26.4 us
    ppermute x22, starting transfers between devices, ring_step(): return lax.ppermute(block, 'wide', pairs)  26 us
    ppermute x24, waiting for transfers between devices, swap(): return lax.ppermute(block, 'narrow', [(n, n ^ bit) for n in range(size)])  14.8 us
    ppermute x24, starting transfers between devices, swap(): return lax.ppermute(block, 'narrow', [(n, n ^ bit) for n in range(size)])  10.3 us
  transfers between devices with their start and end apart: 46, of which 25 were waited for; matrix products, arithmetic and copies ran while one was open for 0% of the time, Pallas kernels for 17%

profile of v3, /device:TPU:0, one launch (start us, length us, event | category | flops | bytes accessed | tf_op | source)
XLA Modules:
  0.0 120.2 jit_solution(421866466886741645)
XLA Ops:
  0.6 1.7 %embed.1 = (f32[256,1024]{1,0:T(8,128)S(1)}, bf16[272,1024]{1,0:T(8,128)(2,1)S(1)}) custom-call(s32[1]{0:T(128)} %bitcast.p_ref, bf16[256,1024]{1,0:T(8,128)(2,1)} %latent_ref.1, s32[1,256]{1,0:T(1,128)} %bitcast.12, bf16[256,1024]{1,0:T(8,128)(2,1)} %table_ref.1, f32[1,1024]{1,0:T(1,128)} %bitcast.11), custom_call_target="tpu_custom_call" | custom-call | flops 134217728 | bytes 2659328 | tf_op jit(solution)/shard_map/embed/pallas_call | solution.py:407
  2.4 0.5 collective-permute-start
  2.9 2.6 %collective-permute-start.1 = (bf16[272,1024]{1,0:T(8,128)(2,1)S(1)}, bf16[272,1024]{1,0:T(8,128)(2,1)S(1)}, u32[]{:S(2)}, u32[]{:S(2)}) collective-permute-start(bf16[272,1024]{1,0:T(8,128)(2,1)S(1)} %get-tuple-element.50.refs_0_), channel_id=1, source_target_pairs={{0,2},{1,3},{2,0},{3,1},{4,6},{5,7},{6,4},{7,5},{8,10},{9,11},{10,... | collective-permute-start | bytes 1671176 | tf_op jit(solution)/shard_map/ppermute | solution.py:29
  5.5 5.3 %begin.1 = (f32[256,1536]{1,0:T(8,128)S(1)}, bf16[1024,512]{1,0:T(8,128)(2,1)S(1)}, bf16[1024,512]{1,0:T(8,128)(2,1)S(1)}, bf16[1024,512]{1,0:T(8,128)(2,1)S(1)}...) custom-call(s32[1]{0:T(128)} %bitcast.p_ref, ...), custom_call_target="tpu_custom_call" | custom-call | flops 1610612736 | bytes 25755648 | tf_op jit(solution)/shard_map/begin/pallas_call | solution.py:407
  10.8 7.9 %collective-permute-done.1.refs_0_.refs_1_ = bf16[272,1024]{1,0:T(8,128)(2,1)S(1)} collective-permute-done((bf16[272,1024]{1,0:T(8,128)(2,1)S(1)}, bf16[272,1024]{1,0:T(8,128)(2,1)S(1)}, u32[]{:S(2)}, u32[]{:S(2)}) %collective-permute-start.1) | collective-permute-done | bytes 557088 | tf_op jit(solution)/shard_map/ppermute | solution.py:29
  18.7 1.0 project.1.acc_ref
  19.7 1.0 collective-permute-done.2.refs_3_.refs_4_
  20.6 2.0 %attend0.1.refs_0_ = bf16[128,512]{1,0:T(8,128)(2,1)S(1)} custom-call(s32[1]{0:T(128)} %bitcast.p_ref, f32[256,1536]{1,0:T(8,128)S(1)} %project.1.acc_ref, bf16[2,512,512]{2,1,0:T(8,128)(2,1)S(1)} %get-tuple-element.55.keys_ref, bf16[2,512,512]{2,1,0:T(8,128)(2,1)S(1)} %get-tuple-element.56.values_ref, bf16[272,1024]{1,0:T(8,128)(2,1)S(1)} %get-tuple-element.50.refs_0_, ...), custom_call_target="tpu_custom_call" | custom-call | tf_op jit(solution)/shard_map/attend0/pallas_call | solution.py:407
  22.7 1.8 %collective-permute-start.6 = (bf16[128,512]{1,0:T(8,128)(2,1)S(1)}, bf16[128,512]{1,0:T(8,128)(2,1)S(1)}, u32[]{:S(2)}, u32[]{:S(2)}) collective-permute-start(bf16[128,512]{1,0:T(8,128)(2,1)S(1)} %attend0.1.refs_0_), channel_id=1, source_target_pairs={{0,2},{1,3},{2,0},{3,1},{4,6},{5,7},{6,4},{7,5},{8,10},{9,11},{10,... | collective-permute-start | bytes 393224 | tf_op jit(solution)/shard_map/ppermute | solution.py:29
  24.5 2.0 %attend1.1.refs_1_ = bf16[128,512]{1,0:T(8,128)(2,1)S(1)} custom-call(s32[1]{0:T(128)} %bitcast.p_ref, f32[256,1536]{1,0:T(8,128)S(1)} %project.1.acc_ref, bf16[2,512,512]{2,1,0:T(8,128)(2,1)S(1)} %get-tuple-element.55.keys_ref, bf16[2,512,512]{2,1,0:T(8,128)(2,1)S(1)} %get-tuple-element.56.values_ref, bf16[272,1024]{1,0:T(8,128)(2,1)S(1)} %get-tuple-element.50.refs_0_, ...), custom_call_target="tpu_custom_call" | custom-call | tf_op jit(solution)/shard_map/attend1/pallas_call | solution.py:407
  26.5 0.6 collective-permute-start.4
  27.1 1.2 collective-permute-done.6.refs_0_
  28.3 1.7 %collective-permute-start.5 = (bf16[128,512]{1,0:T(8,128)(2,1)S(1)}, bf16[128,512]{1,0:T(8,128)(2,1)S(1)}, u32[]{:S(2)}, u32[]{:S(2)}) collective-permute-start(bf16[128,512]{1,0:T(8,128)(2,1)S(1)} %attend1.1.refs_1_), channel_id=1, source_target_pairs={{0,2},{1,3},{2,0},{3,1},{4,6},{5,7},{6,4},{7,5},{8,10},{9,11},{10,... | collective-permute-start | bytes 393224 | tf_op jit(solution)/shard_map/ppermute | solution.py:29
  30.0 1.0 update_near.1.acc_ref
  31.0 1.8 %update0.1 = (bf16[256,1024]{1,0:T(8,128)(2,1)}, f32[256,512]{1,0:T(8,128)S(1)}, bf16[256,512]{1,0:T(8,128)(2,1)S(1)}, f32[8,256]{1,0:T(8,128)S(1)}, bf16[1024,128]{1,0:T(8,128)(2,1)S(1)}) custom-call(s32[1]{0:T(128)} %bitcast.p_ref, f32[256,1024]{1,0:T(8,128)S(1)} %update_near.1.acc_ref, f32[1,1024]{1,0:T(1,128)S(1)} %bitcast.7, ...), custom_call_target="tpu_custom_call" | custom-call | flops 536870912 | bytes 9187328 | tf_op jit(solution)/shard_map/update0/pallas_call | solution.py:407
  32.8 1.6 %collective-permute-start.9 = (bf16[1024,128]{1,0:T(8,128)(2,1)S(1)}, bf16[1024,128]{1,0:T(8,128)(2,1)S(1)}, u32[]{:S(2)}, u32[]{:S(2)}) collective-permute-start(bf16[1024,128]{1,0:T(8,128)(2,1)S(1)} %get-tuple-element.61.refs_0_), channel_id=1, source_target_pairs={{0,8},{8,16},{16,24},{24,28},{28,20},{20,12},{12,4},{4,0},{1,9},{9... | collective-permute-start | bytes 786440 | tf_op jit(solution)/shard_map/ppermute | solution.py:62
  34.4 0.5 collective-permute-start.10
  34.8 1.3 %collective-permute-done.8.refs_1_ = bf16[128,512]{1,0:T(8,128)(2,1)S(1)} collective-permute-done((bf16[128,512]{1,0:T(8,128)(2,1)S(1)}, bf16[128,512]{1,0:T(8,128)(2,1)S(1)}, u32[]{:S(2)}, u32[]{:S(2)}) %collective-permute-start.8) | collective-permute-done | bytes 131104 | tf_op jit(solution)/shard_map/ppermute | solution.py:29
  36.2 1.8 %update1.1 = (bf16[256,1024]{1,0:T(8,128)(2,1)}, f32[256,512]{1,0:T(8,128)S(1)}, bf16[256,512]{1,0:T(8,128)(2,1)S(1)}, f32[8,256]{1,0:T(8,128)S(1)}, bf16[1024,128]{1,0:T(8,128)(2,1)S(1)}) custom-call(s32[1]{0:T(128)} %bitcast.p_ref, f32[256,1024]{1,0:T(8,128)S(1)} %update_near.1.acc_ref, ...), custom_call_target="tpu_custom_call", output_to_operand_aliasing={{0}: (8, {}), {1}: (9, {}), {2}: (10, {}), {3}: (11, {})} | custom-call | flops 536870912 | bytes 10506240 | tf_op jit(solution)/shard_map/update1/pallas_call | solution.py:407
  38.0 1.6 %collective-permute-start.15 = (bf16[1024,128]{1,0:T(8,128)(2,1)S(1)}, bf16[1024,128]{1,0:T(8,128)(2,1)S(1)}, u32[]{:S(2)}, u32[]{:S(2)}) collective-permute-start(bf16[1024,128]{1,0:T(8,128)(2,1)S(1)} %get-tuple-element.71.refs_1_), channel_id=1, source_target_pairs={{0,8},{8,16},{16,24},{24,28},{28,20},{20,12},{12,4},{4,0},{1,9},{9... | collective-permute-start | bytes 786440 | tf_op jit(solution)/shard_map/ppermute | solution.py:62
  40.0 1.8 %collective-permute-done.9.refs_2_ = bf16[1024,128]{1,0:T(8,128)(2,1)S(1)} collective-permute-done((bf16[1024,128]{1,0:T(8,128)(2,1)S(1)}, bf16[1024,128]{1,0:T(8,128)(2,1)S(1)}, u32[]{:S(2)}, u32[]{:S(2)}) %collective-permute-start.9) | collective-permute-done | bytes 262176 | tf_op jit(solution)/shard_map/ppermute | solution.py:62
  41.8 1.3 %collective-permute-done.10.refs_4_ = bf16[1024,128]{1,0:T(8,128)(2,1)S(1)} collective-permute-done((bf16[1024,128]{1,0:T(8,128)(2,1)S(1)}, bf16[1024,128]{1,0:T(8,128)(2,1)S(1)}, u32[]{:S(2)}, u32[]{:S(2)}) %collective-permute-start.10) | collective-permute-done | bytes 262176 | tf_op jit(solution)/shard_map/ppermute | solution.py:62
  43.1 0.5 collective-permute-start.19
  43.6 1.0 collective-permute-done.19
  44.6 1.6 %collective-permute-start.13 = (bf16[1024,128]{1,0:T(8,128)(2,1)S(1)}, bf16[1024,128]{1,0:T(8,128)(2,1)S(1)}, u32[]{:S(2)}, u32[]{:S(2)}) collective-permute-start(bf16[1024,128]{1,0:T(8,128)(2,1)S(1)} %collective-permute-done.9.refs_2_), channel_id=1, source_target_pairs={{0,8},{8,16},{16,24},{24,28},{28,20},{20,12},{12,4},{4,0},{1,9},{9... | collective-permute-start | bytes 786440 | tf_op jit(solution)/shard_map/ppermute | solution.py:62
  46.2 0.7 collective-permute-done.15.refs_3_
  46.9 2.0 %collective-permute-start.14 = (bf16[1024,128]{1,0:T(8,128)(2,1)S(1)}, bf16[1024,128]{1,0:T(8,128)(2,1)S(1)}, u32[]{:S(2)}, u32[]{:S(2)}) collective-permute-start(bf16[1024,128]{1,0:T(8,128)(2,1)S(1)} %collective-permute-done.10.refs_4_), channel_id=1, source_target_pairs={{0,4},{8,0},{16,8},{24,16},{28,24},{20,28},{12,20},{4,12},{1,5},{9... | collective-permute-start | bytes 786440 | tf_op jit(solution)/shard_map/ppermute | solution.py:62
  48.9 0.9 collective-permute-start.17
  49.8 1.1 collective-permute-start.18
  51.1 2.7 %collective-permute-done.13.refs_6_ = bf16[1024,128]{1,0:T(8,128)(2,1)S(1)} collective-permute-done((bf16[1024,128]{1,0:T(8,128)(2,1)S(1)}, bf16[1024,128]{1,0:T(8,128)(2,1)S(1)}, u32[]{:S(2)}, u32[]{:S(2)}) %collective-permute-start.13) | collective-permute-done | bytes 262176 | tf_op jit(solution)/shard_map/ppermute | solution.py:62
  53.8 2.3 %collective-permute-done.14.refs_8_ = bf16[1024,128]{1,0:T(8,128)(2,1)S(1)} collective-permute-done((bf16[1024,128]{1,0:T(8,128)(2,1)S(1)}, bf16[1024,128]{1,0:T(8,128)(2,1)S(1)}, u32[]{:S(2)}, u32[]{:S(2)}) %collective-permute-start.14) | collective-permute-done | bytes 262176 | tf_op jit(solution)/shard_map/ppermute | solution.py:62
  56.1 2.5 %collective-permute-done.17.refs_7_ = bf16[1024,128]{1,0:T(8,128)(2,1)S(1)} collective-permute-done((bf16[1024,128]{1,0:T(8,128)(2,1)S(1)}, bf16[1024,128]{1,0:T(8,128)(2,1)S(1)}, u32[]{:S(2)}, u32[]{:S(2)}) %collective-permute-start.17) | collective-permute-done | bytes 262176 | tf_op jit(solution)/shard_map/ppermute | solution.py:62
  58.6 1.8 %collective-permute-done.18.refs_9_ = bf16[1024,128]{1,0:T(8,128)(2,1)S(1)} collective-permute-done((bf16[1024,128]{1,0:T(8,128)(2,1)S(1)}, bf16[1024,128]{1,0:T(8,128)(2,1)S(1)}, u32[]{:S(2)}, u32[]{:S(2)}) %collective-permute-start.18) | collective-permute-done | bytes 262176 | tf_op jit(solution)/shard_map/ppermute | solution.py:62
  60.4 1.1 heads.1
  61.6 1.2 %collective-permute-done.21 = bf16[64,512]{1,0:T(8,128)(2,1)S(1)} collective-permute-done((bf16[64,512]{1,0:T(8,128)(2,1)S(1)}, bf16[64,512]{1,0:T(8,128)(2,1)S(1)}, u32[]{:S(2)}, u32[]{:S(2)}) %collective-permute-start.21) | collective-permute-done | bytes 65568 | tf_op jit(solution)/shard_map/ppermute | solution.py:29
  62.8 1.6 %collective-permute-start.22 = (bf16[336,512]{1,0:T(8,128)(2,1)S(1)}, bf16[336,512]{1,0:T(8,128)(2,1)S(1)}, u32[]{:S(2)}, u32[]{:S(2)}) collective-permute-start(bf16[336,512]{1,0:T(8,128)(2,1)S(1)} %select_dynamic-update-slice_fusion.refs_0_.refs_18_.refs_14_), channel_id=1, source_target_pairs={{0,8},{8,16},{16,24},{24,28},{28,20},{20,12},{12,4},{4,0},{1,9},{9... | collective-permute-start | bytes 1032200 | tf_op jit(solution)/shard_map/ppermute | solution.py:62
  64.5 0.5 collective-permute-start.23
  64.9 1.6 %collective-permute-start.28 = (bf16[1024,128]{1,0:T(8,128)(2,1)S(1)}, bf16[1024,128]{1,0:T(8,128)(2,1)S(1)}, u32[]{:S(2)}, u32[]{:S(2)}) collective-permute-start(bf16[1024,128]{1,0:T(8,128)(2,1)S(1)} %collective-permute-done.13.refs_6_), channel_id=1, source_target_pairs={{0,8},{8,16},{16,24},{24,28},{28,20},{20,12},{12,4},{4,0},{1,9},{9... | collective-permute-start | bytes 786440 | tf_op jit(solution)/shard_map/ppermute | solution.py:62
  66.9 6.9 %collective-permute-done.22.refs_1_.refs_19_.refs_15_ = bf16[336,512]{1,0:T(8,128)(2,1)S(1)} collective-permute-done((bf16[336,512]{1,0:T(8,128)(2,1)S(1)}, bf16[336,512]{1,0:T(8,128)(2,1)S(1)}, u32[]{:S(2)}, u32[]{:S(2)}) %collective-permute-start.22) | collective-permute-done | bytes 344096 | tf_op jit(solution)/shard_map/ppermute | solution.py:62
  73.8 1.6 %collective-permute-start.24 = (bf16[336,512]{1,0:T(8,128)(2,1)S(1)}, bf16[336,512]{1,0:T(8,128)(2,1)S(1)}, u32[]{:S(2)}, u32[]{:S(2)}) collective-permute-start(bf16[336,512]{1,0:T(8,128)(2,1)S(1)} %collective-permute-done.22.refs_1_.refs_19_.refs_15_), channel_id=1, source_target_pairs={{0,8},{8,16},{16,24},{24,28},{28,20},{20,12},{12,4},{4,0},{1,9},{9... | collective-permute-start | bytes 1032200 | tf_op jit(solution)/shard_map/ppermute | solution.py:62
  75.9 3.5 %collective-permute-done.28.refs_10_ = bf16[1024,128]{1,0:T(8,128)(2,1)S(1)} collective-permute-done((bf16[1024,128]{1,0:T(8,128)(2,1)S(1)}, bf16[1024,128]{1,0:T(8,128)(2,1)S(1)}, u32[]{:S(2)}, u32[]{:S(2)}) %collective-permute-start.28) | collective-permute-done | bytes 262176 | tf_op jit(solution)/shard_map/ppermute | solution.py:62
  79.4 1.6 %collective-permute-done.29.refs_12_ = bf16[1024,128]{1,0:T(8,128)(2,1)S(1)} collective-permute-done((bf16[1024,128]{1,0:T(8,128)(2,1)S(1)}, bf16[1024,128]{1,0:T(8,128)(2,1)S(1)}, u32[]{:S(2)}, u32[]{:S(2)}) %collective-permute-start.29) | collective-permute-done | bytes 262176 | tf_op jit(solution)/shard_map/ppermute | solution.py:62
  81.0 1.6 %collective-permute-start.30 = (bf16[1024,128]{1,0:T(8,128)(2,1)S(1)}, bf16[1024,128]{1,0:T(8,128)(2,1)S(1)}, u32[]{:S(2)}, u32[]{:S(2)}) collective-permute-start(bf16[1024,128]{1,0:T(8,128)(2,1)S(1)} %collective-permute-done.17.refs_7_), channel_id=1, source_target_pairs={{0,8},{8,16},{16,24},{24,28},{28,20},{20,12},{12,4},{4,0},{1,9},{9... | collective-permute-start | bytes 786440 | tf_op jit(solution)/shard_map/ppermute | solution.py:62
  83.1 3.7 %collective-permute-done.24.refs_3_.refs_21_.refs_17_ = bf16[336,512]{1,0:T(8,128)(2,1)S(1)} collective-permute-done((bf16[336,512]{1,0:T(8,128)(2,1)S(1)}, bf16[336,512]{1,0:T(8,128)(2,1)S(1)}, u32[]{:S(2)}, u32[]{:S(2)}) %collective-permute-start.24) | collective-permute-done | bytes 344096 | tf_op jit(solution)/shard_map/ppermute | solution.py:62
  86.8 1.6 %collective-permute-done.25.refs_4_.refs_22_.refs_18_ = bf16[336,512]{1,0:T(8,128)(2,1)S(1)} collective-permute-done((bf16[336,512]{1,0:T(8,128)(2,1)S(1)}, bf16[336,512]{1,0:T(8,128)(2,1)S(1)}, u32[]{:S(2)}, u32[]{:S(2)}) %collective-permute-start.25) | collective-permute-done | bytes 344096 | tf_op jit(solution)/shard_map/ppermute | solution.py:62
  88.4 1.6 %collective-permute-start.26 = (bf16[336,512]{1,0:T(8,128)(2,1)S(1)}, bf16[336,512]{1,0:T(8,128)(2,1)S(1)}, u32[]{:S(2)}, u32[]{:S(2)}) collective-permute-start(bf16[336,512]{1,0:T(8,128)(2,1)S(1)} %collective-permute-done.24.refs_3_.refs_21_.refs_17_), channel_id=1, source_target_pairs={{0,8},{8,16},{16,24},{24,28},{28,20},{20,12},{12,4},{4,0},{1,9},{9... | collective-permute-start | bytes 1032200 | tf_op jit(solution)/shard_map/ppermute | solution.py:62
  90.0 2.4 %collective-permute-done.30.refs_11_ = bf16[1024,128]{1,0:T(8,128)(2,1)S(1)} collective-permute-done((bf16[1024,128]{1,0:T(8,128)(2,1)S(1)}, bf16[1024,128]{1,0:T(8,128)(2,1)S(1)}, u32[]{:S(2)}, u32[]{:S(2)}) %collective-permute-start.30) | collective-permute-done | bytes 262176 | tf_op jit(solution)/shard_map/ppermute | solution.py:62
  92.4 1.5 %collective-permute-start.27 = (bf16[336,512]{1,0:T(8,128)(2,1)S(1)}, bf16[336,512]{1,0:T(8,128)(2,1)S(1)}, u32[]{:S(2)}, u32[]{:S(2)}) collective-permute-start(bf16[336,512]{1,0:T(8,128)(2,1)S(1)} %collective-permute-done.25.refs_4_.refs_22_.refs_18_), channel_id=1, source_target_pairs={{0,4},{8,0},{16,8},{24,16},{28,24},{20,28},{12,20},{4,12},{1,5},{9... | collective-permute-start | bytes 1032200 | tf_op jit(solution)/shard_map/ppermute | solution.py:62
  93.9 0.5 collective-permute-start.37
  94.5 4.5 %collective-permute-done.26.refs_5_.refs_23_.refs_19_ = bf16[336,512]{1,0:T(8,128)(2,1)S(1)} collective-permute-done((bf16[336,512]{1,0:T(8,128)(2,1)S(1)}, bf16[336,512]{1,0:T(8,128)(2,1)S(1)}, u32[]{:S(2)}, u32[]{:S(2)}) %collective-permute-start.26) | collective-permute-done | bytes 344096 | tf_op jit(solution)/shard_map/ppermute | solution.py:62
  99.0 1.9 %collective-permute-done.27.refs_6_.refs_24_.refs_20_ = bf16[336,512]{1,0:T(8,128)(2,1)S(1)} collective-permute-done((bf16[336,512]{1,0:T(8,128)(2,1)S(1)}, bf16[336,512]{1,0:T(8,128)(2,1)S(1)}, u32[]{:S(2)}, u32[]{:S(2)}) %collective-permute-start.27) | collective-permute-done | bytes 344096 | tf_op jit(solution)/shard_map/ppermute | solution.py:62
  100.9 1.6 %collective-permute-start.32 = (bf16[336,256]{1,0:T(8,128)(2,1)S(1)}, bf16[336,256]{1,0:T(8,128)(2,1)S(1)}, u32[]{:S(2)}, u32[]{:S(2)}) collective-permute-start(bf16[336,256]{1,0:T(8,128)(2,1)S(1)} %slice.12), channel_id=1, source_target_pairs={{0,8},{8,16},{16,24},{24,28},{28,20},{20,12},{12,4},{4,0},{1,9},{9... | collective-permute-start | bytes 516104 | tf_op jit(solution)/shard_map/ppermute | solution.py:62
  102.5 0.5 collective-permute-start.33
  103.0 1.6 %collective-permute-start.43 = (bf16[1024,128]{1,0:T(8,128)(2,1)S(1)}, bf16[1024,128]{1,0:T(8,128)(2,1)S(1)}, u32[]{:S(2)}, u32[]{:S(2)}) collective-permute-start(bf16[1024,128]{1,0:T(8,128)(2,1)S(1)} %collective-permute-done.28.refs_10_), channel_id=1, source_target_pairs={{0,8},{8,16},{16,24},{24,28},{28,20},{20,12},{12,4},{4,0},{1,9},{9... | collective-permute-start | bytes 786440 | tf_op jit(solution)/shard_map/ppermute | solution.py:62
  104.7 1.8 %collective-permute-done.32.refs_7_.refs_25_.refs_4_ = bf16[336,256]{1,0:T(8,128)(2,1)S(1)} collective-permute-done((bf16[336,256]{1,0:T(8,128)(2,1)S(1)}, bf16[336,256]{1,0:T(8,128)(2,1)S(1)}, u32[]{:S(2)}, u32[]{:S(2)}) %collective-permute-start.32) | collective-permute-done | bytes 172064 | tf_op jit(solution)/shard_map/ppermute | solution.py:62
  106.4 1.5 %collective-permute-start.44 = (bf16[1024,128]{1,0:T(8,128)(2,1)S(1)}, bf16[1024,128]{1,0:T(8,128)(2,1)S(1)}, u32[]{:S(2)}, u32[]{:S(2)}) collective-permute-start(bf16[1024,128]{1,0:T(8,128)(2,1)S(1)} %collective-permute-done.31.refs_13_), channel_id=1, source_target_pairs={{0,4},{8,0},{16,8},{24,16},{28,24},{20,28},{12,20},{4,12},{1,5},{9... | collective-permute-start | bytes 786440 | tf_op jit(solution)/shard_map/ppermute | solution.py:62
  107.9 0.5 collective-permute-done.33.refs_8_.refs_26_.refs_5_
  108.5 0.5 collective-permute-start.42
  109.0 0.9 collective-permute-done.41.refs_16_.refs_34_.refs_6_
  110.1 0.8 sums.1
  110.9 1.3 %collective-permute-start.45 = (bf16[256,256]{1,0:T(8,128)(2,1)S(1)}, bf16[256,256]{1,0:T(8,128)(2,1)S(1)}, u32[]{:S(2)}, u32[]{:S(2)}) collective-permute-start(bf16[256,256]{1,0:T(8,128)(2,1)S(1)} %get-tuple-element.90.refs_0_), channel_id=1, source_target_pairs={{0,2},{1,3},{2,0},{3,1},{4,6},{5,7},{6,4},{7,5},{8,10},{9,11},{10,... | collective-permute-start | bytes 393224 | tf_op jit(solution)/shard_map/ppermute | solution.py:29
  112.2 4.5 %gradients_start.1 = (f32[1024,512]{1,0:T(8,128)S(1)}, f32[1024,512]{1,0:T(8,128)S(1)}) custom-call(s32[1]{0:T(128)} %bitcast.p_ref, bf16[1024,128]{1,0:T(8,128)(2,1)S(1)} %get-tuple-element.61.refs_0_, bf16[1024,128]{1,0:T(8,128)(2,1)S(1)} %get-tuple-element.71.refs_1_, bf16[1024,128]{1,0:T(8,128)(2,1)S(1)} %collective-permute-done.9.refs_2_, ...), custom_call_target="tpu_custom_call" | custom-call | tf_op jit(solution)/shard_map/gradients_start/pallas_call | solution.py:407
  116.8 2.7 %gradients_end.1 = (bf16[1024,512]{1,0:T(8,128)(2,1)}, bf16[1024,512]{1,0:T(8,128)(2,1)}) custom-call(s32[1]{0:T(128)} %bitcast.p_ref, f32[1024,512]{1,0:T(8,128)S(1)} %get-tuple-element.84.refs_0_, f32[1024,512]{1,0:T(8,128)S(1)} %get-tuple-element.85.refs_1_, bf16[1024,128]{1,0:T(8,128)(2,1)S(1)} %collective-permute-done.43.refs_2_, ...), custom_call_target="tpu_custom_call" | custom-call | flops 536870912 | bytes 7503872 | tf_op jit(solution)/shard_map/gradients_end/pallas_call | solution.py:407
  119.5 0.7 join.1
  (64 shorter events, 2.6 us)
Async XLA Ops:
  2.4 3.1 %collective-permute-start = (bf16[272,1024]{1,0:T(8,128)(2,1)S(1)}, bf16[272,1024]{1,0:T(8,128)(2,1)S(1)}, u32[]{:S(2)}, u32[]{:S(2)}) collective-permute-start(bf16[272,1024]{1,0:T(8,128)(2,1)S(1)} %get-tuple-element.50.refs_0_), channel_id=1, source_target_pairs={{0,1},{1,0},{2,3},{3,2},{4,5},{5,4},{6,7},{7,6},{8,9},{9,8},{10,11... | collective-permute-start | bytes 1671176 | tf_op jit(solution)/shard_map/ppermute | solution.py:29
  2.9 15.8 %collective-permute-start.1 = (bf16[272,1024]{1,0:T(8,128)(2,1)S(1)}, bf16[272,1024]{1,0:T(8,128)(2,1)S(1)}, u32[]{:S(2)}, u32[]{:S(2)}) collective-permute-start(bf16[272,1024]{1,0:T(8,128)(2,1)S(1)} %get-tuple-element.50.refs_0_), channel_id=1, source_target_pairs={{0,2},{1,3},{2,0},{3,1},{4,6},{5,7},{6,4},{7,5},{8,10},{9,11},{10,... | collective-permute-start | bytes 1671176 | tf_op jit(solution)/shard_map/ppermute | solution.py:29
  18.7 2.0 %collective-permute-start.2 = (bf16[272,1024]{1,0:T(8,128)(2,1)S(1)}, bf16[272,1024]{1,0:T(8,128)(2,1)S(1)}, u32[]{:S(2)}, u32[]{:S(2)}) collective-permute-start(bf16[272,1024]{1,0:T(8,128)(2,1)S(1)} %collective-permute-done.1.refs_0_.refs_1_), channel_id=1, source_target_pairs={{0,1},{1,0},{2,3},{3,2},{4,5},{5,4},{6,7},{7,6},{8,9},{9,8},{10,11... | collective-permute-start | bytes 1671176 | tf_op jit(solution)/shard_map/ppermute | solution.py:29
  22.7 7.4 %copy-start = (bf16[2048,1024]{1,0:T(8,128)(2,1)S(1)}, bf16[2048,1024]{1,0:T(8,128)(2,1)}, u32[]{:S(2)}) copy-start(bf16[2048,1024]{1,0:T(8,128)(2,1)} %refs_2_.5) | copy-start | bytes 12582916
  22.7 5.6 %collective-permute-start.6 = (bf16[128,512]{1,0:T(8,128)(2,1)S(1)}, bf16[128,512]{1,0:T(8,128)(2,1)S(1)}, u32[]{:S(2)}, u32[]{:S(2)}) collective-permute-start(bf16[128,512]{1,0:T(8,128)(2,1)S(1)} %attend0.1.refs_0_), channel_id=1, source_target_pairs={{0,2},{1,3},{2,0},{3,1},{4,6},{5,7},{6,4},{7,5},{8,10},{9,11},{10,... | collective-permute-start | bytes 393224 | tf_op jit(solution)/shard_map/ppermute | solution.py:29
  24.5 5.5 %collective-permute-start.3 = (bf16[128,512]{1,0:T(8,128)(2,1)S(1)}, bf16[128,512]{1,0:T(8,128)(2,1)S(1)}, u32[]{:S(2)}, u32[]{:S(2)}) collective-permute-start(bf16[128,512]{1,0:T(8,128)(2,1)S(1)} %attend0.1.refs_0_), channel_id=1, source_target_pairs={{0,1},{1,0},{2,3},{3,2},{4,5},{5,4},{6,7},{7,6},{8,9},{9,8},{10,11... | collective-permute-start | bytes 393224 | tf_op jit(solution)/shard_map/ppermute | solution.py:29
  26.5 4.5 %copy-start.1 = (bf16[1024,512]{1,0:T(8,128)(2,1)S(1)}, bf16[1024,512]{1,0:T(8,128)(2,1)}, u32[]{:S(2)}) copy-start(bf16[1024,512]{1,0:T(8,128)(2,1)} %policy_ref.3) | copy-start | bytes 3145732
  26.5 4.5 %copy-start.2 = (bf16[1024,512]{1,0:T(8,128)(2,1)S(1)}, bf16[1024,512]{1,0:T(8,128)(2,1)}, u32[]{:S(2)}) copy-start(bf16[1024,512]{1,0:T(8,128)(2,1)} %value_ref.3) | copy-start | bytes 3145732
  26.5 4.5 %copy-start.4 = (f32[1024]{0:T(1024)S(1)}, f32[1024]{0:T(1024)}, u32[]{:S(2)}) copy-start(f32[1024]{0:T(1024)} %param.27) | copy-start | bytes 12292
  26.5 3.5 %collective-permute-start.4 = (bf16[128,512]{1,0:T(8,128)(2,1)S(1)}, bf16[128,512]{1,0:T(8,128)(2,1)S(1)}, u32[]{:S(2)}, u32[]{:S(2)}) collective-permute-start(bf16[128,512]{1,0:T(8,128)(2,1)S(1)} %attend1.1.refs_1_), channel_id=1, source_target_pairs={{0,1},{1,0},{2,3},{3,2},{4,5},{5,4},{6,7},{7,6},{8,9},{9,8},{10,11... | collective-permute-start | bytes 393224 | tf_op jit(solution)/shard_map/ppermute | solution.py:29
  28.3 2.7 %collective-permute-start.7 = (bf16[128,512]{1,0:T(8,128)(2,1)S(1)}, bf16[128,512]{1,0:T(8,128)(2,1)S(1)}, u32[]{:S(2)}, u32[]{:S(2)}) collective-permute-start(bf16[128,512]{1,0:T(8,128)(2,1)S(1)} %collective-permute-done.6.refs_0_), channel_id=1, source_target_pairs={{0,1},{1,0},{2,3},{3,2},{4,5},{5,4},{6,7},{7,6},{8,9},{9,8},{10,11... | collective-permute-start | bytes 393224 | tf_op jit(solution)/shard_map/ppermute | solution.py:29
  28.3 6.6 %collective-permute-start.5 = (bf16[128,512]{1,0:T(8,128)(2,1)S(1)}, bf16[128,512]{1,0:T(8,128)(2,1)S(1)}, u32[]{:S(2)}, u32[]{:S(2)}) collective-permute-start(bf16[128,512]{1,0:T(8,128)(2,1)S(1)} %attend1.1.refs_1_), channel_id=1, source_target_pairs={{0,2},{1,3},{2,0},{3,1},{4,6},{5,7},{6,4},{7,5},{8,10},{9,11},{10,... | collective-permute-start | bytes 393224 | tf_op jit(solution)/shard_map/ppermute | solution.py:29
  32.8 9.0 %collective-permute-start.9 = (bf16[1024,128]{1,0:T(8,128)(2,1)S(1)}, bf16[1024,128]{1,0:T(8,128)(2,1)S(1)}, u32[]{:S(2)}, u32[]{:S(2)}) collective-permute-start(bf16[1024,128]{1,0:T(8,128)(2,1)S(1)} %get-tuple-element.61.refs_0_), channel_id=1, source_target_pairs={{0,8},{8,16},{16,24},{24,28},{28,20},{20,12},{12,4},{4,0},{1,9},{9... | collective-permute-start | bytes 786440 | tf_op jit(solution)/shard_map/ppermute | solution.py:62
  34.4 8.7 %collective-permute-start.10 = (bf16[1024,128]{1,0:T(8,128)(2,1)S(1)}, bf16[1024,128]{1,0:T(8,128)(2,1)S(1)}, u32[]{:S(2)}, u32[]{:S(2)}) collective-permute-start(bf16[1024,128]{1,0:T(8,128)(2,1)S(1)} %get-tuple-element.61.refs_0_), channel_id=1, source_target_pairs={{0,4},{8,0},{16,8},{24,16},{28,24},{20,28},{12,20},{4,12},{1,5},{9... | collective-permute-start | bytes 786440 | tf_op jit(solution)/shard_map/ppermute | solution.py:62
  34.8 1.3 %collective-permute-start.8 = (bf16[128,512]{1,0:T(8,128)(2,1)S(1)}, bf16[128,512]{1,0:T(8,128)(2,1)S(1)}, u32[]{:S(2)}, u32[]{:S(2)}) collective-permute-start(bf16[128,512]{1,0:T(8,128)(2,1)S(1)} %collective-permute-done.5.refs_0_), channel_id=1, source_target_pairs={{0,1},{1,0},{2,3},{3,2},{4,5},{5,4},{6,7},{7,6},{8,9},{9,8},{10,11... | collective-permute-start | bytes 393224 | tf_op jit(solution)/shard_map/ppermute | solution.py:29
  36.2 14.9 %copy-start.7 = (bf16[512]{0:T(512)(128)(2,1)S(1)}, bf16[512]{0:T(512)(128)(2,1)}, u32[]{:S(2)}) copy-start(bf16[512]{0:T(512)(128)(2,1)} %param.31) | copy-start | bytes 3076
  36.2 24.1 %copy-start.3 = (bf16[512,256]{1,0:T(8,128)(2,1)S(1)}, bf16[512,256]{1,0:T(8,128)(2,1)}, u32[]{:S(2)}) copy-start(bf16[512,256]{1,0:T(8,128)(2,1)} %policy_out_ref.1) | copy-start | bytes 786436
  36.2 24.1 %copy-start.5 = (s32[256]{0:T(256)S(1)}, s32[256]{0:T(256)}, u32[]{:S(2)}) copy-start(s32[256]{0:T(256)} %param.32) | copy-start | bytes 3076
  36.2 24.1 %copy-start.6 = (f32[256]{0:T(256)S(1)}, f32[256]{0:T(256)}, u32[]{:S(2)}) copy-start(f32[256]{0:T(256)} %param.33) | copy-start | bytes 3076
  38.0 8.9 %collective-permute-start.15 = (bf16[1024,128]{1,0:T(8,128)(2,1)S(1)}, bf16[1024,128]{1,0:T(8,128)(2,1)S(1)}, u32[]{:S(2)}, u32[]{:S(2)}) collective-permute-start(bf16[1024,128]{1,0:T(8,128)(2,1)S(1)} %get-tuple-element.71.refs_1_), channel_id=1, source_target_pairs={{0,8},{8,16},{16,24},{24,28},{28,20},{20,12},{12,4},{4,0},{1,9},{9... | collective-permute-start | bytes 786440 | tf_op jit(solution)/shard_map/ppermute | solution.py:62
  39.5 9.3 %collective-permute-start.16 = (bf16[1024,128]{1,0:T(8,128)(2,1)S(1)}, bf16[1024,128]{1,0:T(8,128)(2,1)S(1)}, u32[]{:S(2)}, u32[]{:S(2)}) collective-permute-start(bf16[1024,128]{1,0:T(8,128)(2,1)S(1)} %get-tuple-element.71.refs_1_), channel_id=1, source_target_pairs={{0,4},{8,0},{16,8},{24,16},{28,24},{20,28},{12,20},{4,12},{1,5},{9... | collective-permute-start | bytes 786440 | tf_op jit(solution)/shard_map/ppermute | solution.py:62
  43.1 6.7 %collective-permute-start.11 = (bf16[256,512]{1,0:T(8,128)(2,1)S(1)}, bf16[256,512]{1,0:T(8,128)(2,1)S(1)}, u32[]{:S(2)}, u32[]{:S(2)}) collective-permute-start(bf16[256,512]{1,0:T(8,128)(2,1)S(1)} %get-tuple-element.70), channel_id=1, source_target_pairs={{0,1},{1,0},{2,3},{3,2},{4,5},{5,4},{6,7},{7,6},{8,9},{9,8},{10,11... | collective-permute-start | bytes 786440 | tf_op jit(solution)/shard_map/ppermute | solution.py:29
  43.1 1.5 %collective-permute-start.19 = (f32[8,256]{1,0:T(8,128)S(1)}, f32[8,256]{1,0:T(8,128)S(1)}, u32[]{:S(2)}, u32[]{:S(2)}) collective-permute-start(f32[8,256]{1,0:T(8,128)S(1)} %get-tuple-element.73), channel_id=1, source_target_pairs={{0,1},{1,0},{2,3},{3,2},{4,5},{5,4},{6,7},{7,6},{8,9},{9,8},{10,11... | collective-permute-start | bytes 24584 | tf_op jit(solution)/shard_map/ppermute | solution.py:29
  44.6 6.4 %collective-permute-start.20 = (f32[8,256]{1,0:T(8,128)S(1)}, f32[8,256]{1,0:T(8,128)S(1)}, u32[]{:S(2)}, u32[]{:S(2)}) collective-permute-start(f32[8,256]{1,0:T(8,128)S(1)} %add.14), channel_id=1, source_target_pairs={{0,2},{1,3},{2,0},{3,1},{4,6},{5,7},{6,4},{7,5},{8,10},{9,11},{10,... | collective-permute-start | bytes 24584 | tf_op jit(solution)/shard_map/ppermute | solution.py:29
  44.6 9.2 %collective-permute-start.13 = (bf16[1024,128]{1,0:T(8,128)(2,1)S(1)}, bf16[1024,128]{1,0:T(8,128)(2,1)S(1)}, u32[]{:S(2)}, u32[]{:S(2)}) collective-permute-start(bf16[1024,128]{1,0:T(8,128)(2,1)S(1)} %collective-permute-done.9.refs_2_), channel_id=1, source_target_pairs={{0,8},{8,16},{16,24},{24,28},{28,20},{20,12},{12,4},{4,0},{1,9},{9... | collective-permute-start | bytes 786440 | tf_op jit(solution)/shard_map/ppermute | solution.py:62
  46.9 9.2 %collective-permute-start.14 = (bf16[1024,128]{1,0:T(8,128)(2,1)S(1)}, bf16[1024,128]{1,0:T(8,128)(2,1)S(1)}, u32[]{:S(2)}, u32[]{:S(2)}) collective-permute-start(bf16[1024,128]{1,0:T(8,128)(2,1)S(1)} %collective-permute-done.10.refs_4_), channel_id=1, source_target_pairs={{0,4},{8,0},{16,8},{24,16},{28,24},{20,28},{12,20},{4,12},{1,5},{9... | collective-permute-start | bytes 786440 | tf_op jit(solution)/shard_map/ppermute | solution.py:62
  48.9 9.7 %collective-permute-start.17 = (bf16[1024,128]{1,0:T(8,128)(2,1)S(1)}, bf16[1024,128]{1,0:T(8,128)(2,1)S(1)}, u32[]{:S(2)}, u32[]{:S(2)}) collective-permute-start(bf16[1024,128]{1,0:T(8,128)(2,1)S(1)} %collective-permute-done.15.refs_3_), channel_id=1, source_target_pairs={{0,8},{8,16},{16,24},{24,28},{28,20},{20,12},{12,4},{4,0},{1,9},{9... | collective-permute-start | bytes 786440 | tf_op jit(solution)/shard_map/ppermute | solution.py:62
  49.8 10.6 %collective-permute-start.18 = (bf16[1024,128]{1,0:T(8,128)(2,1)S(1)}, bf16[1024,128]{1,0:T(8,128)(2,1)S(1)}, u32[]{:S(2)}, u32[]{:S(2)}) collective-permute-start(bf16[1024,128]{1,0:T(8,128)(2,1)S(1)} %collective-permute-done.16.refs_5_), channel_id=1, source_target_pairs={{0,4},{8,0},{16,8},{24,16},{28,24},{20,28},{12,20},{4,12},{1,5},{9... | collective-permute-start | bytes 786440 | tf_op jit(solution)/shard_map/ppermute | solution.py:62
  51.0 9.3 %collective-permute-start.12 = (bf16[256,512]{1,0:T(8,128)(2,1)S(1)}, bf16[256,512]{1,0:T(8,128)(2,1)S(1)}, u32[]{:S(2)}, u32[]{:S(2)}) collective-permute-start(bf16[256,512]{1,0:T(8,128)(2,1)S(1)} %add_convert_fusion.mine_ref), channel_id=1, source_target_pairs={{0,2},{1,3},{2,0},{3,1},{4,6},{5,7},{6,4},{7,5},{8,10},{9,11},{10,... | collective-permute-start | bytes 786440 | tf_op jit(solution)/shard_map/ppermute | solution.py:29
  61.5 1.3 %collective-permute-start.21 = (bf16[64,512]{1,0:T(8,128)(2,1)S(1)}, bf16[64,512]{1,0:T(8,128)(2,1)S(1)}, u32[]{:S(2)}, u32[]{:S(2)}) collective-permute-start(bf16[64,512]{1,0:T(8,128)(2,1)S(1)} %get-tuple-element.76), channel_id=1, source_target_pairs={{0,1},{1,0},{2,3},{3,2},{4,5},{5,4},{6,7},{7,6},{8,9},{9,8},{10,11... | collective-permute-start | bytes 196616 | tf_op jit(solution)/shard_map/ppermute | solution.py:29
  62.8 11.0 %collective-permute-start.22 = (bf16[336,512]{1,0:T(8,128)(2,1)S(1)}, bf16[336,512]{1,0:T(8,128)(2,1)S(1)}, u32[]{:S(2)}, u32[]{:S(2)}) collective-permute-start(bf16[336,512]{1,0:T(8,128)(2,1)S(1)} %select_dynamic-update-slice_fusion.refs_0_.refs_18_.refs_14_), channel_id=1, source_target_pairs={{0,8},{8,16},{16,24},{24,28},{28,20},{20,12},{12,4},{4,0},{1,9},{9... | collective-permute-start | bytes 1032200 | tf_op jit(solution)/shard_map/ppermute | solution.py:62
  64.5 10.9 %collective-permute-start.23 = (bf16[336,512]{1,0:T(8,128)(2,1)S(1)}, bf16[336,512]{1,0:T(8,128)(2,1)S(1)}, u32[]{:S(2)}, u32[]{:S(2)}) collective-permute-start(bf16[336,512]{1,0:T(8,128)(2,1)S(1)} %select_dynamic-update-slice_fusion.refs_0_.refs_18_.refs_14_), channel_id=1, source_target_pairs={{0,4},{8,0},{16,8},{24,16},{28,24},{20,28},{12,20},{4,12},{1,5},{9... | collective-permute-start | bytes 1032200 | tf_op jit(solution)/shard_map/ppermute | solution.py:62
  64.9 14.5 %collective-permute-start.28 = (bf16[1024,128]{1,0:T(8,128)(2,1)S(1)}, bf16[1024,128]{1,0:T(8,128)(2,1)S(1)}, u32[]{:S(2)}, u32[]{:S(2)}) collective-permute-start(bf16[1024,128]{1,0:T(8,128)(2,1)S(1)} %collective-permute-done.13.refs_6_), channel_id=1, source_target_pairs={{0,8},{8,16},{16,24},{24,28},{28,20},{20,12},{12,4},{4,0},{1,9},{9... | collective-permute-start | bytes 786440 | tf_op jit(solution)/shard_map/ppermute | solution.py:62
  66.5 14.5 %collective-permute-start.29 = (bf16[1024,128]{1,0:T(8,128)(2,1)S(1)}, bf16[1024,128]{1,0:T(8,128)(2,1)S(1)}, u32[]{:S(2)}, u32[]{:S(2)}) collective-permute-start(bf16[1024,128]{1,0:T(8,128)(2,1)S(1)} %collective-permute-done.14.refs_8_), channel_id=1, source_target_pairs={{0,4},{8,0},{16,8},{24,16},{28,24},{20,28},{12,20},{4,12},{1,5},{9... | collective-permute-start | bytes 786440 | tf_op jit(solution)/shard_map/ppermute | solution.py:62
  73.8 13.0 %collective-permute-start.24 = (bf16[336,512]{1,0:T(8,128)(2,1)S(1)}, bf16[336,512]{1,0:T(8,128)(2,1)S(1)}, u32[]{:S(2)}, u32[]{:S(2)}) collective-permute-start(bf16[336,512]{1,0:T(8,128)(2,1)S(1)} %collective-permute-done.22.refs_1_.refs_19_.refs_15_), channel_id=1, source_target_pairs={{0,8},{8,16},{16,24},{24,28},{28,20},{20,12},{12,4},{4,0},{1,9},{9... | collective-permute-start | bytes 1032200 | tf_op jit(solution)/shard_map/ppermute | solution.py:62
  75.4 13.0 %collective-permute-start.25 = (bf16[336,512]{1,0:T(8,128)(2,1)S(1)}, bf16[336,512]{1,0:T(8,128)(2,1)S(1)}, u32[]{:S(2)}, u32[]{:S(2)}) collective-permute-start(bf16[336,512]{1,0:T(8,128)(2,1)S(1)} %collective-permute-done.23.refs_2_.refs_20_.refs_16_), channel_id=1, source_target_pairs={{0,4},{8,0},{16,8},{24,16},{28,24},{20,28},{12,20},{4,12},{1,5},{9... | collective-permute-start | bytes 1032200 | tf_op jit(solution)/shard_map/ppermute | solution.py:62
  75.9 18.0 %collective-permute-start.34 = (bf16[336,512]{1,0:T(8,128)(2,1)S(1)}, bf16[336,512]{1,0:T(8,128)(2,1)S(1)}, u32[]{:S(2)}, u32[]{:S(2)}) collective-permute-start(bf16[336,512]{1,0:T(8,128)(2,1)S(1)} %select_dynamic-update-slice_fusion.refs_0_.refs_18_.refs_14_), channel_id=1, source_target_pairs={{0,1},{1,0},{2,3},{3,2},{4,5},{5,4},{6,7},{7,6},{8,9},{9,8},{10,11... | collective-permute-start | bytes 1032200 | tf_op jit(solution)/shard_map/ppermute | solution.py:29
  81.0 11.4 %collective-permute-start.30 = (bf16[1024,128]{1,0:T(8,128)(2,1)S(1)}, bf16[1024,128]{1,0:T(8,128)(2,1)S(1)}, u32[]{:S(2)}, u32[]{:S(2)}) collective-permute-start(bf16[1024,128]{1,0:T(8,128)(2,1)S(1)} %collective-permute-done.17.refs_7_), channel_id=1, source_target_pairs={{0,8},{8,16},{16,24},{24,28},{28,20},{20,12},{12,4},{4,0},{1,9},{9... | collective-permute-start | bytes 786440 | tf_op jit(solution)/shard_map/ppermute | solution.py:62
  82.6 11.3 %collective-permute-start.31 = (bf16[1024,128]{1,0:T(8,128)(2,1)S(1)}, bf16[1024,128]{1,0:T(8,128)(2,1)S(1)}, u32[]{:S(2)}, u32[]{:S(2)}) collective-permute-start(bf16[1024,128]{1,0:T(8,128)(2,1)S(1)} %collective-permute-done.18.refs_9_), channel_id=1, source_target_pairs={{0,4},{8,0},{16,8},{24,16},{28,24},{20,28},{12,20},{4,12},{1,5},{9... | collective-permute-start | bytes 786440 | tf_op jit(solution)/shard_map/ppermute | solution.py:62
  86.8 7.6 %collective-permute-start.35 = (bf16[336,512]{1,0:T(8,128)(2,1)S(1)}, bf16[336,512]{1,0:T(8,128)(2,1)S(1)}, u32[]{:S(2)}, u32[]{:S(2)}) collective-permute-start(bf16[336,512]{1,0:T(8,128)(2,1)S(1)} %collective-permute-done.22.refs_1_.refs_19_.refs_15_), channel_id=1, source_target_pairs={{0,1},{1,0},{2,3},{3,2},{4,5},{5,4},{6,7},{7,6},{8,9},{9,8},{10,11... | collective-permute-start | bytes 1032200 | tf_op jit(solution)/shard_map/ppermute | solution.py:29
  88.4 10.6 %collective-permute-start.26 = (bf16[336,512]{1,0:T(8,128)(2,1)S(1)}, bf16[336,512]{1,0:T(8,128)(2,1)S(1)}, u32[]{:S(2)}, u32[]{:S(2)}) collective-permute-start(bf16[336,512]{1,0:T(8,128)(2,1)S(1)} %collective-permute-done.24.refs_3_.refs_21_.refs_17_), channel_id=1, source_target_pairs={{0,8},{8,16},{16,24},{24,28},{28,20},{20,12},{12,4},{4,0},{1,9},{9... | collective-permute-start | bytes 1032200 | tf_op jit(solution)/shard_map/ppermute | solution.py:62
  92.4 8.5 %collective-permute-start.27 = (bf16[336,512]{1,0:T(8,128)(2,1)S(1)}, bf16[336,512]{1,0:T(8,128)(2,1)S(1)}, u32[]{:S(2)}, u32[]{:S(2)}) collective-permute-start(bf16[336,512]{1,0:T(8,128)(2,1)S(1)} %collective-permute-done.25.refs_4_.refs_22_.refs_18_), channel_id=1, source_target_pairs={{0,4},{8,0},{16,8},{24,16},{28,24},{20,28},{12,20},{4,12},{1,5},{9... | collective-permute-start | bytes 1032200 | tf_op jit(solution)/shard_map/ppermute | solution.py:62
  93.9 8.6 %collective-permute-start.36 = (bf16[336,512]{1,0:T(8,128)(2,1)S(1)}, bf16[336,512]{1,0:T(8,128)(2,1)S(1)}, u32[]{:S(2)}, u32[]{:S(2)}) collective-permute-start(bf16[336,512]{1,0:T(8,128)(2,1)S(1)} %collective-permute-done.23.refs_2_.refs_20_.refs_16_), channel_id=1, source_target_pairs={{0,1},{1,0},{2,3},{3,2},{4,5},{5,4},{6,7},{7,6},{8,9},{9,8},{10,11... | collective-permute-start | bytes 1032200 | tf_op jit(solution)/shard_map/ppermute | solution.py:29
  93.9 9.1 %collective-permute-start.37 = (bf16[336,512]{1,0:T(8,128)(2,1)S(1)}, bf16[336,512]{1,0:T(8,128)(2,1)S(1)}, u32[]{:S(2)}, u32[]{:S(2)}) collective-permute-start(bf16[336,512]{1,0:T(8,128)(2,1)S(1)} %collective-permute-done.24.refs_3_.refs_21_.refs_17_), channel_id=1, source_target_pairs={{0,1},{1,0},{2,3},{3,2},{4,5},{5,4},{6,7},{7,6},{8,9},{9,8},{10,11... | collective-permute-start | bytes 1032200 | tf_op jit(solution)/shard_map/ppermute | solution.py:29
  94.4 8.6 %collective-permute-start.38 = (bf16[336,512]{1,0:T(8,128)(2,1)S(1)}, bf16[336,512]{1,0:T(8,128)(2,1)S(1)}, u32[]{:S(2)}, u32[]{:S(2)}) collective-permute-start(bf16[336,512]{1,0:T(8,128)(2,1)S(1)} %collective-permute-done.25.refs_4_.refs_22_.refs_18_), channel_id=1, source_target_pairs={{0,1},{1,0},{2,3},{3,2},{4,5},{5,4},{6,7},{7,6},{8,9},{9,8},{10,11... | collective-permute-start | bytes 1032200 | tf_op jit(solution)/shard_map/ppermute | solution.py:29
  99.0 9.5 %collective-permute-start.39 = (bf16[336,512]{1,0:T(8,128)(2,1)S(1)}, bf16[336,512]{1,0:T(8,128)(2,1)S(1)}, u32[]{:S(2)}, u32[]{:S(2)}) collective-permute-start(bf16[336,512]{1,0:T(8,128)(2,1)S(1)} %collective-permute-done.26.refs_5_.refs_23_.refs_19_), channel_id=1, source_target_pairs={{0,1},{1,0},{2,3},{3,2},{4,5},{5,4},{6,7},{7,6},{8,9},{9,8},{10,11... | collective-permute-start | bytes 1032200 | tf_op jit(solution)/shard_map/ppermute | solution.py:29
  100.9 5.5 %collective-permute-start.32 = (bf16[336,256]{1,0:T(8,128)(2,1)S(1)}, bf16[336,256]{1,0:T(8,128)(2,1)S(1)}, u32[]{:S(2)}, u32[]{:S(2)}) collective-permute-start(bf16[336,256]{1,0:T(8,128)(2,1)S(1)} %slice.12), channel_id=1, source_target_pairs={{0,8},{8,16},{16,24},{24,28},{28,20},{20,12},{12,4},{4,0},{1,9},{9... | collective-permute-start | bytes 516104 | tf_op jit(solution)/shard_map/ppermute | solution.py:62
  102.5 6.0 %collective-permute-start.33 = (bf16[336,256]{1,0:T(8,128)(2,1)S(1)}, bf16[336,256]{1,0:T(8,128)(2,1)S(1)}, u32[]{:S(2)}, u32[]{:S(2)}) collective-permute-start(bf16[336,256]{1,0:T(8,128)(2,1)S(1)} %slice.13), channel_id=1, source_target_pairs={{0,4},{8,0},{16,8},{24,16},{28,24},{20,28},{12,20},{4,12},{1,5},{9... | collective-permute-start | bytes 516104 | tf_op jit(solution)/shard_map/ppermute | solution.py:62
  103.0 6.0 %collective-permute-start.40 = (bf16[336,512]{1,0:T(8,128)(2,1)S(1)}, bf16[336,512]{1,0:T(8,128)(2,1)S(1)}, u32[]{:S(2)}, u32[]{:S(2)}) collective-permute-start(bf16[336,512]{1,0:T(8,128)(2,1)S(1)} %collective-permute-done.27.refs_6_.refs_24_.refs_20_), channel_id=1, source_target_pairs={{0,1},{1,0},{2,3},{3,2},{4,5},{5,4},{6,7},{7,6},{8,9},{9,8},{10,11... | collective-permute-start | bytes 1032200 | tf_op jit(solution)/shard_map/ppermute | solution.py:29
  103.0 13.7 %collective-permute-start.43 = (bf16[1024,128]{1,0:T(8,128)(2,1)S(1)}, bf16[1024,128]{1,0:T(8,128)(2,1)S(1)}, u32[]{:S(2)}, u32[]{:S(2)}) collective-permute-start(bf16[1024,128]{1,0:T(8,128)(2,1)S(1)} %collective-permute-done.28.refs_10_), channel_id=1, source_target_pairs={{0,8},{8,16},{16,24},{24,28},{28,20},{20,12},{12,4},{4,0},{1,9},{9... | collective-permute-start | bytes 786440 | tf_op jit(solution)/shard_map/ppermute | solution.py:62
  106.4 10.3 %collective-permute-start.44 = (bf16[1024,128]{1,0:T(8,128)(2,1)S(1)}, bf16[1024,128]{1,0:T(8,128)(2,1)S(1)}, u32[]{:S(2)}, u32[]{:S(2)}) collective-permute-start(bf16[1024,128]{1,0:T(8,128)(2,1)S(1)} %collective-permute-done.31.refs_13_), channel_id=1, source_target_pairs={{0,4},{8,0},{16,8},{24,16},{28,24},{20,28},{12,20},{4,12},{1,5},{9... | collective-permute-start | bytes 786440 | tf_op jit(solution)/shard_map/ppermute | solution.py:62
  108.5 1.4 %collective-permute-start.41 = (bf16[336,256]{1,0:T(8,128)(2,1)S(1)}, bf16[336,256]{1,0:T(8,128)(2,1)S(1)}, u32[]{:S(2)}, u32[]{:S(2)}) collective-permute-start(bf16[336,256]{1,0:T(8,128)(2,1)S(1)} %collective-permute-done.32.refs_7_.refs_25_.refs_4_), channel_id=1, source_target_pairs={{0,1},{1,0},{2,3},{3,2},{4,5},{5,4},{6,7},{7,6},{8,9},{9,8},{10,11... | collective-permute-start | bytes 516104 | tf_op jit(solution)/shard_map/ppermute | solution.py:29
  108.5 1.6 %collective-permute-start.42 = (bf16[336,256]{1,0:T(8,128)(2,1)S(1)}, bf16[336,256]{1,0:T(8,128)(2,1)S(1)}, u32[]{:S(2)}, u32[]{:S(2)}) collective-permute-start(bf16[336,256]{1,0:T(8,128)(2,1)S(1)} %collective-permute-done.33.refs_8_.refs_26_.refs_5_), channel_id=1, source_target_pairs={{0,1},{1,0},{2,3},{3,2},{4,5},{5,4},{6,7},{7,6},{8,9},{9,8},{10,11... | collective-permute-start | bytes 516104 | tf_op jit(solution)/shard_map/ppermute | solution.py:29
  110.9 8.6 %collective-permute-start.45 = (bf16[256,256]{1,0:T(8,128)(2,1)S(1)}, bf16[256,256]{1,0:T(8,128)(2,1)S(1)}, u32[]{:S(2)}, u32[]{:S(2)}) collective-permute-start(bf16[256,256]{1,0:T(8,128)(2,1)S(1)} %get-tuple-element.90.refs_0_), channel_id=1, source_target_pairs={{0,2},{1,3},{2,0},{3,1},{4,6},{5,7},{6,4},{7,5},{8,10},{9,11},{10,... | collective-permute-start | bytes 393224 | tf_op jit(solution)/shard_map/ppermute | solution.py:29

commit v4 on v3

--- a/solution.py
+++ b/solution.py
@@ -657,7 +657,7 @@
     split = wide_size - 1
     payload_other = [swap(b, 1) for b in payload_own[:split]]
 
-    block = 256
+    block = 512
     grad_spec = pl.BlockSpec((block, hidden_count), lambda i, p: (i, 0))
     grad_flops = 4 * rows * width * hidden_count
 
@@ -676,7 +676,7 @@
                 ],
             ],
             [jax.ShapeDtypeStruct((width, hidden_count), dtype)] * 2, [grad_spec] * 2,
-            grad_flops * count, 18 * MIB,
+            grad_flops * count, 26 * MIB,
         )
 
     starts = gradient(

time: 120 us -> 119 us (level)
  no operation moved by 1% of the time
where the time goes in v4:
time: 119 us
  waiting for transfers between devices  56.3 us (47%)
  starting transfers between devices  36.4 us (31%)
  Pallas kernels  25.5 us (21%)
    ppermute x22, waiting for transfers between devices, ring_step(): return lax.ppermute(block, 'wide', pairs)  41.5 us
    ppermute x22, starting transfers between devices, ring_step(): return lax.ppermute(block, 'wide', pairs)  26.1 us
    pallas_call x13, Pallas kernels, call(): pl.pallas_call(body, name=name, out_shape=outs, input_output_aliases=alia...  25.5 us
    ppermute x24, waiting for transfers between devices, swap(): return lax.ppermute(block, 'narrow', [(n, n ^ bit) for n in range(size)])  14.8 us
    ppermute x24, starting transfers between devices, swap(): return lax.ppermute(block, 'narrow', [(n, n ^ bit) for n in range(size)])  10.3 us
  transfers between devices with their start and end apart: 46, of which 25 were waited for; matrix products, arithmetic and copies ran while one was open for 0% of the time, Pallas kernels for 17%

profile of v4, /device:TPU:0, one launch (start us, length us, event | category | flops | bytes accessed | tf_op | source)
XLA Modules:
  0.0 119.3 jit_solution(7262323791162890399)
XLA Ops:
  0.6 1.7 %embed.1 = (f32[256,1024]{1,0:T(8,128)S(1)}, bf16[272,1024]{1,0:T(8,128)(2,1)S(1)}) custom-call(s32[1]{0:T(128)} %bitcast.p_ref, bf16[256,1024]{1,0:T(8,128)(2,1)} %latent_ref.1, s32[1,256]{1,0:T(1,128)} %bitcast.12, bf16[256,1024]{1,0:T(8,128)(2,1)} %table_ref.1, f32[1,1024]{1,0:T(1,128)} %bitcast.11), custom_call_target="tpu_custom_call" | custom-call | flops 134217728 | bytes 2659328 | tf_op jit(solution)/shard_map/embed/pallas_call | solution.py:407
  2.4 0.5 collective-permute-start
  2.9 2.6 %collective-permute-start.1 = (bf16[272,1024]{1,0:T(8,128)(2,1)S(1)}, bf16[272,1024]{1,0:T(8,128)(2,1)S(1)}, u32[]{:S(2)}, u32[]{:S(2)}) collective-permute-start(bf16[272,1024]{1,0:T(8,128)(2,1)S(1)} %get-tuple-element.50.refs_0_), channel_id=1, source_target_pairs={{0,2},{1,3},{2,0},{3,1},{4,6},{5,7},{6,4},{7,5},{8,10},{9,11},{10,... | collective-permute-start | bytes 1671176 | tf_op jit(solution)/shard_map/ppermute | solution.py:29
  5.5 5.3 %begin.1 = (f32[256,1536]{1,0:T(8,128)S(1)}, bf16[1024,512]{1,0:T(8,128)(2,1)S(1)}, bf16[1024,512]{1,0:T(8,128)(2,1)S(1)}, bf16[1024,512]{1,0:T(8,128)(2,1)S(1)}...) custom-call(s32[1]{0:T(128)} %bitcast.p_ref, ...), custom_call_target="tpu_custom_call" | custom-call | flops 1610612736 | bytes 25755648 | tf_op jit(solution)/shard_map/begin/pallas_call | solution.py:407
  10.8 7.9 %collective-permute-done.1.refs_0_.refs_1_ = bf16[272,1024]{1,0:T(8,128)(2,1)S(1)} collective-permute-done((bf16[272,1024]{1,0:T(8,128)(2,1)S(1)}, bf16[272,1024]{1,0:T(8,128)(2,1)S(1)}, u32[]{:S(2)}, u32[]{:S(2)}) %collective-permute-start.1) | collective-permute-done | bytes 557088 | tf_op jit(solution)/shard_map/ppermute | solution.py:29
  18.7 1.0 project.1.acc_ref
  19.7 1.0 collective-permute-done.2.refs_3_.refs_4_
  20.6 2.0 %attend0.1.refs_0_ = bf16[128,512]{1,0:T(8,128)(2,1)S(1)} custom-call(s32[1]{0:T(128)} %bitcast.p_ref, f32[256,1536]{1,0:T(8,128)S(1)} %project.1.acc_ref, bf16[2,512,512]{2,1,0:T(8,128)(2,1)S(1)} %get-tuple-element.55.keys_ref, bf16[2,512,512]{2,1,0:T(8,128)(2,1)S(1)} %get-tuple-element.56.values_ref, bf16[272,1024]{1,0:T(8,128)(2,1)S(1)} %get-tuple-element.50.refs_0_, ...), custom_call_target="tpu_custom_call" | custom-call | tf_op jit(solution)/shard_map/attend0/pallas_call | solution.py:407
  22.7 1.8 %collective-permute-start.6 = (bf16[128,512]{1,0:T(8,128)(2,1)S(1)}, bf16[128,512]{1,0:T(8,128)(2,1)S(1)}, u32[]{:S(2)}, u32[]{:S(2)}) collective-permute-start(bf16[128,512]{1,0:T(8,128)(2,1)S(1)} %attend0.1.refs_0_), channel_id=1, source_target_pairs={{0,2},{1,3},{2,0},{3,1},{4,6},{5,7},{6,4},{7,5},{8,10},{9,11},{10,... | collective-permute-start | bytes 393224 | tf_op jit(solution)/shard_map/ppermute | solution.py:29
  24.5 2.0 %attend1.1.refs_1_ = bf16[128,512]{1,0:T(8,128)(2,1)S(1)} custom-call(s32[1]{0:T(128)} %bitcast.p_ref, f32[256,1536]{1,0:T(8,128)S(1)} %project.1.acc_ref, bf16[2,512,512]{2,1,0:T(8,128)(2,1)S(1)} %get-tuple-element.55.keys_ref, bf16[2,512,512]{2,1,0:T(8,128)(2,1)S(1)} %get-tuple-element.56.values_ref, bf16[272,1024]{1,0:T(8,128)(2,1)S(1)} %get-tuple-element.50.refs_0_, ...), custom_call_target="tpu_custom_call" | custom-call | tf_op jit(solution)/shard_map/attend1/pallas_call | solution.py:407
  26.5 0.6 collective-permute-start.4
  27.1 1.2 collective-permute-done.6.refs_0_
  28.3 1.7 %collective-permute-start.5 = (bf16[128,512]{1,0:T(8,128)(2,1)S(1)}, bf16[128,512]{1,0:T(8,128)(2,1)S(1)}, u32[]{:S(2)}, u32[]{:S(2)}) collective-permute-start(bf16[128,512]{1,0:T(8,128)(2,1)S(1)} %attend1.1.refs_1_), channel_id=1, source_target_pairs={{0,2},{1,3},{2,0},{3,1},{4,6},{5,7},{6,4},{7,5},{8,10},{9,11},{10,... | collective-permute-start | bytes 393224 | tf_op jit(solution)/shard_map/ppermute | solution.py:29
  30.0 1.0 update_near.1.acc_ref
  31.0 1.8 %update0.1 = (bf16[256,1024]{1,0:T(8,128)(2,1)}, f32[256,512]{1,0:T(8,128)S(1)}, bf16[256,512]{1,0:T(8,128)(2,1)S(1)}, f32[8,256]{1,0:T(8,128)S(1)}, bf16[1024,128]{1,0:T(8,128)(2,1)S(1)}) custom-call(s32[1]{0:T(128)} %bitcast.p_ref, f32[256,1024]{1,0:T(8,128)S(1)} %update_near.1.acc_ref, f32[1,1024]{1,0:T(1,128)S(1)} %bitcast.7, ...), custom_call_target="tpu_custom_call" | custom-call | flops 536870912 | bytes 9187328 | tf_op jit(solution)/shard_map/update0/pallas_call | solution.py:407
  32.8 1.6 %collective-permute-start.9 = (bf16[1024,128]{1,0:T(8,128)(2,1)S(1)}, bf16[1024,128]{1,0:T(8,128)(2,1)S(1)}, u32[]{:S(2)}, u32[]{:S(2)}) collective-permute-start(bf16[1024,128]{1,0:T(8,128)(2,1)S(1)} %get-tuple-element.61.refs_0_), channel_id=1, source_target_pairs={{0,8},{8,16},{16,24},{24,28},{28,20},{20,12},{12,4},{4,0},{1,9},{9... | collective-permute-start | bytes 786440 | tf_op jit(solution)/shard_map/ppermute | solution.py:62
  34.4 0.4 collective-permute-start.10
  34.8 1.3 %collective-permute-done.8.refs_1_ = bf16[128,512]{1,0:T(8,128)(2,1)S(1)} collective-permute-done((bf16[128,512]{1,0:T(8,128)(2,1)S(1)}, bf16[128,512]{1,0:T(8,128)(2,1)S(1)}, u32[]{:S(2)}, u32[]{:S(2)}) %collective-permute-start.8) | collective-permute-done | bytes 131104 | tf_op jit(solution)/shard_map/ppermute | solution.py:29
  36.2 1.8 %update1.1 = (bf16[256,1024]{1,0:T(8,128)(2,1)}, f32[256,512]{1,0:T(8,128)S(1)}, bf16[256,512]{1,0:T(8,128)(2,1)S(1)}, f32[8,256]{1,0:T(8,128)S(1)}, bf16[1024,128]{1,0:T(8,128)(2,1)S(1)}) custom-call(s32[1]{0:T(128)} %bitcast.p_ref, f32[256,1024]{1,0:T(8,128)S(1)} %update_near.1.acc_ref, ...), custom_call_target="tpu_custom_call", output_to_operand_aliasing={{0}: (8, {}), {1}: (9, {}), {2}: (10, {}), {3}: (11, {})} | custom-call | flops 536870912 | bytes 10506240 | tf_op jit(solution)/shard_map/update1/pallas_call | solution.py:407
  38.0 1.6 %collective-permute-start.15 = (bf16[1024,128]{1,0:T(8,128)(2,1)S(1)}, bf16[1024,128]{1,0:T(8,128)(2,1)S(1)}, u32[]{:S(2)}, u32[]{:S(2)}) collective-permute-start(bf16[1024,128]{1,0:T(8,128)(2,1)S(1)} %get-tuple-element.71.refs_1_), channel_id=1, source_target_pairs={{0,8},{8,16},{16,24},{24,28},{28,20},{20,12},{12,4},{4,0},{1,9},{9... | collective-permute-start | bytes 786440 | tf_op jit(solution)/shard_map/ppermute | solution.py:62
  40.0 1.8 %collective-permute-done.9.refs_2_ = bf16[1024,128]{1,0:T(8,128)(2,1)S(1)} collective-permute-done((bf16[1024,128]{1,0:T(8,128)(2,1)S(1)}, bf16[1024,128]{1,0:T(8,128)(2,1)S(1)}, u32[]{:S(2)}, u32[]{:S(2)}) %collective-permute-start.9) | collective-permute-done | bytes 262176 | tf_op jit(solution)/shard_map/ppermute | solution.py:62
  41.8 1.3 %collective-permute-done.10.refs_4_ = bf16[1024,128]{1,0:T(8,128)(2,1)S(1)} collective-permute-done((bf16[1024,128]{1,0:T(8,128)(2,1)S(1)}, bf16[1024,128]{1,0:T(8,128)(2,1)S(1)}, u32[]{:S(2)}, u32[]{:S(2)}) %collective-permute-start.10) | collective-permute-done | bytes 262176 | tf_op jit(solution)/shard_map/ppermute | solution.py:62
  43.1 0.5 collective-permute-start.19
  43.6 1.0 collective-permute-done.19
  44.6 1.6 %collective-permute-start.13 = (bf16[1024,128]{1,0:T(8,128)(2,1)S(1)}, bf16[1024,128]{1,0:T(8,128)(2,1)S(1)}, u32[]{:S(2)}, u32[]{:S(2)}) collective-permute-start(bf16[1024,128]{1,0:T(8,128)(2,1)S(1)} %collective-permute-done.9.refs_2_), channel_id=1, source_target_pairs={{0,8},{8,16},{16,24},{24,28},{28,20},{20,12},{12,4},{4,0},{1,9},{9... | collective-permute-start | bytes 786440 | tf_op jit(solution)/shard_map/ppermute | solution.py:62
  46.2 0.7 collective-permute-done.15.refs_3_
  46.9 2.0 %collective-permute-start.14 = (bf16[1024,128]{1,0:T(8,128)(2,1)S(1)}, bf16[1024,128]{1,0:T(8,128)(2,1)S(1)}, u32[]{:S(2)}, u32[]{:S(2)}) collective-permute-start(bf16[1024,128]{1,0:T(8,128)(2,1)S(1)} %collective-permute-done.10.refs_4_), channel_id=1, source_target_pairs={{0,4},{8,0},{16,8},{24,16},{28,24},{20,28},{12,20},{4,12},{1,5},{9... | collective-permute-start | bytes 786440 | tf_op jit(solution)/shard_map/ppermute | solution.py:62
  48.9 0.9 collective-permute-start.17
  49.8 1.1 collective-permute-start.18
  51.1 2.7 %collective-permute-done.13.refs_6_ = bf16[1024,128]{1,0:T(8,128)(2,1)S(1)} collective-permute-done((bf16[1024,128]{1,0:T(8,128)(2,1)S(1)}, bf16[1024,128]{1,0:T(8,128)(2,1)S(1)}, u32[]{:S(2)}, u32[]{:S(2)}) %collective-permute-start.13) | collective-permute-done | bytes 262176 | tf_op jit(solution)/shard_map/ppermute | solution.py:62
  53.8 2.3 %collective-permute-done.14.refs_8_ = bf16[1024,128]{1,0:T(8,128)(2,1)S(1)} collective-permute-done((bf16[1024,128]{1,0:T(8,128)(2,1)S(1)}, bf16[1024,128]{1,0:T(8,128)(2,1)S(1)}, u32[]{:S(2)}, u32[]{:S(2)}) %collective-permute-start.14) | collective-permute-done | bytes 262176 | tf_op jit(solution)/shard_map/ppermute | solution.py:62
  56.1 2.5 %collective-permute-done.17.refs_7_ = bf16[1024,128]{1,0:T(8,128)(2,1)S(1)} collective-permute-done((bf16[1024,128]{1,0:T(8,128)(2,1)S(1)}, bf16[1024,128]{1,0:T(8,128)(2,1)S(1)}, u32[]{:S(2)}, u32[]{:S(2)}) %collective-permute-start.17) | collective-permute-done | bytes 262176 | tf_op jit(solution)/shard_map/ppermute | solution.py:62
  58.6 1.7 %collective-permute-done.18.refs_9_ = bf16[1024,128]{1,0:T(8,128)(2,1)S(1)} collective-permute-done((bf16[1024,128]{1,0:T(8,128)(2,1)S(1)}, bf16[1024,128]{1,0:T(8,128)(2,1)S(1)}, u32[]{:S(2)}, u32[]{:S(2)}) %collective-permute-start.18) | collective-permute-done | bytes 262176 | tf_op jit(solution)/shard_map/ppermute | solution.py:62
  60.3 1.1 heads.1
  61.6 1.2 %collective-permute-done.21 = bf16[64,512]{1,0:T(8,128)(2,1)S(1)} collective-permute-done((bf16[64,512]{1,0:T(8,128)(2,1)S(1)}, bf16[64,512]{1,0:T(8,128)(2,1)S(1)}, u32[]{:S(2)}, u32[]{:S(2)}) %collective-permute-start.21) | collective-permute-done | bytes 65568 | tf_op jit(solution)/shard_map/ppermute | solution.py:29
  62.8 1.6 %collective-permute-start.22 = (bf16[336,512]{1,0:T(8,128)(2,1)S(1)}, bf16[336,512]{1,0:T(8,128)(2,1)S(1)}, u32[]{:S(2)}, u32[]{:S(2)}) collective-permute-start(bf16[336,512]{1,0:T(8,128)(2,1)S(1)} %select_dynamic-update-slice_fusion.refs_0_.refs_18_.refs_14_), channel_id=1, source_target_pairs={{0,8},{8,16},{16,24},{24,28},{28,20},{20,12},{12,4},{4,0},{1,9},{9... | collective-permute-start | bytes 1032200 | tf_op jit(solution)/shard_map/ppermute | solution.py:62
  64.9 1.6 %collective-permute-start.28 = (bf16[1024,128]{1,0:T(8,128)(2,1)S(1)}, bf16[1024,128]{1,0:T(8,128)(2,1)S(1)}, u32[]{:S(2)}, u32[]{:S(2)}) collective-permute-start(bf16[1024,128]{1,0:T(8,128)(2,1)S(1)} %collective-permute-done.13.refs_6_), channel_id=1, source_target_pairs={{0,8},{8,16},{16,24},{24,28},{28,20},{20,12},{12,4},{4,0},{1,9},{9... | collective-permute-start | bytes 786440 | tf_op jit(solution)/shard_map/ppermute | solution.py:62
  66.9 6.9 %collective-permute-done.22.refs_1_.refs_19_.refs_15_ = bf16[336,512]{1,0:T(8,128)(2,1)S(1)} collective-permute-done((bf16[336,512]{1,0:T(8,128)(2,1)S(1)}, bf16[336,512]{1,0:T(8,128)(2,1)S(1)}, u32[]{:S(2)}, u32[]{:S(2)}) %collective-permute-start.22) | collective-permute-done | bytes 344096 | tf_op jit(solution)/shard_map/ppermute | solution.py:62
  73.8 1.6 %collective-permute-start.24 = (bf16[336,512]{1,0:T(8,128)(2,1)S(1)}, bf16[336,512]{1,0:T(8,128)(2,1)S(1)}, u32[]{:S(2)}, u32[]{:S(2)}) collective-permute-start(bf16[336,512]{1,0:T(8,128)(2,1)S(1)} %collective-permute-done.22.refs_1_.refs_19_.refs_15_), channel_id=1, source_target_pairs={{0,8},{8,16},{16,24},{24,28},{28,20},{20,12},{12,4},{4,0},{1,9},{9... | collective-permute-start | bytes 1032200 | tf_op jit(solution)/shard_map/ppermute | solution.py:62
  75.9 3.5 %collective-permute-done.28.refs_10_ = bf16[1024,128]{1,0:T(8,128)(2,1)S(1)} collective-permute-done((bf16[1024,128]{1,0:T(8,128)(2,1)S(1)}, bf16[1024,128]{1,0:T(8,128)(2,1)S(1)}, u32[]{:S(2)}, u32[]{:S(2)}) %collective-permute-start.28) | collective-permute-done | bytes 262176 | tf_op jit(solution)/shard_map/ppermute | solution.py:62
  79.4 1.6 %collective-permute-done.29.refs_12_ = bf16[1024,128]{1,0:T(8,128)(2,1)S(1)} collective-permute-done((bf16[1024,128]{1,0:T(8,128)(2,1)S(1)}, bf16[1024,128]{1,0:T(8,128)(2,1)S(1)}, u32[]{:S(2)}, u32[]{:S(2)}) %collective-permute-start.29) | collective-permute-done | bytes 262176 | tf_op jit(solution)/shard_map/ppermute | solution.py:62
  81.0 1.6 %collective-permute-start.30 = (bf16[1024,128]{1,0:T(8,128)(2,1)S(1)}, bf16[1024,128]{1,0:T(8,128)(2,1)S(1)}, u32[]{:S(2)}, u32[]{:S(2)}) collective-permute-start(bf16[1024,128]{1,0:T(8,128)(2,1)S(1)} %collective-permute-done.17.refs_7_), channel_id=1, source_target_pairs={{0,8},{8,16},{16,24},{24,28},{28,20},{20,12},{12,4},{4,0},{1,9},{9... | collective-permute-start | bytes 786440 | tf_op jit(solution)/shard_map/ppermute | solution.py:62
  82.6 0.5 collective-permute-start.31
  83.1 3.7 %collective-permute-done.24.refs_3_.refs_21_.refs_17_ = bf16[336,512]{1,0:T(8,128)(2,1)S(1)} collective-permute-done((bf16[336,512]{1,0:T(8,128)(2,1)S(1)}, bf16[336,512]{1,0:T(8,128)(2,1)S(1)}, u32[]{:S(2)}, u32[]{:S(2)}) %collective-permute-start.24) | collective-permute-done | bytes 344096 | tf_op jit(solution)/shard_map/ppermute | solution.py:62
  86.8 1.6 %collective-permute-done.25.refs_4_.refs_22_.refs_18_ = bf16[336,512]{1,0:T(8,128)(2,1)S(1)} collective-permute-done((bf16[336,512]{1,0:T(8,128)(2,1)S(1)}, bf16[336,512]{1,0:T(8,128)(2,1)S(1)}, u32[]{:S(2)}, u32[]{:S(2)}) %collective-permute-start.25) | collective-permute-done | bytes 344096 | tf_op jit(solution)/shard_map/ppermute | solution.py:62
  88.4 1.6 %collective-permute-start.26 = (bf16[336,512]{1,0:T(8,128)(2,1)S(1)}, bf16[336,512]{1,0:T(8,128)(2,1)S(1)}, u32[]{:S(2)}, u32[]{:S(2)}) collective-permute-start(bf16[336,512]{1,0:T(8,128)(2,1)S(1)} %collective-permute-done.24.refs_3_.refs_21_.refs_17_), channel_id=1, source_target_pairs={{0,8},{8,16},{16,24},{24,28},{28,20},{20,12},{12,4},{4,0},{1,9},{9... | collective-permute-start | bytes 1032200 | tf_op jit(solution)/shard_map/ppermute | solution.py:62
  90.0 2.4 %collective-permute-done.30.refs_11_ = bf16[1024,128]{1,0:T(8,128)(2,1)S(1)} collective-permute-done((bf16[1024,128]{1,0:T(8,128)(2,1)S(1)}, bf16[1024,128]{1,0:T(8,128)(2,1)S(1)}, u32[]{:S(2)}, u32[]{:S(2)}) %collective-permute-start.30) | collective-permute-done | bytes 262176 | tf_op jit(solution)/shard_map/ppermute | solution.py:62
  92.4 1.5 %collective-permute-start.27 = (bf16[336,512]{1,0:T(8,128)(2,1)S(1)}, bf16[336,512]{1,0:T(8,128)(2,1)S(1)}, u32[]{:S(2)}, u32[]{:S(2)}) collective-permute-start(bf16[336,512]{1,0:T(8,128)(2,1)S(1)} %collective-permute-done.25.refs_4_.refs_22_.refs_18_), channel_id=1, source_target_pairs={{0,4},{8,0},{16,8},{24,16},{28,24},{20,28},{12,20},{4,12},{1,5},{9... | collective-permute-start | bytes 1032200 | tf_op jit(solution)/shard_map/ppermute | solution.py:62
  93.9 0.5 collective-permute-start.37
  94.5 4.5 %collective-permute-done.26.refs_5_.refs_23_.refs_19_ = bf16[336,512]{1,0:T(8,128)(2,1)S(1)} collective-permute-done((bf16[336,512]{1,0:T(8,128)(2,1)S(1)}, bf16[336,512]{1,0:T(8,128)(2,1)S(1)}, u32[]{:S(2)}, u32[]{:S(2)}) %collective-permute-start.26) | collective-permute-done | bytes 344096 | tf_op jit(solution)/shard_map/ppermute | solution.py:62
  99.0 1.9 %collective-permute-done.27.refs_6_.refs_24_.refs_20_ = bf16[336,512]{1,0:T(8,128)(2,1)S(1)} collective-permute-done((bf16[336,512]{1,0:T(8,128)(2,1)S(1)}, bf16[336,512]{1,0:T(8,128)(2,1)S(1)}, u32[]{:S(2)}, u32[]{:S(2)}) %collective-permute-start.27) | collective-permute-done | bytes 344096 | tf_op jit(solution)/shard_map/ppermute | solution.py:62
  100.9 1.6 %collective-permute-start.32 = (bf16[336,256]{1,0:T(8,128)(2,1)S(1)}, bf16[336,256]{1,0:T(8,128)(2,1)S(1)}, u32[]{:S(2)}, u32[]{:S(2)}) collective-permute-start(bf16[336,256]{1,0:T(8,128)(2,1)S(1)} %slice.12), channel_id=1, source_target_pairs={{0,8},{8,16},{16,24},{24,28},{28,20},{20,12},{12,4},{4,0},{1,9},{9... | collective-permute-start | bytes 516104 | tf_op jit(solution)/shard_map/ppermute | solution.py:62
  102.5 0.5 collective-permute-start.33
  103.0 1.6 %collective-permute-start.43 = (bf16[1024,128]{1,0:T(8,128)(2,1)S(1)}, bf16[1024,128]{1,0:T(8,128)(2,1)S(1)}, u32[]{:S(2)}, u32[]{:S(2)}) collective-permute-start(bf16[1024,128]{1,0:T(8,128)(2,1)S(1)} %collective-permute-done.28.refs_10_), channel_id=1, source_target_pairs={{0,8},{8,16},{16,24},{24,28},{28,20},{20,12},{12,4},{4,0},{1,9},{9... | collective-permute-start | bytes 786440 | tf_op jit(solution)/shard_map/ppermute | solution.py:62
  104.7 1.8 %collective-permute-done.32.refs_7_.refs_25_.refs_4_ = bf16[336,256]{1,0:T(8,128)(2,1)S(1)} collective-permute-done((bf16[336,256]{1,0:T(8,128)(2,1)S(1)}, bf16[336,256]{1,0:T(8,128)(2,1)S(1)}, u32[]{:S(2)}, u32[]{:S(2)}) %collective-permute-start.32) | collective-permute-done | bytes 172064 | tf_op jit(solution)/shard_map/ppermute | solution.py:62
  106.4 1.5 %collective-permute-start.44 = (bf16[1024,128]{1,0:T(8,128)(2,1)S(1)}, bf16[1024,128]{1,0:T(8,128)(2,1)S(1)}, u32[]{:S(2)}, u32[]{:S(2)}) collective-permute-start(bf16[1024,128]{1,0:T(8,128)(2,1)S(1)} %collective-permute-done.31.refs_13_), channel_id=1, source_target_pairs={{0,4},{8,0},{16,8},{24,16},{28,24},{20,28},{12,20},{4,12},{1,5},{9... | collective-permute-start | bytes 786440 | tf_op jit(solution)/shard_map/ppermute | solution.py:62
  107.9 0.6 collective-permute-done.33.refs_8_.refs_26_.refs_5_
  108.5 0.5 collective-permute-start.42
  109.0 0.9 collective-permute-done.41.refs_16_.refs_34_.refs_6_
  110.1 0.8 sums.1
  110.9 1.3 %collective-permute-start.45 = (bf16[256,256]{1,0:T(8,128)(2,1)S(1)}, bf16[256,256]{1,0:T(8,128)(2,1)S(1)}, u32[]{:S(2)}, u32[]{:S(2)}) collective-permute-start(bf16[256,256]{1,0:T(8,128)(2,1)S(1)} %get-tuple-element.90.refs_0_), channel_id=1, source_target_pairs={{0,2},{1,3},{2,0},{3,1},{4,6},{5,7},{6,4},{7,5},{8,10},{9,11},{10,... | collective-permute-start | bytes 393224 | tf_op jit(solution)/shard_map/ppermute | solution.py:29
  112.2 4.1 %gradients_start.1 = (f32[1024,512]{1,0:T(8,128)S(1)}, f32[1024,512]{1,0:T(8,128)S(1)}) custom-call(s32[1]{0:T(128)} %bitcast.p_ref, bf16[1024,128]{1,0:T(8,128)(2,1)S(1)} %get-tuple-element.61.refs_0_, bf16[1024,128]{1,0:T(8,128)(2,1)S(1)} %get-tuple-element.71.refs_1_, bf16[1024,128]{1,0:T(8,128)(2,1)S(1)} %collective-permute-done.9.refs_2_, ...), custom_call_target="tpu_custom_call" | custom-call | tf_op jit(solution)/shard_map/gradients_start/pallas_call | solution.py:407
  116.4 2.1 %gradients_end.1 = (bf16[1024,512]{1,0:T(8,128)(2,1)}, bf16[1024,512]{1,0:T(8,128)(2,1)}) custom-call(s32[1]{0:T(128)} %bitcast.p_ref, f32[1024,512]{1,0:T(8,128)S(1)} %get-tuple-element.84.refs_0_, f32[1024,512]{1,0:T(8,128)S(1)} %get-tuple-element.85.refs_1_, bf16[1024,128]{1,0:T(8,128)(2,1)S(1)} %collective-permute-done.43.refs_2_, ...), custom_call_target="tpu_custom_call" | custom-call | flops 536870912 | bytes 7503872 | tf_op jit(solution)/shard_map/gradients_end/pallas_call | solution.py:407
  118.5 0.7 join.1
  (64 shorter events, 2.5 us)
Async XLA Ops:
  2.4 3.1 %collective-permute-start = (bf16[272,1024]{1,0:T(8,128)(2,1)S(1)}, bf16[272,1024]{1,0:T(8,128)(2,1)S(1)}, u32[]{:S(2)}, u32[]{:S(2)}) collective-permute-start(bf16[272,1024]{1,0:T(8,128)(2,1)S(1)} %get-tuple-element.50.refs_0_), channel_id=1, source_target_pairs={{0,1},{1,0},{2,3},{3,2},{4,5},{5,4},{6,7},{7,6},{8,9},{9,8},{10,11... | collective-permute-start | bytes 1671176 | tf_op jit(solution)/shard_map/ppermute | solution.py:29
  2.9 15.8 %collective-permute-start.1 = (bf16[272,1024]{1,0:T(8,128)(2,1)S(1)}, bf16[272,1024]{1,0:T(8,128)(2,1)S(1)}, u32[]{:S(2)}, u32[]{:S(2)}) collective-permute-start(bf16[272,1024]{1,0:T(8,128)(2,1)S(1)} %get-tuple-element.50.refs_0_), channel_id=1, source_target_pairs={{0,2},{1,3},{2,0},{3,1},{4,6},{5,7},{6,4},{7,5},{8,10},{9,11},{10,... | collective-permute-start | bytes 1671176 | tf_op jit(solution)/shard_map/ppermute | solution.py:29
  18.7 2.0 %collective-permute-start.2 = (bf16[272,1024]{1,0:T(8,128)(2,1)S(1)}, bf16[272,1024]{1,0:T(8,128)(2,1)S(1)}, u32[]{:S(2)}, u32[]{:S(2)}) collective-permute-start(bf16[272,1024]{1,0:T(8,128)(2,1)S(1)} %collective-permute-done.1.refs_0_.refs_1_), channel_id=1, source_target_pairs={{0,1},{1,0},{2,3},{3,2},{4,5},{5,4},{6,7},{7,6},{8,9},{9,8},{10,11... | collective-permute-start | bytes 1671176 | tf_op jit(solution)/shard_map/ppermute | solution.py:29
  22.6 7.4 %copy-start = (bf16[2048,1024]{1,0:T(8,128)(2,1)S(1)}, bf16[2048,1024]{1,0:T(8,128)(2,1)}, u32[]{:S(2)}) copy-start(bf16[2048,1024]{1,0:T(8,128)(2,1)} %refs_2_.5) | copy-start | bytes 12582916
  22.7 5.6 %collective-permute-start.6 = (bf16[128,512]{1,0:T(8,128)(2,1)S(1)}, bf16[128,512]{1,0:T(8,128)(2,1)S(1)}, u32[]{:S(2)}, u32[]{:S(2)}) collective-permute-start(bf16[128,512]{1,0:T(8,128)(2,1)S(1)} %attend0.1.refs_0_), channel_id=1, source_target_pairs={{0,2},{1,3},{2,0},{3,1},{4,6},{5,7},{6,4},{7,5},{8,10},{9,11},{10,... | collective-permute-start | bytes 393224 | tf_op jit(solution)/shard_map/ppermute | solution.py:29
  24.5 5.5 %collective-permute-start.3 = (bf16[128,512]{1,0:T(8,128)(2,1)S(1)}, bf16[128,512]{1,0:T(8,128)(2,1)S(1)}, u32[]{:S(2)}, u32[]{:S(2)}) collective-permute-start(bf16[128,512]{1,0:T(8,128)(2,1)S(1)} %attend0.1.refs_0_), channel_id=1, source_target_pairs={{0,1},{1,0},{2,3},{3,2},{4,5},{5,4},{6,7},{7,6},{8,9},{9,8},{10,11... | collective-permute-start | bytes 393224 | tf_op jit(solution)/shard_map/ppermute | solution.py:29
  26.5 4.5 %copy-start.1 = (bf16[1024,512]{1,0:T(8,128)(2,1)S(1)}, bf16[1024,512]{1,0:T(8,128)(2,1)}, u32[]{:S(2)}) copy-start(bf16[1024,512]{1,0:T(8,128)(2,1)} %policy_ref.3) | copy-start | bytes 3145732
  26.5 4.5 %copy-start.2 = (bf16[1024,512]{1,0:T(8,128)(2,1)S(1)}, bf16[1024,512]{1,0:T(8,128)(2,1)}, u32[]{:S(2)}) copy-start(bf16[1024,512]{1,0:T(8,128)(2,1)} %value_ref.3) | copy-start | bytes 3145732
  26.5 4.5 %copy-start.4 = (f32[1024]{0:T(1024)S(1)}, f32[1024]{0:T(1024)}, u32[]{:S(2)}) copy-start(f32[1024]{0:T(1024)} %param.27) | copy-start | bytes 12292
  26.5 3.5 %collective-permute-start.4 = (bf16[128,512]{1,0:T(8,128)(2,1)S(1)}, bf16[128,512]{1,0:T(8,128)(2,1)S(1)}, u32[]{:S(2)}, u32[]{:S(2)}) collective-permute-start(bf16[128,512]{1,0:T(8,128)(2,1)S(1)} %attend1.1.refs_1_), channel_id=1, source_target_pairs={{0,1},{1,0},{2,3},{3,2},{4,5},{5,4},{6,7},{7,6},{8,9},{9,8},{10,11... | collective-permute-start | bytes 393224 | tf_op jit(solution)/shard_map/ppermute | solution.py:29
  28.3 2.7 %collective-permute-start.7 = (bf16[128,512]{1,0:T(8,128)(2,1)S(1)}, bf16[128,512]{1,0:T(8,128)(2,1)S(1)}, u32[]{:S(2)}, u32[]{:S(2)}) collective-permute-start(bf16[128,512]{1,0:T(8,128)(2,1)S(1)} %collective-permute-done.6.refs_0_), channel_id=1, source_target_pairs={{0,1},{1,0},{2,3},{3,2},{4,5},{5,4},{6,7},{7,6},{8,9},{9,8},{10,11... | collective-permute-start | bytes 393224 | tf_op jit(solution)/shard_map/ppermute | solution.py:29
  28.3 6.6 %collective-permute-start.5 = (bf16[128,512]{1,0:T(8,128)(2,1)S(1)}, bf16[128,512]{1,0:T(8,128)(2,1)S(1)}, u32[]{:S(2)}, u32[]{:S(2)}) collective-permute-start(bf16[128,512]{1,0:T(8,128)(2,1)S(1)} %attend1.1.refs_1_), channel_id=1, source_target_pairs={{0,2},{1,3},{2,0},{3,1},{4,6},{5,7},{6,4},{7,5},{8,10},{9,11},{10,... | collective-permute-start | bytes 393224 | tf_op jit(solution)/shard_map/ppermute | solution.py:29
  32.8 9.0 %collective-permute-start.9 = (bf16[1024,128]{1,0:T(8,128)(2,1)S(1)}, bf16[1024,128]{1,0:T(8,128)(2,1)S(1)}, u32[]{:S(2)}, u32[]{:S(2)}) collective-permute-start(bf16[1024,128]{1,0:T(8,128)(2,1)S(1)} %get-tuple-element.61.refs_0_), channel_id=1, source_target_pairs={{0,8},{8,16},{16,24},{24,28},{28,20},{20,12},{12,4},{4,0},{1,9},{9... | collective-permute-start | bytes 786440 | tf_op jit(solution)/shard_map/ppermute | solution.py:62
  34.4 8.7 %collective-permute-start.10 = (bf16[1024,128]{1,0:T(8,128)(2,1)S(1)}, bf16[1024,128]{1,0:T(8,128)(2,1)S(1)}, u32[]{:S(2)}, u32[]{:S(2)}) collective-permute-start(bf16[1024,128]{1,0:T(8,128)(2,1)S(1)} %get-tuple-element.61.refs_0_), channel_id=1, source_target_pairs={{0,4},{8,0},{16,8},{24,16},{28,24},{20,28},{12,20},{4,12},{1,5},{9... | collective-permute-start | bytes 786440 | tf_op jit(solution)/shard_map/ppermute | solution.py:62
  34.8 1.3 %collective-permute-start.8 = (bf16[128,512]{1,0:T(8,128)(2,1)S(1)}, bf16[128,512]{1,0:T(8,128)(2,1)S(1)}, u32[]{:S(2)}, u32[]{:S(2)}) collective-permute-start(bf16[128,512]{1,0:T(8,128)(2,1)S(1)} %collective-permute-done.5.refs_0_), channel_id=1, source_target_pairs={{0,1},{1,0},{2,3},{3,2},{4,5},{5,4},{6,7},{7,6},{8,9},{9,8},{10,11... | collective-permute-start | bytes 393224 | tf_op jit(solution)/shard_map/ppermute | solution.py:29
  36.2 14.9 %copy-start.7 = (bf16[512]{0:T(512)(128)(2,1)S(1)}, bf16[512]{0:T(512)(128)(2,1)}, u32[]{:S(2)}) copy-start(bf16[512]{0:T(512)(128)(2,1)} %param.31) | copy-start | bytes 3076
  36.2 24.1 %copy-start.3 = (bf16[512,256]{1,0:T(8,128)(2,1)S(1)}, bf16[512,256]{1,0:T(8,128)(2,1)}, u32[]{:S(2)}) copy-start(bf16[512,256]{1,0:T(8,128)(2,1)} %policy_out_ref.1) | copy-start | bytes 786436
  36.2 24.1 %copy-start.5 = (s32[256]{0:T(256)S(1)}, s32[256]{0:T(256)}, u32[]{:S(2)}) copy-start(s32[256]{0:T(256)} %param.32) | copy-start | bytes 3076
  36.2 24.1 %copy-start.6 = (f32[256]{0:T(256)S(1)}, f32[256]{0:T(256)}, u32[]{:S(2)}) copy-start(f32[256]{0:T(256)} %param.33) | copy-start | bytes 3076
  38.0 8.9 %collective-permute-start.15 = (bf16[1024,128]{1,0:T(8,128)(2,1)S(1)}, bf16[1024,128]{1,0:T(8,128)(2,1)S(1)}, u32[]{:S(2)}, u32[]{:S(2)}) collective-permute-start(bf16[1024,128]{1,0:T(8,128)(2,1)S(1)} %get-tuple-element.71.refs_1_), channel_id=1, source_target_pairs={{0,8},{8,16},{16,24},{24,28},{28,20},{20,12},{12,4},{4,0},{1,9},{9... | collective-permute-start | bytes 786440 | tf_op jit(solution)/shard_map/ppermute | solution.py:62
  39.5 9.3 %collective-permute-start.16 = (bf16[1024,128]{1,0:T(8,128)(2,1)S(1)}, bf16[1024,128]{1,0:T(8,128)(2,1)S(1)}, u32[]{:S(2)}, u32[]{:S(2)}) collective-permute-start(bf16[1024,128]{1,0:T(8,128)(2,1)S(1)} %get-tuple-element.71.refs_1_), channel_id=1, source_target_pairs={{0,4},{8,0},{16,8},{24,16},{28,24},{20,28},{12,20},{4,12},{1,5},{9... | collective-permute-start | bytes 786440 | tf_op jit(solution)/shard_map/ppermute | solution.py:62
  43.1 6.7 %collective-permute-start.11 = (bf16[256,512]{1,0:T(8,128)(2,1)S(1)}, bf16[256,512]{1,0:T(8,128)(2,1)S(1)}, u32[]{:S(2)}, u32[]{:S(2)}) collective-permute-start(bf16[256,512]{1,0:T(8,128)(2,1)S(1)} %get-tuple-element.70), channel_id=1, source_target_pairs={{0,1},{1,0},{2,3},{3,2},{4,5},{5,4},{6,7},{7,6},{8,9},{9,8},{10,11... | collective-permute-start | bytes 786440 | tf_op jit(solution)/shard_map/ppermute | solution.py:29
  43.1 1.5 %collective-permute-start.19 = (f32[8,256]{1,0:T(8,128)S(1)}, f32[8,256]{1,0:T(8,128)S(1)}, u32[]{:S(2)}, u32[]{:S(2)}) collective-permute-start(f32[8,256]{1,0:T(8,128)S(1)} %get-tuple-element.73), channel_id=1, source_target_pairs={{0,1},{1,0},{2,3},{3,2},{4,5},{5,4},{6,7},{7,6},{8,9},{9,8},{10,11... | collective-permute-start | bytes 24584 | tf_op jit(solution)/shard_map/ppermute | solution.py:29
  44.6 6.4 %collective-permute-start.20 = (f32[8,256]{1,0:T(8,128)S(1)}, f32[8,256]{1,0:T(8,128)S(1)}, u32[]{:S(2)}, u32[]{:S(2)}) collective-permute-start(f32[8,256]{1,0:T(8,128)S(1)} %add.14), channel_id=1, source_target_pairs={{0,2},{1,3},{2,0},{3,1},{4,6},{5,7},{6,4},{7,5},{8,10},{9,11},{10,... | collective-permute-start | bytes 24584 | tf_op jit(solution)/shard_map/ppermute | solution.py:29
  44.6 9.1 %collective-permute-start.13 = (bf16[1024,128]{1,0:T(8,128)(2,1)S(1)}, bf16[1024,128]{1,0:T(8,128)(2,1)S(1)}, u32[]{:S(2)}, u32[]{:S(2)}) collective-permute-start(bf16[1024,128]{1,0:T(8,128)(2,1)S(1)} %collective-permute-done.9.refs_2_), channel_id=1, source_target_pairs={{0,8},{8,16},{16,24},{24,28},{28,20},{20,12},{12,4},{4,0},{1,9},{9... | collective-permute-start | bytes 786440 | tf_op jit(solution)/shard_map/ppermute | solution.py:62
  46.9 9.2 %collective-permute-start.14 = (bf16[1024,128]{1,0:T(8,128)(2,1)S(1)}, bf16[1024,128]{1,0:T(8,128)(2,1)S(1)}, u32[]{:S(2)}, u32[]{:S(2)}) collective-permute-start(bf16[1024,128]{1,0:T(8,128)(2,1)S(1)} %collective-permute-done.10.refs_4_), channel_id=1, source_target_pairs={{0,4},{8,0},{16,8},{24,16},{28,24},{20,28},{12,20},{4,12},{1,5},{9... | collective-permute-start | bytes 786440 | tf_op jit(solution)/shard_map/ppermute | solution.py:62
  48.9 9.7 %collective-permute-start.17 = (bf16[1024,128]{1,0:T(8,128)(2,1)S(1)}, bf16[1024,128]{1,0:T(8,128)(2,1)S(1)}, u32[]{:S(2)}, u32[]{:S(2)}) collective-permute-start(bf16[1024,128]{1,0:T(8,128)(2,1)S(1)} %collective-permute-done.15.refs_3_), channel_id=1, source_target_pairs={{0,8},{8,16},{16,24},{24,28},{28,20},{20,12},{12,4},{4,0},{1,9},{9... | collective-permute-start | bytes 786440 | tf_op jit(solution)/shard_map/ppermute | solution.py:62
  49.8 10.6 %collective-permute-start.18 = (bf16[1024,128]{1,0:T(8,128)(2,1)S(1)}, bf16[1024,128]{1,0:T(8,128)(2,1)S(1)}, u32[]{:S(2)}, u32[]{:S(2)}) collective-permute-start(bf16[1024,128]{1,0:T(8,128)(2,1)S(1)} %collective-permute-done.16.refs_5_), channel_id=1, source_target_pairs={{0,4},{8,0},{16,8},{24,16},{28,24},{20,28},{12,20},{4,12},{1,5},{9... | collective-permute-start | bytes 786440 | tf_op jit(solution)/shard_map/ppermute | solution.py:62
  51.0 9.3 %collective-permute-start.12 = (bf16[256,512]{1,0:T(8,128)(2,1)S(1)}, bf16[256,512]{1,0:T(8,128)(2,1)S(1)}, u32[]{:S(2)}, u32[]{:S(2)}) collective-permute-start(bf16[256,512]{1,0:T(8,128)(2,1)S(1)} %add_convert_fusion.mine_ref), channel_id=1, source_target_pairs={{0,2},{1,3},{2,0},{3,1},{4,6},{5,7},{6,4},{7,5},{8,10},{9,11},{10,... | collective-permute-start | bytes 786440 | tf_op jit(solution)/shard_map/ppermute | solution.py:29
  61.5 1.3 %collective-permute-start.21 = (bf16[64,512]{1,0:T(8,128)(2,1)S(1)}, bf16[64,512]{1,0:T(8,128)(2,1)S(1)}, u32[]{:S(2)}, u32[]{:S(2)}) collective-permute-start(bf16[64,512]{1,0:T(8,128)(2,1)S(1)} %get-tuple-element.76), channel_id=1, source_target_pairs={{0,1},{1,0},{2,3},{3,2},{4,5},{5,4},{6,7},{7,6},{8,9},{9,8},{10,11... | collective-permute-start | bytes 196616 | tf_op jit(solution)/shard_map/ppermute | solution.py:29
  62.8 11.0 %collective-permute-start.22 = (bf16[336,512]{1,0:T(8,128)(2,1)S(1)}, bf16[336,512]{1,0:T(8,128)(2,1)S(1)}, u32[]{:S(2)}, u32[]{:S(2)}) collective-permute-start(bf16[336,512]{1,0:T(8,128)(2,1)S(1)} %select_dynamic-update-slice_fusion.refs_0_.refs_18_.refs_14_), channel_id=1, source_target_pairs={{0,8},{8,16},{16,24},{24,28},{28,20},{20,12},{12,4},{4,0},{1,9},{9... | collective-permute-start | bytes 1032200 | tf_op jit(solution)/shard_map/ppermute | solution.py:62
  64.5 10.9 %collective-permute-start.23 = (bf16[336,512]{1,0:T(8,128)(2,1)S(1)}, bf16[336,512]{1,0:T(8,128)(2,1)S(1)}, u32[]{:S(2)}, u32[]{:S(2)}) collective-permute-start(bf16[336,512]{1,0:T(8,128)(2,1)S(1)} %select_dynamic-update-slice_fusion.refs_0_.refs_18_.refs_14_), channel_id=1, source_target_pairs={{0,4},{8,0},{16,8},{24,16},{28,24},{20,28},{12,20},{4,12},{1,5},{9... | collective-permute-start | bytes 1032200 | tf_op jit(solution)/shard_map/ppermute | solution.py:62
  64.9 14.5 %collective-permute-start.28 = (bf16[1024,128]{1,0:T(8,128)(2,1)S(1)}, bf16[1024,128]{1,0:T(8,128)(2,1)S(1)}, u32[]{:S(2)}, u32[]{:S(2)}) collective-permute-start(bf16[1024,128]{1,0:T(8,128)(2,1)S(1)} %collective-permute-done.13.refs_6_), channel_id=1, source_target_pairs={{0,8},{8,16},{16,24},{24,28},{28,20},{20,12},{12,4},{4,0},{1,9},{9... | collective-permute-start | bytes 786440 | tf_op jit(solution)/shard_map/ppermute | solution.py:62
  66.5 14.5 %collective-permute-start.29 = (bf16[1024,128]{1,0:T(8,128)(2,1)S(1)}, bf16[1024,128]{1,0:T(8,128)(2,1)S(1)}, u32[]{:S(2)}, u32[]{:S(2)}) collective-permute-start(bf16[1024,128]{1,0:T(8,128)(2,1)S(1)} %collective-permute-done.14.refs_8_), channel_id=1, source_target_pairs={{0,4},{8,0},{16,8},{24,16},{28,24},{20,28},{12,20},{4,12},{1,5},{9... | collective-permute-start | bytes 786440 | tf_op jit(solution)/shard_map/ppermute | solution.py:62
  73.8 13.0 %collective-permute-start.24 = (bf16[336,512]{1,0:T(8,128)(2,1)S(1)}, bf16[336,512]{1,0:T(8,128)(2,1)S(1)}, u32[]{:S(2)}, u32[]{:S(2)}) collective-permute-start(bf16[336,512]{1,0:T(8,128)(2,1)S(1)} %collective-permute-done.22.refs_1_.refs_19_.refs_15_), channel_id=1, source_target_pairs={{0,8},{8,16},{16,24},{24,28},{28,20},{20,12},{12,4},{4,0},{1,9},{9... | collective-permute-start | bytes 1032200 | tf_op jit(solution)/shard_map/ppermute | solution.py:62
  75.4 13.0 %collective-permute-start.25 = (bf16[336,512]{1,0:T(8,128)(2,1)S(1)}, bf16[336,512]{1,0:T(8,128)(2,1)S(1)}, u32[]{:S(2)}, u32[]{:S(2)}) collective-permute-start(bf16[336,512]{1,0:T(8,128)(2,1)S(1)} %collective-permute-done.23.refs_2_.refs_20_.refs_16_), channel_id=1, source_target_pairs={{0,4},{8,0},{16,8},{24,16},{28,24},{20,28},{12,20},{4,12},{1,5},{9... | collective-permute-start | bytes 1032200 | tf_op jit(solution)/shard_map/ppermute | solution.py:62
  75.9 18.1 %collective-permute-start.34 = (bf16[336,512]{1,0:T(8,128)(2,1)S(1)}, bf16[336,512]{1,0:T(8,128)(2,1)S(1)}, u32[]{:S(2)}, u32[]{:S(2)}) collective-permute-start(bf16[336,512]{1,0:T(8,128)(2,1)S(1)} %select_dynamic-update-slice_fusion.refs_0_.refs_18_.refs_14_), channel_id=1, source_target_pairs={{0,1},{1,0},{2,3},{3,2},{4,5},{5,4},{6,7},{7,6},{8,9},{9,8},{10,11... | collective-permute-start | bytes 1032200 | tf_op jit(solution)/shard_map/ppermute | solution.py:29
  81.0 11.4 %collective-permute-start.30 = (bf16[1024,128]{1,0:T(8,128)(2,1)S(1)}, bf16[1024,128]{1,0:T(8,128)(2,1)S(1)}, u32[]{:S(2)}, u32[]{:S(2)}) collective-permute-start(bf16[1024,128]{1,0:T(8,128)(2,1)S(1)} %collective-permute-done.17.refs_7_), channel_id=1, source_target_pairs={{0,8},{8,16},{16,24},{24,28},{28,20},{20,12},{12,4},{4,0},{1,9},{9... | collective-permute-start | bytes 786440 | tf_op jit(solution)/shard_map/ppermute | solution.py:62
  82.6 11.3 %collective-permute-start.31 = (bf16[1024,128]{1,0:T(8,128)(2,1)S(1)}, bf16[1024,128]{1,0:T(8,128)(2,1)S(1)}, u32[]{:S(2)}, u32[]{:S(2)}) collective-permute-start(bf16[1024,128]{1,0:T(8,128)(2,1)S(1)} %collective-permute-done.18.refs_9_), channel_id=1, source_target_pairs={{0,4},{8,0},{16,8},{24,16},{28,24},{20,28},{12,20},{4,12},{1,5},{9... | collective-permute-start | bytes 786440 | tf_op jit(solution)/shard_map/ppermute | solution.py:62
  86.8 7.6 %collective-permute-start.35 = (bf16[336,512]{1,0:T(8,128)(2,1)S(1)}, bf16[336,512]{1,0:T(8,128)(2,1)S(1)}, u32[]{:S(2)}, u32[]{:S(2)}) collective-permute-start(bf16[336,512]{1,0:T(8,128)(2,1)S(1)} %collective-permute-done.22.refs_1_.refs_19_.refs_15_), channel_id=1, source_target_pairs={{0,1},{1,0},{2,3},{3,2},{4,5},{5,4},{6,7},{7,6},{8,9},{9,8},{10,11... | collective-permute-start | bytes 1032200 | tf_op jit(solution)/shard_map/ppermute | solution.py:29
  88.4 10.6 %collective-permute-start.26 = (bf16[336,512]{1,0:T(8,128)(2,1)S(1)}, bf16[336,512]{1,0:T(8,128)(2,1)S(1)}, u32[]{:S(2)}, u32[]{:S(2)}) collective-permute-start(bf16[336,512]{1,0:T(8,128)(2,1)S(1)} %collective-permute-done.24.refs_3_.refs_21_.refs_17_), channel_id=1, source_target_pairs={{0,8},{8,16},{16,24},{24,28},{28,20},{20,12},{12,4},{4,0},{1,9},{9... | collective-permute-start | bytes 1032200 | tf_op jit(solution)/shard_map/ppermute | solution.py:62
  92.4 8.5 %collective-permute-start.27 = (bf16[336,512]{1,0:T(8,128)(2,1)S(1)}, bf16[336,512]{1,0:T(8,128)(2,1)S(1)}, u32[]{:S(2)}, u32[]{:S(2)}) collective-permute-start(bf16[336,512]{1,0:T(8,128)(2,1)S(1)} %collective-permute-done.25.refs_4_.refs_22_.refs_18_), channel_id=1, source_target_pairs={{0,4},{8,0},{16,8},{24,16},{28,24},{20,28},{12,20},{4,12},{1,5},{9... | collective-permute-start | bytes 1032200 | tf_op jit(solution)/shard_map/ppermute | solution.py:62
  93.9 8.6 %collective-permute-start.36 = (bf16[336,512]{1,0:T(8,128)(2,1)S(1)}, bf16[336,512]{1,0:T(8,128)(2,1)S(1)}, u32[]{:S(2)}, u32[]{:S(2)}) collective-permute-start(bf16[336,512]{1,0:T(8,128)(2,1)S(1)} %collective-permute-done.23.refs_2_.refs_20_.refs_16_), channel_id=1, source_target_pairs={{0,1},{1,0},{2,3},{3,2},{4,5},{5,4},{6,7},{7,6},{8,9},{9,8},{10,11... | collective-permute-start | bytes 1032200 | tf_op jit(solution)/shard_map/ppermute | solution.py:29
  93.9 9.1 %collective-permute-start.37 = (bf16[336,512]{1,0:T(8,128)(2,1)S(1)}, bf16[336,512]{1,0:T(8,128)(2,1)S(1)}, u32[]{:S(2)}, u32[]{:S(2)}) collective-permute-start(bf16[336,512]{1,0:T(8,128)(2,1)S(1)} %collective-permute-done.24.refs_3_.refs_21_.refs_17_), channel_id=1, source_target_pairs={{0,1},{1,0},{2,3},{3,2},{4,5},{5,4},{6,7},{7,6},{8,9},{9,8},{10,11... | collective-permute-start | bytes 1032200 | tf_op jit(solution)/shard_map/ppermute | solution.py:29
  94.4 8.6 %collective-permute-start.38 = (bf16[336,512]{1,0:T(8,128)(2,1)S(1)}, bf16[336,512]{1,0:T(8,128)(2,1)S(1)}, u32[]{:S(2)}, u32[]{:S(2)}) collective-permute-start(bf16[336,512]{1,0:T(8,128)(2,1)S(1)} %collective-permute-done.25.refs_4_.refs_22_.refs_18_), channel_id=1, source_target_pairs={{0,1},{1,0},{2,3},{3,2},{4,5},{5,4},{6,7},{7,6},{8,9},{9,8},{10,11... | collective-permute-start | bytes 1032200 | tf_op jit(solution)/shard_map/ppermute | solution.py:29
  99.0 9.5 %collective-permute-start.39 = (bf16[336,512]{1,0:T(8,128)(2,1)S(1)}, bf16[336,512]{1,0:T(8,128)(2,1)S(1)}, u32[]{:S(2)}, u32[]{:S(2)}) collective-permute-start(bf16[336,512]{1,0:T(8,128)(2,1)S(1)} %collective-permute-done.26.refs_5_.refs_23_.refs_19_), channel_id=1, source_target_pairs={{0,1},{1,0},{2,3},{3,2},{4,5},{5,4},{6,7},{7,6},{8,9},{9,8},{10,11... | collective-permute-start | bytes 1032200 | tf_op jit(solution)/shard_map/ppermute | solution.py:29
  100.9 5.5 %collective-permute-start.32 = (bf16[336,256]{1,0:T(8,128)(2,1)S(1)}, bf16[336,256]{1,0:T(8,128)(2,1)S(1)}, u32[]{:S(2)}, u32[]{:S(2)}) collective-permute-start(bf16[336,256]{1,0:T(8,128)(2,1)S(1)} %slice.12), channel_id=1, source_target_pairs={{0,8},{8,16},{16,24},{24,28},{28,20},{20,12},{12,4},{4,0},{1,9},{9... | collective-permute-start | bytes 516104 | tf_op jit(solution)/shard_map/ppermute | solution.py:62
  102.5 6.0 %collective-permute-start.33 = (bf16[336,256]{1,0:T(8,128)(2,1)S(1)}, bf16[336,256]{1,0:T(8,128)(2,1)S(1)}, u32[]{:S(2)}, u32[]{:S(2)}) collective-permute-start(bf16[336,256]{1,0:T(8,128)(2,1)S(1)} %slice.13), channel_id=1, source_target_pairs={{0,4},{8,0},{16,8},{24,16},{28,24},{20,28},{12,20},{4,12},{1,5},{9... | collective-permute-start | bytes 516104 | tf_op jit(solution)/shard_map/ppermute | solution.py:62
  103.0 6.0 %collective-permute-start.40 = (bf16[336,512]{1,0:T(8,128)(2,1)S(1)}, bf16[336,512]{1,0:T(8,128)(2,1)S(1)}, u32[]{:S(2)}, u32[]{:S(2)}) collective-permute-start(bf16[336,512]{1,0:T(8,128)(2,1)S(1)} %collective-permute-done.27.refs_6_.refs_24_.refs_20_), channel_id=1, source_target_pairs={{0,1},{1,0},{2,3},{3,2},{4,5},{5,4},{6,7},{7,6},{8,9},{9,8},{10,11... | collective-permute-start | bytes 1032200 | tf_op jit(solution)/shard_map/ppermute | solution.py:29
  103.0 13.4 %collective-permute-start.43 = (bf16[1024,128]{1,0:T(8,128)(2,1)S(1)}, bf16[1024,128]{1,0:T(8,128)(2,1)S(1)}, u32[]{:S(2)}, u32[]{:S(2)}) collective-permute-start(bf16[1024,128]{1,0:T(8,128)(2,1)S(1)} %collective-permute-done.28.refs_10_), channel_id=1, source_target_pairs={{0,8},{8,16},{16,24},{24,28},{28,20},{20,12},{12,4},{4,0},{1,9},{9... | collective-permute-start | bytes 786440 | tf_op jit(solution)/shard_map/ppermute | solution.py:62
  106.4 10.0 %collective-permute-start.44 = (bf16[1024,128]{1,0:T(8,128)(2,1)S(1)}, bf16[1024,128]{1,0:T(8,128)(2,1)S(1)}, u32[]{:S(2)}, u32[]{:S(2)}) collective-permute-start(bf16[1024,128]{1,0:T(8,128)(2,1)S(1)} %collective-permute-done.31.refs_13_), channel_id=1, source_target_pairs={{0,4},{8,0},{16,8},{24,16},{28,24},{20,28},{12,20},{4,12},{1,5},{9... | collective-permute-start | bytes 786440 | tf_op jit(solution)/shard_map/ppermute | solution.py:62
  108.5 1.4 %collective-permute-start.41 = (bf16[336,256]{1,0:T(8,128)(2,1)S(1)}, bf16[336,256]{1,0:T(8,128)(2,1)S(1)}, u32[]{:S(2)}, u32[]{:S(2)}) collective-permute-start(bf16[336,256]{1,0:T(8,128)(2,1)S(1)} %collective-permute-done.32.refs_7_.refs_25_.refs_4_), channel_id=1, source_target_pairs={{0,1},{1,0},{2,3},{3,2},{4,5},{5,4},{6,7},{7,6},{8,9},{9,8},{10,11... | collective-permute-start | bytes 516104 | tf_op jit(solution)/shard_map/ppermute | solution.py:29
  108.5 1.6 %collective-permute-start.42 = (bf16[336,256]{1,0:T(8,128)(2,1)S(1)}, bf16[336,256]{1,0:T(8,128)(2,1)S(1)}, u32[]{:S(2)}, u32[]{:S(2)}) collective-permute-start(bf16[336,256]{1,0:T(8,128)(2,1)S(1)} %collective-permute-done.33.refs_8_.refs_26_.refs_5_), channel_id=1, source_target_pairs={{0,1},{1,0},{2,3},{3,2},{4,5},{5,4},{6,7},{7,6},{8,9},{9,8},{10,11... | collective-permute-start | bytes 516104 | tf_op jit(solution)/shard_map/ppermute | solution.py:29
  110.9 7.6 %collective-permute-start.45 = (bf16[256,256]{1,0:T(8,128)(2,1)S(1)}, bf16[256,256]{1,0:T(8,128)(2,1)S(1)}, u32[]{:S(2)}, u32[]{:S(2)}) collective-permute-start(bf16[256,256]{1,0:T(8,128)(2,1)S(1)} %get-tuple-element.90.refs_0_), channel_id=1, source_target_pairs={{0,2},{1,3},{2,0},{3,1},{4,6},{5,7},{6,4},{7,5},{8,10},{9,11},{10,... | collective-permute-start | bytes 393224 | tf_op jit(solution)/shard_map/ppermute | solution.py:29
